TPU v7x, 128 devices: a whole 4x4x4 slice. The times are simulated.
128 devices in a mesh: row: 16 (over y, z), col: 8 (over x, core).
Axes of the slice: x: 4, y: 4, z: 4, core: 2. Of those that a mesh axis runs over, the one named last changes fastest.
Arguments:
- front: float32 [6, 16, 128, 12, 8, 128], P(None, 'row', None, None, 'col'), may hold values from -2.01 to 16, as said below
- child_updates: float32 [6, 16, 128, 6, 8, 128], P(None, 'row', None, None, 'col'), may hold values from -0.5 to 0.005, as said below
- child_maps: int32 [2, 48], replicated, may hold values from 0 to 62, as said below
- child_orders: int32 [2], replicated, may hold values from 6017 to 6144, as said below
Outputs:
- factored: float32 [6, 16, 128, 12, 8, 128], P(None, 'row', None, None, 'col')
Inputs may be any that keep to these rules, and one draw needn't show every extreme that they name: `front`: symmetric; with the children's updates added as above it is positive definite. `child_updates`: each child's update is symmetric. `child_maps`: each child's map adds to a tile's index an offset that is the same over aligned runs of 8 child tiles, rises strictly from run to run, is 0 on the first run and 15 on the last, and differs modulo 8 between runs. `child_orders`: each order lies in the last tile of its padded update; one of the two is 6144.
All inputs are finite; a program needn't handle non-finite values.
Results may differ from a plain program's by a relative error of at most 0.00005.
Values sent between devices are 32-bit elements; how exact they have to be, the bound alone decides.
No kernel may reach another device: no remote copies, remote signals or barrier semaphores. Data moves between devices by JAX's collectives and lax.ppermute only.
A program may use at most 128 MiB of HBM per device.

v0:
```python
import jax
import jax.numpy as jnp
from jax import lax
from jax.sharding import PartitionSpec as P

PT = 5
PANELS = 1
RUN = 8


highest = lax.Precision.HIGHEST


def spread(value, axis, source):
    kept = jnp.where(lax.axis_index(axis) == source, value, 0).astype(value.dtype)
    return lax.psum(kept, axis)


def earlier_equal(values):
    length = values.shape[-1]
    matches = values[..., :, None] == values[..., None, :]
    earlier = jnp.arange(length)[None, :] < jnp.arange(length)[:, None]
    return jnp.sum(jnp.logical_and(matches, earlier), axis=-1)


def one_hot(values, length):
    return (values[..., None] == jnp.arange(length, dtype=jnp.int32)).astype(jnp.float32)


def shards(front, child_updates, child_maps, child_orders):
    row_tiles, tile_size, col_tiles = (front.shape[0], front.shape[2], front.shape[3])
    child_rows, child_cols = (child_updates.shape[0], child_updates.shape[3])
    rows_count = lax.axis_size("row")
    cols_count = lax.axis_size("col")
    half_rows = rows_count // 2
    group_size = rows_count // cols_count
    row_id = lax.axis_index("row")
    col_id = lax.axis_index("col")
    matrix = front.reshape(row_tiles, tile_size, col_tiles, tile_size)
    pieces = child_updates.reshape(child_rows, tile_size, child_cols, tile_size)
    cap_rows = max(1, 2 * RUN // rows_count)
    cap_cols = max(1, RUN // cols_count) ** 2
    sources = jnp.arange(rows_count, dtype=jnp.int32)
    source_child = sources // half_rows
    source_maps = jnp.where(
        source_child[:, None] == 0, child_maps[0][None, :], child_maps[1][None, :]
    )
    child_row_index = (
        jnp.arange(child_rows, dtype=jnp.int32)[None, :] * half_rows
        + (sources % half_rows)[:, None]
    )
    mapped_rows = jnp.take_along_axis(source_maps, child_row_index, axis=1)
    dest_rows = mapped_rows % rows_count
    slot_rows = mapped_rows // rows_count
    child_col_index = (
        jnp.arange(child_cols, dtype=jnp.int32)[None, :] * cols_count
        + jnp.arange(cols_count, dtype=jnp.int32)[:, None]
    )
    mapped_cols = child_maps[:, child_col_index]
    dest_cols = mapped_cols % cols_count
    slot_cols = mapped_cols // cols_count
    my_child = row_id // half_rows
    my_order = jnp.where(my_child == 0, child_orders[0], child_orders[1])
    my_rows = child_row_index[row_id]
    my_cols = jnp.arange(child_cols, dtype=jnp.int32) * cols_count + col_id
    offsets = jnp.arange(tile_size, dtype=jnp.int32)[None, :]
    row_keep = (my_rows[:, None] * tile_size + offsets < my_order).astype(jnp.float32)
    col_keep = (my_cols[:, None] * tile_size + offsets < my_order).astype(jnp.float32)
    pieces = pieces * row_keep[:, :, None, None] * col_keep[None, None, :, :]
    rank_rows = earlier_equal(dest_rows)
    send_rows = (
        one_hot(dest_rows[row_id], rows_count)[:, :, None]
        * one_hot(rank_rows[row_id], cap_rows)[:, None, :]
    )
    outgoing = jnp.einsum("tjq,trus->jqrus", send_rows, pieces, precision=highest)
    incoming = lax.all_to_all(outgoing, "row", split_axis=0, concat_axis=0, tiled=True)
    arrive_rows = (dest_rows == row_id).astype(jnp.float32)
    place_rows = jnp.einsum(
        "jt,jk,jta,jtq->kajq",
        arrive_rows,
        one_hot(source_child, 2),
        one_hot(slot_rows, row_tiles),
        one_hot(rank_rows, cap_rows),
        precision=highest,
    )
    placed = jnp.einsum("kajq,jqrus->karus", place_rows, incoming, precision=highest)
    rank_cols = earlier_equal(dest_cols)
    send_cols = (
        one_hot(dest_cols[:, col_id], cols_count)[..., None]
        * one_hot(rank_cols[:, col_id], cap_cols)[..., None, :]
    )
    outgoing_cols = jnp.einsum("kulq,karus->lqkars", send_cols, placed, precision=highest)
    incoming_cols = lax.all_to_all(outgoing_cols, "col", split_axis=0, concat_axis=0, tiled=True)
    arrive_cols = (dest_cols == col_id).astype(jnp.float32)
    place_cols = jnp.einsum(
        "klu,klub,kluq->blqk",
        arrive_cols,
        one_hot(slot_cols, col_tiles),
        one_hot(rank_cols, cap_cols),
        precision=highest,
    )
    added = jnp.einsum("blqk,lqkars->arbs", place_cols, incoming_cols, precision=highest)
    matrix = matrix + added
    glob_rows = jnp.arange(row_tiles, dtype=jnp.int32) * rows_count + row_id
    glob_cols = jnp.arange(col_tiles, dtype=jnp.int32) * cols_count + col_id
    identity = jnp.eye(tile_size, dtype=jnp.float32)

    def factor_column(matrix, column_tile):
        owner_col = column_tile % cols_count
        local_col = column_tile // cols_count
        owner_row = column_tile % rows_count
        local_row = column_tile // rows_count
        column = lax.dynamic_index_in_dim(matrix, local_col, 2, keepdims=False)
        pivot_local = lax.dynamic_index_in_dim(column, local_row, 0, keepdims=False)
        pivot_local = jnp.where(col_id == owner_col, pivot_local, identity)
        pivot = spread(pivot_local, "row", owner_row)
        factor = jnp.tril(jnp.linalg.cholesky(pivot))
        solved = lax.linalg.triangular_solve(
            factor,
            column.reshape(row_tiles * tile_size, tile_size),
            left_side=False,
            lower=True,
            transpose_a=True,
        ).reshape(row_tiles, tile_size, tile_size)
        below = (glob_rows > column_tile)[:, None, None]
        diagonal = (glob_rows == column_tile)[:, None, None]
        panel_part = jnp.where(below, solved, jnp.where(diagonal, factor[None], 0.0))
        lower_rows = spread(panel_part, "col", owner_col)
        received = []
        for member in range(group_size):
            received.append(spread(lower_rows, "row", col_id + member * cols_count))
        lower_cols = jnp.stack(received, 1).reshape(col_tiles, tile_size, tile_size)
        new_column = jnp.where(col_id == owner_col, panel_part, column)
        matrix = lax.dynamic_update_index_in_dim(matrix, new_column, local_col, 2)
        lower_rows = jnp.where(below, lower_rows, 0.0)
        lower_cols = jnp.where((glob_cols > column_tile)[:, None, None], lower_cols, 0.0)
        return (matrix, lower_rows, lower_cols)

    def column_turn(column, matrix):
        matrix, lower_rows, lower_cols = factor_column(matrix, 0 + column)
        return matrix - jnp.einsum("trx,usx->trus", lower_rows, lower_cols, precision=highest)

    matrix = lax.fori_loop(0, PT, column_turn, matrix)
    factored_tiles = PANELS * PT
    upper_block = jnp.logical_and(
        (glob_rows < factored_tiles)[:, None], (glob_cols >= factored_tiles)[None, :]
    )
    matrix = jnp.where(upper_block[:, None, :, None], 0.0, matrix)
    return matrix.reshape(row_tiles, 1, tile_size, col_tiles, 1, tile_size)


def solution(mesh):
    in_specs = (
        P(None, "row", None, None, "col", None),
        P(None, "row", None, None, "col", None),
        P(),
        P(),
    )
    out_specs = P(None, "row", None, None, "col", None)
    return jax.shard_map(shards, mesh=mesh, in_specs=in_specs, out_specs=out_specs, check_vma=False)
```

profile of v0, /device:TPU:16, one launch (start us, length us, event | category | flops | bytes accessed | tf_op | source)
XLA Modules:
  0.0 1627.7 jit_solution(2012659851449914901)
XLA Ops:
  36.7 88.3 %all-to-all-done = f32[16,1,128,6,128]{4,2,3,1,0:T(8,128)} async-done(((f32[16,1,128,6,128]{4,2,3,1,0:T(8,128)}), f32[16,1,128,6,128]{4,2,3,1,0:T(8,128)}, u32[]{:S(2)}, u32[]{:S(2)}) %all-to-all-start) | async-done | bytes 6291488 | tf_op jit(solution)/shard_map/all_to_all | solution.py:76
  125.0 13.5 fusion.22
  154.5 71.6 %all-to-all-done.1 = f32[8,1,2,6,128,128]{5,4,3,2,1,0:T(8,128)} async-done(((f32[8,1,2,6,128,128]{5,4,3,2,1,0:T(8,128)}), f32[8,1,2,6,128,128]{5,4,3,2,1,0:T(8,128)}, u32[]{:S(2)}, u32[]{:S(2)}) %all-to-all-start.1) | async-done | bytes 6291488 | tf_op jit(solution)/shard_map/all_to_all | solution.py:93
  226.1 11.8 fusion.20
  244.1 1362.4 %while.18 = (s32[]{:T(128)}, f32[6,128,12,128]{3,1,2,0:T(8,128)}, s32[]{:T(128)}, s32[]{:T(128)}, s32[]{:T(128)}, /*index=5*/s32[]{:T(128)}, s32[]{:T(128)}, s32...) while((s32[]{:T(128)}, f32[6,128,12,128]{3,1,2,0:T(8,128)}, ...), condition=%wide.region_9.10_spmd.clone.clone, body=%wide.region_2.9_spmd.clone.clone.sunk | while | flops 1965736192 | bytes 67307408 | solution.py:143
  246.0 97.8 %all-reduce.7.cloned.1.call-done = f32[128,128]{1,0:T(8,128)} async-done(((f32[128,128]{1,0:T(8,128)}), f32[128,128]{1,0:T(8,128)}) %all-reduce.7.cloned.1.call-update) | async-done | bytes 65552 | tf_op jit(solution)/shard_map/while/body/eval_jaxpr/psum | solution.py:16
  345.5 11.7 cholesky.69
  370.8 60.6 %all-reduce.9.cloned.1.call-done = f32[6,128,128]{2,1,0:T(8,128)} async-done(((f32[6,128,128]{2,1,0:T(8,128)}), f32[6,128,128]{2,1,0:T(8,128)}) %all-reduce.9.cloned.1.call-update) | async-done | bytes 393232 | tf_op jit(solution)/shard_map/while/body/eval_jaxpr/psum | solution.py:16
  435.3 83.8 %all-reduce.11.cloned.1.call-done = (f32[6,1,128,128]{3,2,0,1:T(8,128)}, f32[6,1,128,128]{3,2,0,1:T(8,128)}) async-done(((f32[6,1,128,128]{3,2,0,1:T(8,128)}, f32[6,1,128,128]{3,2,0,1:T(8,128)}), (f32[6,1,128,128]{3,2,0,1:T(8,128)}, f32[6,1,128,128]{3,2,0,1:T(8,128)})) %all-reduce.11.cloned.1.call-update) | async-done | bytes 786448 | tf_op jit(solution)/shard_map/while/body/eval_jaxpr/psum | solution.py:16
  530.5 82.5 %all-reduce.7.cloned.1.call-done = f32[128,128]{1,0:T(8,128)} async-done(((f32[128,128]{1,0:T(8,128)}), f32[128,128]{1,0:T(8,128)}) %all-reduce.7.cloned.1.call-update) | async-done | bytes 65552 | tf_op jit(solution)/shard_map/while/body/eval_jaxpr/psum | solution.py:16
  614.8 11.7 cholesky.69
  640.1 60.6 %all-reduce.9.cloned.1.call-done = f32[6,128,128]{2,1,0:T(8,128)} async-done(((f32[6,128,128]{2,1,0:T(8,128)}), f32[6,128,128]{2,1,0:T(8,128)}) %all-reduce.9.cloned.1.call-update) | async-done | bytes 393232 | tf_op jit(solution)/shard_map/while/body/eval_jaxpr/psum | solution.py:16
  704.6 83.7 %all-reduce.11.cloned.1.call-done = (f32[6,1,128,128]{3,2,0,1:T(8,128)}, f32[6,1,128,128]{3,2,0,1:T(8,128)}) async-done(((f32[6,1,128,128]{3,2,0,1:T(8,128)}, f32[6,1,128,128]{3,2,0,1:T(8,128)}), (f32[6,1,128,128]{3,2,0,1:T(8,128)}, f32[6,1,128,128]{3,2,0,1:T(8,128)})) %all-reduce.11.cloned.1.call-update) | async-done | bytes 786448 | tf_op jit(solution)/shard_map/while/body/eval_jaxpr/psum | solution.py:16
  799.6 82.8 %all-reduce.7.cloned.1.call-done = f32[128,128]{1,0:T(8,128)} async-done(((f32[128,128]{1,0:T(8,128)}), f32[128,128]{1,0:T(8,128)}) %all-reduce.7.cloned.1.call-update) | async-done | bytes 65552 | tf_op jit(solution)/shard_map/while/body/eval_jaxpr/psum | solution.py:16
  884.2 11.7 cholesky.69
  909.4 60.6 %all-reduce.9.cloned.1.call-done = f32[6,128,128]{2,1,0:T(8,128)} async-done(((f32[6,128,128]{2,1,0:T(8,128)}), f32[6,128,128]{2,1,0:T(8,128)}) %all-reduce.9.cloned.1.call-update) | async-done | bytes 393232 | tf_op jit(solution)/shard_map/while/body/eval_jaxpr/psum | solution.py:16
  974.0 83.8 %all-reduce.11.cloned.1.call-done = (f32[6,1,128,128]{3,2,0,1:T(8,128)}, f32[6,1,128,128]{3,2,0,1:T(8,128)}) async-done(((f32[6,1,128,128]{3,2,0,1:T(8,128)}, f32[6,1,128,128]{3,2,0,1:T(8,128)}), (f32[6,1,128,128]{3,2,0,1:T(8,128)}, f32[6,1,128,128]{3,2,0,1:T(8,128)})) %all-reduce.11.cloned.1.call-update) | async-done | bytes 786448 | tf_op jit(solution)/shard_map/while/body/eval_jaxpr/psum | solution.py:16
  1069.2 82.5 %all-reduce.7.cloned.1.call-done = f32[128,128]{1,0:T(8,128)} async-done(((f32[128,128]{1,0:T(8,128)}), f32[128,128]{1,0:T(8,128)}) %all-reduce.7.cloned.1.call-update) | async-done | bytes 65552 | tf_op jit(solution)/shard_map/while/body/eval_jaxpr/psum | solution.py:16
  1153.5 11.7 cholesky.69
  1178.8 60.6 %all-reduce.9.cloned.1.call-done = f32[6,128,128]{2,1,0:T(8,128)} async-done(((f32[6,128,128]{2,1,0:T(8,128)}), f32[6,128,128]{2,1,0:T(8,128)}) %all-reduce.9.cloned.1.call-update) | async-done | bytes 393232 | tf_op jit(solution)/shard_map/while/body/eval_jaxpr/psum | solution.py:16
  1243.3 83.7 %all-reduce.11.cloned.1.call-done = (f32[6,1,128,128]{3,2,0,1:T(8,128)}, f32[6,1,128,128]{3,2,0,1:T(8,128)}) async-done(((f32[6,1,128,128]{3,2,0,1:T(8,128)}, f32[6,1,128,128]{3,2,0,1:T(8,128)}), (f32[6,1,128,128]{3,2,0,1:T(8,128)}, f32[6,1,128,128]{3,2,0,1:T(8,128)})) %all-reduce.11.cloned.1.call-update) | async-done | bytes 786448 | tf_op jit(solution)/shard_map/while/body/eval_jaxpr/psum | solution.py:16
  1338.3 82.9 %all-reduce.7.cloned.1.call-done = f32[128,128]{1,0:T(8,128)} async-done(((f32[128,128]{1,0:T(8,128)}), f32[128,128]{1,0:T(8,128)}) %all-reduce.7.cloned.1.call-update) | async-done | bytes 65552 | tf_op jit(solution)/shard_map/while/body/eval_jaxpr/psum | solution.py:16
  1448.2 60.6 %all-reduce.9.cloned.1.call-done = f32[6,128,128]{2,1,0:T(8,128)} async-done(((f32[6,128,128]{2,1,0:T(8,128)}), f32[6,128,128]{2,1,0:T(8,128)}) %all-reduce.9.cloned.1.call-update) | async-done | bytes 393232 | tf_op jit(solution)/shard_map/while/body/eval_jaxpr/psum | solution.py:16
  1512.7 83.6 %all-reduce.11.cloned.1.call-done = (f32[6,1,128,128]{3,2,0,1:T(8,128)}, f32[6,1,128,128]{3,2,0,1:T(8,128)}) async-done(((f32[6,1,128,128]{3,2,0,1:T(8,128)}, f32[6,1,128,128]{3,2,0,1:T(8,128)}), (f32[6,1,128,128]{3,2,0,1:T(8,128)}, f32[6,1,128,128]{3,2,0,1:T(8,128)})) %all-reduce.11.cloned.1.call-update) | async-done | bytes 786448 | tf_op jit(solution)/shard_map/while/body/eval_jaxpr/psum | solution.py:16
  (213 shorter events, 229.1 us)
Async XLA Ops:
  26.4 98.6 %all-to-all-start = ((f32[16,1,128,6,128]{4,2,3,1,0:T(8,128)}), f32[16,1,128,6,128]{4,2,3,1,0:T(8,128)}, u32[]{:S(2)}, u32[]{:S(2)}) async-start(f32[16,1,128,6,128]{4,2,3,1,0:T(8,128)} %copy.116), calls=%async_computation | async-start | bytes 12582912 | tf_op jit(solution)/shard_map/all_to_all | solution.py:76
  148.9 89.1 %slice-start = ((s8[4718592]{0:T(1024)(128)(4,1)}), s8[524288]{0:T(1024)(128)(4,1)S(1)}, s32[]{:S(2)}) async-start(s8[4718592]{0:T(1024)(128)(4,1)} %bitcast.156), calls=%async_computation.5 | async-start | bytes 1048576
  148.9 77.2 %all-to-all-start.1 = ((f32[8,1,2,6,128,128]{5,4,3,2,1,0:T(8,128)}), f32[8,1,2,6,128,128]{5,4,3,2,1,0:T(8,128)}, u32[]{:S(2)}, u32[]{:S(2)}) async-start(f32[8,1,2,6,128,128]{5,4,3,2,1,0:T(8,128)} %copy.124), calls=%async_computation.1 | async-start | bytes 12582912 | tf_op jit(solution)/shard_map/all_to_all | solution.py:93
  226.1 11.9 slice-start.1
  244.3 99.5 %all-reduce.7.cloned.1.call-start = ((), (), s32[]{:S(2)}) async-start(), calls=%async_computation.2 | async-start | bytes 131072 | tf_op jit(solution)/shard_map/while/body/eval_jaxpr/psum | solution.py:16
  245.9 185.5 %all-reduce.9.cloned.1.call-start = ((), (), s32[]{:S(2)}) async-start(), calls=%async_computation.3 | async-start | bytes 786432 | tf_op jit(solution)/shard_map/while/body/eval_jaxpr/psum | solution.py:16
  370.7 148.4 %all-reduce.11.cloned.1.call-start = ((), (), s32[]{:S(2)}) async-start(), calls=%async_computation.4 | async-start | bytes 1572864 | tf_op jit(solution)/shard_map/while/body/eval_jaxpr/psum | solution.py:16
  431.4 89.3 %copy-start.2 = (f32[6,128,128]{2,1,0:T(8,128)S(1)}, f32[6,128,128]{2,1,0:T(8,128)}, u32[]{:S(2)}) copy-start(f32[6,128,128]{2,1,0:T(8,128)} %all-reduce.9.cloned.1.call-done) | copy-start | bytes 1179652 | tf_op jit(solution)/shard_map/while
  528.9 84.1 %all-reduce.7.cloned.1.call-start = ((), (), s32[]{:S(2)}) async-start(), calls=%async_computation.2 | async-start | bytes 131072 | tf_op jit(solution)/shard_map/while/body/eval_jaxpr/psum | solution.py:16
  530.4 170.2 %all-reduce.9.cloned.1.call-start = ((), (), s32[]{:S(2)}) async-start(), calls=%async_computation.3 | async-start | bytes 786432 | tf_op jit(solution)/shard_map/while/body/eval_jaxpr/psum | solution.py:16
  640.0 148.2 %all-reduce.11.cloned.1.call-start = ((), (), s32[]{:S(2)}) async-start(), calls=%async_computation.4 | async-start | bytes 1572864 | tf_op jit(solution)/shard_map/while/body/eval_jaxpr/psum | solution.py:16
  700.6 89.1 %copy-start.2 = (f32[6,128,128]{2,1,0:T(8,128)S(1)}, f32[6,128,128]{2,1,0:T(8,128)}, u32[]{:S(2)}) copy-start(f32[6,128,128]{2,1,0:T(8,128)} %all-reduce.9.cloned.1.call-done) | copy-start | bytes 1179652 | tf_op jit(solution)/shard_map/while
  798.0 84.4 %all-reduce.7.cloned.1.call-start = ((), (), s32[]{:S(2)}) async-start(), calls=%async_computation.2 | async-start | bytes 131072 | tf_op jit(solution)/shard_map/while/body/eval_jaxpr/psum | solution.py:16
  799.5 170.5 %all-reduce.9.cloned.1.call-start = ((), (), s32[]{:S(2)}) async-start(), calls=%async_computation.3 | async-start | bytes 786432 | tf_op jit(solution)/shard_map/while/body/eval_jaxpr/psum | solution.py:16
  909.4 148.5 %all-reduce.11.cloned.1.call-start = ((), (), s32[]{:S(2)}) async-start(), calls=%async_computation.4 | async-start | bytes 1572864 | tf_op jit(solution)/shard_map/while/body/eval_jaxpr/psum | solution.py:16
  970.1 89.3 %copy-start.2 = (f32[6,128,128]{2,1,0:T(8,128)S(1)}, f32[6,128,128]{2,1,0:T(8,128)}, u32[]{:S(2)}) copy-start(f32[6,128,128]{2,1,0:T(8,128)} %all-reduce.9.cloned.1.call-done) | copy-start | bytes 1179652 | tf_op jit(solution)/shard_map/while
  1067.6 84.1 %all-reduce.7.cloned.1.call-start = ((), (), s32[]{:S(2)}) async-start(), calls=%async_computation.2 | async-start | bytes 131072 | tf_op jit(solution)/shard_map/while/body/eval_jaxpr/psum | solution.py:16
  1069.1 170.2 %all-reduce.9.cloned.1.call-start = ((), (), s32[]{:S(2)}) async-start(), calls=%async_computation.3 | async-start | bytes 786432 | tf_op jit(solution)/shard_map/while/body/eval_jaxpr/psum | solution.py:16
  1178.7 148.3 %all-reduce.11.cloned.1.call-start = ((), (), s32[]{:S(2)}) async-start(), calls=%async_computation.4 | async-start | bytes 1572864 | tf_op jit(solution)/shard_map/while/body/eval_jaxpr/psum | solution.py:16
  1239.4 89.1 %copy-start.2 = (f32[6,128,128]{2,1,0:T(8,128)S(1)}, f32[6,128,128]{2,1,0:T(8,128)}, u32[]{:S(2)}) copy-start(f32[6,128,128]{2,1,0:T(8,128)} %all-reduce.9.cloned.1.call-done) | copy-start | bytes 1179652 | tf_op jit(solution)/shard_map/while
  1336.8 84.4 %all-reduce.7.cloned.1.call-start = ((), (), s32[]{:S(2)}) async-start(), calls=%async_computation.2 | async-start | bytes 131072 | tf_op jit(solution)/shard_map/while/body/eval_jaxpr/psum | solution.py:16
  1338.3 170.5 %all-reduce.9.cloned.1.call-start = ((), (), s32[]{:S(2)}) async-start(), calls=%async_computation.3 | async-start | bytes 786432 | tf_op jit(solution)/shard_map/while/body/eval_jaxpr/psum | solution.py:16
  1448.2 148.2 %all-reduce.11.cloned.1.call-start = ((), (), s32[]{:S(2)}) async-start(), calls=%async_computation.4 | async-start | bytes 1572864 | tf_op jit(solution)/shard_map/while/body/eval_jaxpr/psum | solution.py:16
  1508.8 89.1 %copy-start.2 = (f32[6,128,128]{2,1,0:T(8,128)S(1)}, f32[6,128,128]{2,1,0:T(8,128)}, u32[]{:S(2)}) copy-start(f32[6,128,128]{2,1,0:T(8,128)} %all-reduce.9.cloned.1.call-done) | copy-start | bytes 1179652 | tf_op jit(solution)/shard_map/while
  (12 other events, 38.3 us)
Sparse Core Ops, SparseCore 0:
  248.3 95.3 all-reduce.6
  370.8 60.4 all-reduce.8
  434.7 84.3 all-reduce.10
  532.6 80.3 all-reduce.6
  640.1 60.4 all-reduce.8
  703.8 84.3 all-reduce.10
  802.0 80.3 all-reduce.6
  909.5 60.5 all-reduce.8
  973.4 84.3 all-reduce.10
  1071.3 80.3 all-reduce.6
  1178.8 60.4 all-reduce.8
  1242.5 84.3 all-reduce.10
  1340.8 80.3 all-reduce.6
  1448.3 60.4 all-reduce.8
  1512.0 84.3 all-reduce.10
where the time goes:
time: 1640 us; the launch traced here: 1630 us
  waiting for transfers between devices  1310 us (80%)
  other arithmetic  155 us (9%)
  matrix products  75.4 us (5%)
  local copies, waits for them, and re-layouts  56.2 us (3%)
    psum x15, waiting for transfers between devices, spread(): return lax.psum(kept, axis)  1150 us
    all_to_all x1, waiting for transfers between devices, shards(): lax.all_to_all(outgoing, 'row', split_axis=0, concat_axis=0, tiled=True)  88.3 us
    all_to_all x1, waiting for transfers between devices, shards(): lax.all_to_all(outgoing_cols, 'col', split_axis=0, concat_axis=0, tiled=T...  71.6 us
    another operation x15, other arithmetic, factor_column(): factor = jnp.tril(jnp.linalg.cholesky(pivot))  62.3 us
    another operation x10, other arithmetic, factor_column(): lax.linalg.triangular_solve(factor, column.reshape(row_tiles * tile_size,...  52.3 us
  transfers between devices with their start and end apart: 17, of which 17 were waited for; matrix products, arithmetic and copies ran while one was open for 1% of the time, Pallas kernels for 0%

commit v1 on v0

v1 whole, which is shorter than its diff:
```python
import jax
import jax.numpy as jnp
from jax import lax
from jax.experimental import pallas as pl
from jax.experimental.pallas import tpu as pltpu
from jax.sharding import Mesh
from jax.sharding import PartitionSpec as P

T = 128
PT = 5
ROW_TILES = 6
COL_TILES = 12
CHILD_TILES = 6
ROWS = ("k", "i")
HIGHEST = lax.Precision.HIGHEST
F32 = jnp.float32

VMEM = pl.BlockSpec(memory_space=pltpu.VMEM)
SMEM = pl.BlockSpec(memory_space=pltpu.SMEM)


def shape(*dims):
    return jax.ShapeDtypeStruct(dims, F32)


def params(mib):
    return pltpu.CompilerParams(vmem_limit_bytes=mib * 2**20)


def place():
    return lax.axis_index("k"), lax.axis_index("i"), lax.axis_index("col")


def offset(maps, child, run):
    return maps[child, 8 * run] - 8 * run


def child_tile(child, order, i, j, g, h):
    tile = child[pl.ds(g * T * CHILD_TILES + h, T, stride=CHILD_TILES), :]
    if g == CHILD_TILES - 1:
        rows = lax.broadcasted_iota(jnp.int32, (T, T), 0) + (8 * g + i) * T
        tile = jnp.where(rows < order, tile, 0.0)
    if h == CHILD_TILES - 1:
        cols = lax.broadcasted_iota(jnp.int32, (T, T), 1) + (8 * h + j) * T
        tile = jnp.where(cols < order, tile, 0.0)
    return tile


def pack_panel(maps, orders, front, child, out_rows, out_cols):
    k, i, j = place()
    order = orders[k]
    cols = lax.broadcasted_iota(jnp.int32, (8, T), 1) + (8 * (CHILD_TILES - 1) + j) * T
    for v in range(16):
        for s in range(COL_TILES):
            out_rows[v, s] = front[pl.ds(8 * v * COL_TILES + s, 8, stride=COL_TILES), :]
        for h in range(CHILD_TILES):
            piece = child[pl.ds(8 * v * CHILD_TILES + h, 8, stride=CHILD_TILES), :]
            if h == CHILD_TILES - 1:
                piece = jnp.where(cols < order, piece, 0.0)
            out_rows[v, COL_TILES + h] = piece
    for g in range(CHILD_TILES):
        out_cols[(8 * g + i + offset(maps, k, g)) % 16] = child_tile(child, order, i, j, g, 0)


def pack_main(maps, orders, child, out):
    k, i, j = place()
    order = orders[k]
    for g in range(CHILD_TILES):
        to_i = (i + offset(maps, k, g)) % 8
        for h in range(CHILD_TILES):
            to_j = (j + offset(maps, k, h)) % 8
            out[to_i * 8 + to_j] = child_tile(child, order, i, j, g, h)


def pack_slices(maps, got, out, lead):
    j = lax.axis_index("col")
    for child in range(2):
        for h in range(CHILD_TILES):
            dest = (j + offset(maps, child, h)) % 8
            for b in range(PT):
                out[dest, child, b] = got[8 * child + b, COL_TILES + h]
    for b in range(PT):
        lead[b] = got[b, 0] + got[b, COL_TILES] + got[8 + b, COL_TILES]


def add_slices(maps, got, moved, slab):
    j = lax.axis_index("col")
    for b in range(PT):
        for s in range(COL_TILES):
            slab[b, s] = got[b, s]
    for child in range(2):
        for h in range(CHILD_TILES):
            shift = offset(maps, child, h)
            source = (j - shift) % 8
            s = (8 * h + source + shift) // 8
            for b in range(PT):
                slab[b, s] = slab[b, s] + moved[source, child, b]


def add_column(maps, front, moved, out):
    k, i, j = place()
    row = k * 8 + i
    for t in range(ROW_TILES):
        out[t] = front[pl.ds(t * T * COL_TILES, T, stride=COL_TILES), :]
    for child in range(2):
        for g in range(CHILD_TILES):
            shift = offset(maps, child, g)
            source = (row - 8 * g - shift) % 16

            @pl.when(source < 8)
            def _():
                t = (8 * g + source + shift) // 16
                out[t] = out[t] + moved[8 * child + source]


def invert_factor(lead, out, matrix, work):
    for b in range(PT):
        for c in range(PT):
            for r in range(16):
                matrix[b * T + 8 * r:b * T + 8 * r + 8, c * T:c * T + T] = lead[r * 8 + c, b]
    out[...] = jnp.zeros_like(out)
    sub = lax.broadcasted_iota(jnp.int32, (8, T), 0)
    lane = lax.broadcasted_iota(jnp.int32, (8, T), 1)
    eye = (
        lax.broadcasted_iota(jnp.int32, (T, T), 0) == lax.broadcasted_iota(jnp.int32, (T, T), 1)
    ).astype(F32)
    for b in range(PT):
        lo, hi = b * T, b * T + T
        work[:, :T] = matrix[lo:hi, lo:hi]
        work[:, T:] = eye
        for p in range(16):
            first = 8 * p
            rows = work[first:first + 8, :T]
            other = work[first:first + 8, T:]
            columns = [
                jnp.broadcast_to(rows[:, first + m:first + m + 1], (8, T)) for m in range(8)
            ]
            pivots = jnp.ones((8, T), F32)
            for m in range(8):
                pivot = jnp.broadcast_to(columns[m][m:m + 1, :], (8, T))
                pivots = jnp.where(sub == m, pivot, pivots)
                if m == 7:
                    break
                scale = jnp.where(sub > m, columns[m] * (1.0 / pivot), 0.0)
                rows = rows - scale * rows[m:m + 1, :]
                other = other - scale * other[m:m + 1, :]
                for n in range(m + 1, 8):
                    columns[n] = columns[n] - scale * columns[n][m:m + 1, :]
            out[lo + first:lo + first + 8, lo:hi] = other * lax.rsqrt(pivots)
            if p < 15:
                scaled = jnp.where(lane >= first + 8, rows * (1.0 / pivots), 0.0)
                both = jnp.concatenate([rows, other], axis=1)
                change = lax.dot_general(
                    scaled, both, (((0,), (0,)), ((), ())),
                    precision=HIGHEST, preferred_element_type=F32,
                )
                work[first + 8:, :] = work[first + 8:, :] - change[first + 8:, :]
        inverse = out[lo:hi, lo:hi]
        if b > 0:
            out[lo:hi, :lo] = jnp.dot(
                inverse, out[lo:hi, :lo], precision=HIGHEST, preferred_element_type=F32
            )
        if b < PT - 1:
            right = jnp.dot(
                inverse, matrix[lo:hi, hi:], precision=HIGHEST, preferred_element_type=F32
            )
            matrix[hi:, hi:] = matrix[hi:, hi:] - lax.dot_general(
                right, right, (((0,), (0,)), ((), ())),
                precision=HIGHEST, preferred_element_type=F32,
            )
            out[hi:, :hi] = out[hi:, :hi] - lax.dot_general(
                right, out[lo:hi, :hi], (((0,), (0,)), ((), ())),
                precision=HIGHEST, preferred_element_type=F32,
            )


SPLITS = ((0, 256), (256, 512), (512, 640))


def eliminate(front, across, down, inverse, out, upper, lower, pivot_rows):
    k, i, j = place()
    row = k * 8 + i
    for b in range(PT):
        for r in range(16):
            for s in range(COL_TILES):
                pivot_rows[b * T + 8 * r:b * T + 8 * r + 8, s * T:s * T + T] = across[r, b, s]

    def solve_upper(n, carry):
        part = pl.ds(pl.multiple_of(n * 512, 512), 512)
        for lo, hi in SPLITS:
            upper[lo:hi, part] = jnp.dot(
                inverse[lo:hi, :hi], pivot_rows[:hi, part],
                precision=HIGHEST, preferred_element_type=F32,
            )
        return carry

    lax.fori_loop(0, COL_TILES // 4, solve_upper, 0)

    def solve_lower(t, carry):
        mine = jnp.concatenate([down[b, t] for b in range(PT)], axis=1)
        part = pl.ds(pl.multiple_of(t * T, T), T)
        for lo, hi in SPLITS:
            lower[part, lo:hi] = lax.dot_general(
                mine[:, :hi], inverse[lo:hi, :hi], (((1,), (1,)), ((), ())),
                precision=HIGHEST, preferred_element_type=F32,
            )
        return carry

    lax.fori_loop(0, ROW_TILES, solve_lower, 0)

    def subtract(t, carry):
        part = pl.ds(pl.multiple_of(t * T, T), T)
        for n in range(COL_TILES // 4):
            product = jnp.dot(
                lower[part, :], upper[:, n * 512:n * 512 + 512],
                precision=HIGHEST, preferred_element_type=F32,
            )
            for s in range(4):
                where = pl.ds(t * T * COL_TILES + 4 * n + s, T, stride=COL_TILES)
                out[where, :] = front[where, :] - product[:, s * T:s * T + T]
        return carry

    lax.fori_loop(0, ROW_TILES, subtract, 0)

    x = lax.broadcasted_iota(jnp.int32, (T, T), 0)
    y = lax.broadcasted_iota(jnp.int32, (T, T), 1)

    @pl.when(row < PT)
    def _():
        for s in range(COL_TILES):
            out[pl.ds(s, T, stride=COL_TILES), :] = jnp.zeros((T, T), F32)

    @pl.when(j < PT)
    def _():
        for t in range(ROW_TILES):
            tile = lower[t * T:t * T + T, pl.ds(pl.multiple_of(j * T, T), T)]
            if t == 0:
                tile = jnp.where(row * T + x >= j * T + y, tile, 0.0)
            out[pl.ds(t * T * COL_TILES, T, stride=COL_TILES), :] = tile


def pack_other(maps, moved, out):
    k, i, j = place()
    rank = jnp.int32(0)
    for g in range(CHILD_TILES):
        shift = offset(maps, k, g)
        source = (i - shift) % 8
        leaves = (8 * g + source + shift) // 8 % 2 != k
        here = jnp.minimum(rank, 3)

        @pl.when(leaves)
        def _():
            for h in range(CHILD_TILES):
                out[here, h] = moved[source * 8 + (j - offset(maps, k, h)) % 8]

        rank = rank + leaves.astype(jnp.int32)


def add_children(maps, start, moved, other, out):
    k, i, j = place()
    out[...] = start[...]

    def add(child, g, source, shift, tile_of):
        p = 8 * g + source + shift
        for h in range(CHILD_TILES):
            across = offset(maps, child, h)
            from_j = (j - across) % 8
            q = 8 * h + from_j + across

            @pl.when(jnp.logical_and(p >= PT, q >= PT))
            def _():
                where = pl.ds(p // 16 * (T * COL_TILES) + q // 8, T, stride=COL_TILES)
                out[where, :] = out[where, :] + tile_of(h, from_j)

    rank = jnp.int32(0)
    for g in range(CHILD_TILES):
        shift = offset(maps, k, g)
        source = (i - shift) % 8

        @pl.when((8 * g + source + shift) // 8 % 2 == k)
        def _():
            add(k, g, source, shift, lambda h, from_j: moved[source * 8 + from_j])

        far = 1 - k
        far_shift = offset(maps, far, g)
        far_source = (i - far_shift) % 8
        comes = (8 * g + far_source + far_shift) // 8 % 2 == k
        here = jnp.minimum(rank, 3)

        @pl.when(comes)
        def _():
            add(far, g, far_source, far_shift, lambda h, from_j: other[here, h])

        rank = rank + comes.astype(jnp.int32)


def shards(front, child_updates, child_maps, child_orders):
    front = front.reshape(ROW_TILES * T * COL_TILES, T)
    child = child_updates.reshape(CHILD_TILES * T * CHILD_TILES, T)
    maps = child_maps
    row_slices, column_tiles = pl.pallas_call(
        pack_panel,
        out_shape=(shape(16, 18, 8, T), shape(16, T, T)),
        grid=(1,),
        in_specs=[
            SMEM, SMEM,
            pl.BlockSpec((T * COL_TILES, T), lambda n: (0, 0)),
            pl.BlockSpec((CHILD_TILES * T * CHILD_TILES, T), lambda n: (0, 0)),
        ],
        out_specs=[
            pl.BlockSpec((16, 18, 8, T), lambda n: (0, 0, 0, 0)),
            pl.BlockSpec((16, T, T), lambda n: (0, 0, 0)),
        ],
        compiler_params=params(24),
        name="pack_panel",
    )(maps, child_orders, front, child)
    row_slices = lax.all_to_all(row_slices, ROWS, 0, 0, tiled=True)
    slices, lead = pl.pallas_call(
        pack_slices,
        out_shape=(shape(8, 2, PT, 8, T), shape(PT, 8, T)),
        in_specs=[SMEM, VMEM],
        out_specs=[VMEM, VMEM],
        compiler_params=params(16),
        name="pack_slices",
    )(maps, row_slices)
    lead = lax.all_gather(lead, ("k", "i", "col"))
    slices = lax.all_to_all(slices, "col", 0, 0, tiled=True)
    slab = pl.pallas_call(
        add_slices,
        out_shape=shape(PT, COL_TILES, 8, T),
        in_specs=[SMEM, VMEM, VMEM],
        out_specs=VMEM,
        compiler_params=params(16),
        name="add_slices",
    )(maps, row_slices, slices)
    across = lax.all_gather(slab, ROWS)
    column_tiles = lax.all_to_all(column_tiles, ROWS, 0, 0, tiled=True)
    column = pl.pallas_call(
        add_column,
        out_shape=shape(ROW_TILES, T, T),
        in_specs=[SMEM, VMEM, VMEM],
        out_specs=VMEM,
        compiler_params=params(24),
        name="add_column",
    )(maps, front, column_tiles)
    down = lax.all_gather(column, "col")
    main = pl.pallas_call(
        pack_main,
        out_shape=shape(64, T, T),
        in_specs=[SMEM, SMEM, VMEM],
        out_specs=VMEM,
        compiler_params=params(24),
        name="pack_main",
    )(maps, child_orders, child)
    main = lax.all_to_all(main, ("i", "col"), 0, 0, tiled=True)
    inverse = pl.pallas_call(
        invert_factor,
        out_shape=shape(PT * T, PT * T),
        in_specs=[VMEM],
        out_specs=VMEM,
        scratch_shapes=[pltpu.VMEM((PT * T, PT * T), F32), pltpu.VMEM((T, 2 * T), F32)],
        compiler_params=params(32),
        cost_estimate=pl.CostEstimate(flops=40 * 10**9, bytes_accessed=4 * 2**20, transcendentals=0),
        name="invert_factor",
    )(lead)
    other = pl.pallas_call(
        pack_other,
        out_shape=shape(4, CHILD_TILES, T, T),
        in_specs=[SMEM, VMEM],
        out_specs=VMEM,
        compiler_params=params(24),
        name="pack_other",
    )(maps, main)
    other = lax.ppermute(other, "k", [(0, 1), (1, 0)])
    start = pl.pallas_call(
        eliminate,
        out_shape=shape(ROW_TILES * T * COL_TILES, T),
        in_specs=[VMEM] * 4,
        out_specs=VMEM,
        scratch_shapes=[
            pltpu.VMEM((PT * T, COL_TILES * T), F32),
            pltpu.VMEM((ROW_TILES * T, PT * T), F32),
            pltpu.VMEM((PT * T, COL_TILES * T), F32),
        ],
        compiler_params=params(48),
        cost_estimate=pl.CostEstimate(flops=25 * 10**9, bytes_accessed=20 * 2**20, transcendentals=0),
        name="eliminate",
    )(front, across, down, inverse)
    out = pl.pallas_call(
        add_children,
        out_shape=shape(ROW_TILES * T * COL_TILES, T),
        in_specs=[SMEM, VMEM, VMEM, VMEM],
        out_specs=VMEM,
        compiler_params=params(32),
        name="add_children",
    )(maps, start, main, other)
    return out.reshape(ROW_TILES, 1, T, COL_TILES, 1, T)


def solution(mesh):
    split = Mesh(mesh.devices.reshape(2, 8, 8), ("k", "i", "col"))
    tiles = P(None, ROWS, None, None, "col", None)
    return jax.shard_map(
        shards, mesh=split, in_specs=(tiles, tiles, P(), P()), out_specs=tiles, check_vma=False
    )
```

time: 1640 us -> 273 us (0.17)
  waiting for transfers between devices: 1310 us -> 88.1 us
  other arithmetic: 155 us -> 0 us
  Pallas kernels: 0 us -> 93.6 us
  matrix products: 75.4 us -> 0 us
  blocking collectives: 0 us -> 43.7 us
  local copies, waits for them, and re-layouts: 56.2 us -> 19.7 us
    psum x15 -> x0, waiting for transfers between devices: 1150 us -> none  [spread(): return lax.psum(kept, axis)]
    another operation x36 -> x0, other arithmetic: 132 us -> none  [the longest x15 62.3 us: factor_column(): factor = jnp.tril(jnp.linalg.cholesky(pivot))]
    all_to_all x2, waiting for transfers between devices: 160 us -> 58.2 us  [the longest x1 52.6 us: shards(): main = lax.all_to_all(main, ('i', 'col'), 0, 0, tiled=True)]
    pallas_call x0 -> x9, Pallas kernels: none -> 93.6 us  [the longest x1 47.2 us: shards(): pl.pallas_call(invert_factor, out_shape=shape(PT * T, PT * T), in_specs=[...]
    dot_general x10 -> x0, matrix products: 64.3 us -> none  [the longest x5 25.1 us: column_turn(): jnp.einsum('trx,usx->trus', lower_rows, lower_cols, precision=highest)]
    all_to_all x0 -> x2, blocking collectives: none -> 43.7 us  [the longest x1 24.5 us: shards(): row_slices = lax.all_to_all(row_slices, ROWS, 0, 0, tiled=True)]
    all_gather x0 -> x3, waiting for transfers between devices: none -> 29.8 us  [the longest x1 29.8 us: shards(): across = lax.all_gather(slab, ROWS)]
  transfers between devices with their start and end apart: 17 -> 6, of which waited for: 17 -> 3; matrix products, arithmetic and copies ran while one was open for 1% -> 0% of each run, Pallas kernels for 0% -> 32%
where the time goes in v1:
time: 273 us; the launch traced here: 271 us
  Pallas kernels  93.6 us (34%)
  waiting for transfers between devices  88.1 us (32%)
  blocking collectives  43.7 us (16%)
  local copies, waits for them, and re-layouts  19.7 us (7%)
  between operations  13.2 us (5%)
  starting transfers between devices  12.8 us (5%)
    all_to_all x1, waiting for transfers between devices, shards(): main = lax.all_to_all(main, ('i', 'col'), 0, 0, tiled=True)  52.6 us
    pallas_call x1, Pallas kernels, shards(): pl.pallas_call(invert_factor, out_shape=shape(PT * T, PT * T), in_specs=[...  47.2 us
    pallas_call x1, Pallas kernels, shards(): pl.pallas_call(eliminate, out_shape=shape(ROW_TILES * T * COL_TILES, T),...  32.8 us
    all_gather x1, waiting for transfers between devices, shards(): across = lax.all_gather(slab, ROWS)  29.8 us
    all_to_all x1, blocking collectives, shards(): row_slices = lax.all_to_all(row_slices, ROWS, 0, 0, tiled=True)  24.5 us
    unnamed x32, local copies, waits for them, and re-layouts  19.7 us
    all_to_all x1, blocking collectives, shards(): column_tiles = lax.all_to_all(column_tiles, ROWS, 0, 0, tiled=True)  19.2 us
    all_to_all x1, starting transfers between devices, shards(): main = lax.all_to_all(main, ('i', 'col'), 0, 0, tiled=True)  5.66 us
  transfers between devices with their start and end apart: 6, of which 3 were waited for; matrix products, arithmetic and copies ran while one was open for 0% of the time, Pallas kernels for 32%

profile of v1, /device:TPU:16, one launch (start us, length us, event | category | flops | bytes accessed | tf_op | source)
XLA Modules:
  0.0 271.1 jit_solution(1453417197011513500)
XLA Ops:
  6.5 2.3 copy-done
  8.9 1.7 copy-done.3
  12.6 24.5 %all_to_all.20.got = f32[16,18,8,128]{3,2,1,0:T(8,128)S(1)} all-to-all(f32[16,18,8,128]{3,2,1,0:T(8,128)S(1)} %get-tuple-element.9), channel_id=1, replica_groups=mesh['k'=2,'i'=8,'col'=8] {'k','i'}, dimensions={0} | all-to-all | bytes 2359296 | tf_op jit(solution)/shard_map/all_to_all | solution.py:317
  37.0 1.2 pack_slices.1
  39.0 19.2 %all_to_all.21.moved = f32[16,128,128]{2,1,0:T(8,128)S(1)} all-to-all(f32[16,128,128]{2,1,0:T(8,128)S(1)} %get-tuple-element.11), channel_id=1, replica_groups=mesh['k'=2,'i'=8,'col'=8] {'k','i'}, dimensions={0} | all-to-all | bytes 2097152 | tf_op jit(solution)/shard_map/all_to_all | solution.py:337
  58.3 2.3 copy-done.1
  62.2 4.4 %all-to-all-start.1 = ((f32[8,2,5,8,128]{4,3,2,1,0:T(8,128)}), f32[8,2,5,8,128]{4,3,2,1,0:T(8,128)}, u32[]{:S(2)}, u32[]{:S(2)}) async-start(f32[8,2,5,8,128]{4,3,2,1,0:T(8,128)} %copy-done.7), calls=%async_computation.1 | async-start | bytes 655360 | tf_op jit(solution)/shard_map/all_to_all | solution.py:327
  66.5 0.9 pack_main.1
  67.5 2.0 copy-done.2
  69.5 5.6 %all-to-all-done.1.moved = f32[8,2,5,8,128]{4,3,2,1,0:T(8,128)} async-done(((f32[8,2,5,8,128]{4,3,2,1,0:T(8,128)}), f32[8,2,5,8,128]{4,3,2,1,0:T(8,128)}, u32[]{:S(2)}, u32[]{:S(2)}) %all-to-all-start.1) | async-done | bytes 327712 | tf_op jit(solution)/shard_map/all_to_all | solution.py:327
  75.1 5.7 %all-to-all-start.3 = ((f32[64,128,128]{2,1,0:T(8,128)}), f32[64,128,128]{2,1,0:T(8,128)}, u32[]{:S(2)}, u32[]{:S(2)}) async-start(f32[64,128,128]{2,1,0:T(8,128)} %copy-done.2), calls=%async_computation.3 | async-start | bytes 8388608 | tf_op jit(solution)/shard_map/all_to_all | solution.py:355
  80.9 1.8 add_slices.1
  82.7 52.6 %all-to-all-done.3.moved = f32[64,128,128]{2,1,0:T(8,128)} async-done(((f32[64,128,128]{2,1,0:T(8,128)}), f32[64,128,128]{2,1,0:T(8,128)}, u32[]{:S(2)}, u32[]{:S(2)}) %all-to-all-start.3) | async-done | bytes 4194336 | tf_op jit(solution)/shard_map/all_to_all | solution.py:355
  135.3 2.5 pack_other.1
  137.8 2.7 %collective-permute-start = (f32[4,6,128,128]{3,2,1,0:T(8,128)S(1)}, f32[4,6,128,128]{3,2,1,0:T(8,128)S(1)}, u32[]{:S(2)}, u32[]{:S(2)}) collective-permute-start(f32[4,6,128,128]{3,2,1,0:T(8,128)S(1)} %pack_other.1), channel_id=1, source_target_pairs={{0,64},{64,0},{1,65},{65,1},{2,66},{66,2},{3,67},{67,3},{4,68},{68... | collective-permute-start | bytes 4718600 | tf_op jit(solution)/shard_map/ppermute | solution.py:374
  140.5 1.7 copy-done.13
  142.3 47.2 %invert_factor.1.inverse = f32[640,640]{1,0:T(8,128)S(1)} custom-call(f32[128,5,8,128]{3,2,1,0:T(8,128)S(1)} %bitcast.12), custom_call_target="tpu_custom_call" | custom-call | flops 40000000000 | bytes 4194304 | tf_op jit(solution)/shard_map/invert_factor/pallas_call | solution.py:356
  189.5 1.2 copy-done.14
  190.6 29.8 %all-gather.7.cloned.1.call-done = f32[80,12,8,128]{3,2,1,0:T(8,128)} async-done(((f32[5,12,8,128]{3,2,1,0:T(8,128)}), f32[80,12,8,128]{3,2,1,0:T(8,128)}) %all-gather.7.cloned.1.call-update) | async-done | bytes 3932176 | tf_op jit(solution)/shard_map/all_gather | solution.py:336
  220.4 1.9 copy-done.12
  222.3 1.4 copy-done.15
  223.7 32.8 %eliminate.1.start = f32[9216,128]{1,0:T(8,128)} custom-call(f32[9216,128]{1,0:T(8,128)} %bitcast.6, f32[16,5,12,8,128]{4,3,2,1,0:T(8,128)} %bitcast.13, f32[8,6,128,128]{3,2,1,0:T(8,128)S(1)} %bitcast.11, f32[640,640]{1,0:T(8,128)S(1)} %copy-done.15), custom_call_target="tpu_custom_call" | custom-call | flops 24999999488 | bytes 20971520 | tf_op jit(solution)/shard_map/eliminate/pallas_call | solution.py:375
  256.6 2.3 copy-done.5
  258.9 5.7 %add_children.1 = f32[9216,128]{1,0:T(8,128)} custom-call(s32[2,48]{1,0:T(2,128)S(1)} %copy-done.9, f32[9216,128]{1,0:T(8,128)S(1)} %copy-done.5, f32[64,128,128]{2,1,0:T(8,128)} %all-to-all-done.3.moved, f32[4,6,128,128]{3,2,1,0:T(8,128)S(1)} %collective-permute-done.other), custom_call_target="tpu_custom_call" | custom-call | tf_op jit(solution)/shard_map/add_children/pallas_call | solution.py:389
  (34 shorter events, 4.4 us)
Async XLA Ops:
  6.5 134.0 %all-gather.11.cloned.1.call-start = ((), (), s32[]{:S(2)}) async-start(), calls=%async_computation.6 | async-start | bytes 2641920 | tf_op jit(solution)/shard_map/all_gather | solution.py:326
  6.5 2.3 copy-start
  8.9 1.7 copy-start.3
  10.5 0.7 copy-start.8
  11.2 0.7 copy-start.10
  12.6 45.7 %copy-start.9 = (s32[2,48]{1,0:T(2,128)S(1)}, s32[2,48]{1,0:T(2,128)}, u32[]{:S(2)}) copy-start(s32[2,48]{1,0:T(2,128)} %maps.13) | copy-start | bytes 1156
  38.2 0.7 copy-start.7
  39.0 151.7 %all-gather.9.cloned.1.call-start = ((), (), s32[]{:S(2)}) async-start(), calls=%async_computation.5 | async-start | bytes 3538944 | tf_op jit(solution)/shard_map/all_gather | solution.py:346
  58.3 2.3 copy-start.1
  60.6 5.9 %copy-start.4 = (f32[6,1,128,6,1,128]{5,4,3,2,1,0:T(1,128)S(1)}, f32[6,1,128,6,1,128]{5,4,3,2,1,0:T(1,128)}, u32[]{:S(2)}) copy-start(f32[6,1,128,6,1,128]{5,4,3,2,1,0:T(1,128)} %param.5) | copy-start | bytes 7077892
  60.6 5.9 %copy-start.11 = (s32[2]{0:T(128)S(1)}, s32[2]{0:T(128)}, u32[]{:S(2)}) copy-start(s32[2]{0:T(128)} %orders.3) | copy-start | bytes 28
  61.4 0.7 copy-start.6
  62.2 13.0 %all-to-all-start.1 = ((f32[8,2,5,8,128]{4,3,2,1,0:T(8,128)}), f32[8,2,5,8,128]{4,3,2,1,0:T(8,128)}, u32[]{:S(2)}, u32[]{:S(2)}) async-start(f32[8,2,5,8,128]{4,3,2,1,0:T(8,128)} %copy-done.7), calls=%async_computation.1 | async-start | bytes 655360 | tf_op jit(solution)/shard_map/all_to_all | solution.py:327
  67.5 2.0 copy-start.2
  75.1 60.1 %all-to-all-start.3 = ((f32[64,128,128]{2,1,0:T(8,128)}), f32[64,128,128]{2,1,0:T(8,128)}, u32[]{:S(2)}, u32[]{:S(2)}) async-start(f32[64,128,128]{2,1,0:T(8,128)} %copy-done.2), calls=%async_computation.3 | async-start | bytes 8388608 | tf_op jit(solution)/shard_map/all_to_all | solution.py:355
  80.8 139.6 %all-gather.7.cloned.1.call-start = ((), (), s32[]{:S(2)}) async-start(), calls=%async_computation.4 | async-start | bytes 4177920 | tf_op jit(solution)/shard_map/all_gather | solution.py:336
  137.8 118.8 %collective-permute-start = (f32[4,6,128,128]{3,2,1,0:T(8,128)S(1)}, f32[4,6,128,128]{3,2,1,0:T(8,128)S(1)}, u32[]{:S(2)}, u32[]{:S(2)}) collective-permute-start(f32[4,6,128,128]{3,2,1,0:T(8,128)S(1)} %pack_other.1), channel_id=1, source_target_pairs={{0,64},{64,0},{1,65},{65,1},{2,66},{66,2},{3,67},{67,3},{4,68},{68... | collective-permute-start | bytes 4718600 | tf_op jit(solution)/shard_map/ppermute | solution.py:374
  140.5 1.7 copy-start.13
  189.5 1.2 copy-start.14
  220.4 1.9 copy-start.12
  222.3 1.4 copy-start.15
  256.6 2.3 copy-start.5
Sparse Core Ops, SparseCore 0:
  39.1 93.4 all-gather.10
  134.3 32.9 all-gather.8
  169.4 50.9 all-gather.6

commit v2 on v1

--- a/solution.py
+++ b/solution.py
@@ -12,6 +12,8 @@
 COL_TILES = 12
 CHILD_TILES = 6
 ROWS = ("k", "i")
+PIECES = 8 * (COL_TILES + CHILD_TILES)
+UPPER = [(b, c) for b in range(PT) for c in range(b, PT)]
 HIGHEST = lax.Precision.HIGHEST
 F32 = jnp.float32
 
@@ -46,20 +48,24 @@
     return tile
 
 
-def pack_panel(maps, orders, front, child, out_rows, out_cols):
+def pack_panel(maps, orders, front, child, out, column):
     k, i, j = place()
     order = orders[k]
     cols = lax.broadcasted_iota(jnp.int32, (8, T), 1) + (8 * (CHILD_TILES - 1) + j) * T
     for v in range(16):
         for s in range(COL_TILES):
-            out_rows[v, s] = front[pl.ds(8 * v * COL_TILES + s, 8, stride=COL_TILES), :]
+            out[v, 8 * s:8 * s + 8] = front[pl.ds(8 * v * COL_TILES + s, 8, stride=COL_TILES), :]
         for h in range(CHILD_TILES):
             piece = child[pl.ds(8 * v * CHILD_TILES + h, 8, stride=CHILD_TILES), :]
             if h == CHILD_TILES - 1:
                 piece = jnp.where(cols < order, piece, 0.0)
-            out_rows[v, COL_TILES + h] = piece
+            s = COL_TILES + h
+            out[v, 8 * s:8 * s + 8] = piece
     for g in range(CHILD_TILES):
-        out_cols[(8 * g + i + offset(maps, k, g)) % 16] = child_tile(child, order, i, j, g, 0)
+        tile = child_tile(child, order, i, j, g, 0)
+        out[(8 * g + i + offset(maps, k, g)) % 16, PIECES:] = tile
+    for t in range(ROW_TILES):
+        column[t] = front[pl.ds(t * T * COL_TILES, T, stride=COL_TILES), :]
 
 
 def pack_main(maps, orders, child, out):
@@ -72,36 +78,45 @@
             out[to_i * 8 + to_j] = child_tile(child, order, i, j, g, h)
 
 
-def pack_slices(maps, got, out, lead):
+def pack_slices(maps, got, out):
     j = lax.axis_index("col")
+
+    def piece(source, s):
+        return got[source, 8 * s:8 * s + 8]
+
     for child in range(2):
         for h in range(CHILD_TILES):
             dest = (j + offset(maps, child, h)) % 8
             for b in range(PT):
-                out[dest, child, b] = got[8 * child + b, COL_TILES + h]
+                out[dest, child * PT + b] = piece(8 * child + b, COL_TILES + h)
     for b in range(PT):
-        lead[b] = got[b, 0] + got[b, COL_TILES] + got[8 + b, COL_TILES]
-
-
-def add_slices(maps, got, moved, slab):
+        lead = piece(b, 0) + piece(b, COL_TILES) + piece(8 + b, COL_TILES)
+        for dest in range(8):
+            out[dest, 2 * PT + b] = lead
+
+
+def add_slices(maps, got, moved, slab, lead):
     j = lax.axis_index("col")
+    for n, (b, c) in enumerate(UPPER):
+        piece = moved[c, 2 * PT + b]
+        for v in range(16):
+            lead[v, n] = piece
     for b in range(PT):
         for s in range(COL_TILES):
-            slab[b, s] = got[b, s]
+            slab[b, s] = got[b, 8 * s:8 * s + 8]
     for child in range(2):
         for h in range(CHILD_TILES):
             shift = offset(maps, child, h)
             source = (j - shift) % 8
             s = (8 * h + source + shift) // 8
             for b in range(PT):
-                slab[b, s] = slab[b, s] + moved[source, child, b]
-
-
-def add_column(maps, front, moved, out):
+                slab[b, s] = slab[b, s] + moved[source, child * PT + b]
+
+
+def add_column(maps, start, moved, out):
     k, i, j = place()
     row = k * 8 + i
-    for t in range(ROW_TILES):
-        out[t] = front[pl.ds(t * T * COL_TILES, T, stride=COL_TILES), :]
+    out[...] = start[...]
     for child in range(2):
         for g in range(CHILD_TILES):
             shift = offset(maps, child, g)
@@ -110,14 +125,13 @@
             @pl.when(source < 8)
             def _():
                 t = (8 * g + source + shift) // 16
-                out[t] = out[t] + moved[8 * child + source]
+                out[t] = out[t] + moved[8 * child + source, PIECES:]
 
 
 def invert_factor(lead, out, matrix, work):
-    for b in range(PT):
-        for c in range(PT):
-            for r in range(16):
-                matrix[b * T + 8 * r:b * T + 8 * r + 8, c * T:c * T + T] = lead[r * 8 + c, b]
+    for n, (b, c) in enumerate(UPPER):
+        for r in range(16):
+            matrix[b * T + 8 * r:b * T + 8 * r + 8, c * T:c * T + T] = lead[r, n]
     out[...] = jnp.zeros_like(out)
     sub = lax.broadcasted_iota(jnp.int32, (8, T), 0)
     lane = lax.broadcasted_iota(jnp.int32, (8, T), 1)
@@ -164,14 +178,17 @@
             right = jnp.dot(
                 inverse, matrix[lo:hi, hi:], precision=HIGHEST, preferred_element_type=F32
             )
-            matrix[hi:, hi:] = matrix[hi:, hi:] - lax.dot_general(
-                right, right, (((0,), (0,)), ((), ())),
-                precision=HIGHEST, preferred_element_type=F32,
-            )
-            out[hi:, :hi] = out[hi:, :hi] - lax.dot_general(
-                right, out[lo:hi, :hi], (((0,), (0,)), ((), ())),
-                precision=HIGHEST, preferred_element_type=F32,
-            )
+            for n in range(b + 1, PT):
+                low, high = n * T, n * T + T
+                factor = right[:, low - hi:high - hi]
+                matrix[low:high, low:] = matrix[low:high, low:] - lax.dot_general(
+                    factor, right[:, low - hi:], (((0,), (0,)), ((), ())),
+                    precision=HIGHEST, preferred_element_type=F32,
+                )
+                out[low:high, :hi] = out[low:high, :hi] - lax.dot_general(
+                    factor, out[lo:hi, :hi], (((0,), (0,)), ((), ())),
+                    precision=HIGHEST, preferred_element_type=F32,
+                )
 
 
 SPLITS = ((0, 256), (256, 512), (512, 640))
@@ -258,38 +275,40 @@
 
 def add_children(maps, start, moved, other, out):
     k, i, j = place()
+    t = pl.program_id(0)
     out[...] = start[...]
 
-    def add(child, g, source, shift, tile_of):
-        p = 8 * g + source + shift
+    def add(child, p, tile_of):
         for h in range(CHILD_TILES):
             across = offset(maps, child, h)
             from_j = (j - across) % 8
             q = 8 * h + from_j + across
 
-            @pl.when(jnp.logical_and(p >= PT, q >= PT))
+            @pl.when(q >= PT)
             def _():
-                where = pl.ds(p // 16 * (T * COL_TILES) + q // 8, T, stride=COL_TILES)
+                where = pl.ds(q // 8, T, stride=COL_TILES)
                 out[where, :] = out[where, :] + tile_of(h, from_j)
 
     rank = jnp.int32(0)
     for g in range(CHILD_TILES):
         shift = offset(maps, k, g)
         source = (i - shift) % 8
-
-        @pl.when((8 * g + source + shift) // 8 % 2 == k)
+        p = 8 * g + source + shift
+        mine = jnp.logical_and(p // 8 % 2 == k, p >= PT)
+
+        @pl.when(jnp.logical_and(mine, p // 16 == t))
         def _():
-            add(k, g, source, shift, lambda h, from_j: moved[source * 8 + from_j])
+            add(k, p, lambda h, from_j: moved[source * 8 + from_j])
 
         far = 1 - k
         far_shift = offset(maps, far, g)
-        far_source = (i - far_shift) % 8
-        comes = (8 * g + far_source + far_shift) // 8 % 2 == k
+        far_p = 8 * g + (i - far_shift) % 8 + far_shift
+        comes = far_p // 8 % 2 == k
         here = jnp.minimum(rank, 3)
 
-        @pl.when(comes)
+        @pl.when(jnp.logical_and(jnp.logical_and(comes, far_p >= PT), far_p // 16 == t))
         def _():
-            add(far, g, far_source, far_shift, lambda h, from_j: other[here, h])
+            add(far, far_p, lambda h, from_j: other[here, h])
 
         rank = rank + comes.astype(jnp.int32)
 
@@ -298,43 +317,24 @@
     front = front.reshape(ROW_TILES * T * COL_TILES, T)
     child = child_updates.reshape(CHILD_TILES * T * CHILD_TILES, T)
     maps = child_maps
-    row_slices, column_tiles = pl.pallas_call(
+    panel, column = pl.pallas_call(
         pack_panel,
-        out_shape=(shape(16, 18, 8, T), shape(16, T, T)),
-        grid=(1,),
-        in_specs=[
-            SMEM, SMEM,
-            pl.BlockSpec((T * COL_TILES, T), lambda n: (0, 0)),
-            pl.BlockSpec((CHILD_TILES * T * CHILD_TILES, T), lambda n: (0, 0)),
-        ],
-        out_specs=[
-            pl.BlockSpec((16, 18, 8, T), lambda n: (0, 0, 0, 0)),
-            pl.BlockSpec((16, T, T), lambda n: (0, 0, 0)),
-        ],
+        out_shape=(shape(16, PIECES + T, T), shape(ROW_TILES, T, T)),
+        in_specs=[SMEM, SMEM, VMEM, VMEM],
+        out_specs=[VMEM, VMEM],
         compiler_params=params(24),
         name="pack_panel",
     )(maps, child_orders, front, child)
-    row_slices = lax.all_to_all(row_slices, ROWS, 0, 0, tiled=True)
-    slices, lead = pl.pallas_call(
+    panel = lax.all_to_all(panel, ROWS, 0, 0, tiled=True)
+    slices = pl.pallas_call(
         pack_slices,
-        out_shape=(shape(8, 2, PT, 8, T), shape(PT, 8, T)),
+        out_shape=shape(8, 3 * PT, 8, T),
         in_specs=[SMEM, VMEM],
-        out_specs=[VMEM, VMEM],
+        out_specs=VMEM,
         compiler_params=params(16),
         name="pack_slices",
-    )(maps, row_slices)
-    lead = lax.all_gather(lead, ("k", "i", "col"))
+    )(maps, panel)
     slices = lax.all_to_all(slices, "col", 0, 0, tiled=True)
-    slab = pl.pallas_call(
-        add_slices,
-        out_shape=shape(PT, COL_TILES, 8, T),
-        in_specs=[SMEM, VMEM, VMEM],
-        out_specs=VMEM,
-        compiler_params=params(16),
-        name="add_slices",
-    )(maps, row_slices, slices)
-    across = lax.all_gather(slab, ROWS)
-    column_tiles = lax.all_to_all(column_tiles, ROWS, 0, 0, tiled=True)
     column = pl.pallas_call(
         add_column,
         out_shape=shape(ROW_TILES, T, T),
@@ -342,8 +342,18 @@
         out_specs=VMEM,
         compiler_params=params(24),
         name="add_column",
-    )(maps, front, column_tiles)
+    )(maps, column, panel)
     down = lax.all_gather(column, "col")
+    slab, lead = pl.pallas_call(
+        add_slices,
+        out_shape=(shape(PT, COL_TILES, 8, T), shape(16, len(UPPER), 8, T)),
+        in_specs=[SMEM, VMEM, VMEM],
+        out_specs=[VMEM, VMEM],
+        compiler_params=params(16),
+        name="add_slices",
+    )(maps, panel, slices)
+    across = lax.all_gather(slab, ROWS)
+    lead = lax.all_to_all(lead, ROWS, 0, 0, tiled=True)
     main = pl.pallas_call(
         pack_main,
         out_shape=shape(64, T, T),
@@ -386,11 +396,14 @@
         cost_estimate=pl.CostEstimate(flops=25 * 10**9, bytes_accessed=20 * 2**20, transcendentals=0),
         name="eliminate",
     )(front, across, down, inverse)
+    block = pl.BlockSpec((T * COL_TILES, T), lambda t: (t, 0))
     out = pl.pallas_call(
         add_children,
         out_shape=shape(ROW_TILES * T * COL_TILES, T),
-        in_specs=[SMEM, VMEM, VMEM, VMEM],
-        out_specs=VMEM,
+        grid=(4,),
+        in_specs=[SMEM, block, VMEM, VMEM],
+        out_specs=block,
+        input_output_aliases={1: 0},
         compiler_params=params(32),
         name="add_children",
     )(maps, start, main, other)

time: 273 us -> 254 us (0.930)
  waiting for transfers between devices: 88.1 us -> 65.4 us
  blocking collectives: 43.7 us -> 51.6 us
  local copies, waits for them, and re-layouts: 19.7 us -> 13.6 us
    all_to_all x1, waiting for transfers between devices: 52.6 us -> 4.68 us  [shards(): main = lax.all_to_all(main, ('i', 'col'), 0, 0, tiled=True)]
    all_gather x1, waiting for transfers between devices: 29.8 us -> 51.8 us  [shards(): across = lax.all_gather(slab, ROWS)]
    all_to_all x2, blocking collectives: 43.7 us -> 51.6 us  [the longest x1 35.8 us: shards(): panel = lax.all_to_all(panel, ROWS, 0, 0, tiled=True)]
    unnamed x32 -> x22, local copies, waits for them, and re-layouts: 19.7 us -> 13.6 us
    all_to_all x1, waiting for transfers between devices: 5.65 us -> 8.87 us  [shards(): lead = lax.all_to_all(lead, ROWS, 0, 0, tiled=True)]
    all_to_all x1, starting transfers between devices: 4.36 us -> 7.33 us  [shards(): lead = lax.all_to_all(lead, ROWS, 0, 0, tiled=True)]
  transfers between devices with their start and end apart: 6 -> 5, of which waited for: 3 -> 3; matrix products, arithmetic and copies ran while one was open for 0% -> 0% of each run, Pallas kernels for 32% -> 34%
where the time goes in v2:
time: 254 us; the launch traced here: 253 us
  Pallas kernels  93.8 us (37%)
  waiting for transfers between devices  65.4 us (26%)
  blocking collectives  51.6 us (20%)
  starting transfers between devices  15.3 us (6%)
  local copies, waits for them, and re-layouts  13.6 us (5%)
  between operations  13.5 us (5%)
    all_gather x1, waiting for transfers between devices, shards(): across = lax.all_gather(slab, ROWS)  51.8 us
    pallas_call x1, Pallas kernels, shards(): pl.pallas_call(invert_factor, out_shape=shape(PT * T, PT * T), in_specs=[...  46.4 us
    all_to_all x1, blocking collectives, shards(): panel = lax.all_to_all(panel, ROWS, 0, 0, tiled=True)  35.8 us
    pallas_call x1, Pallas kernels, shards(): pl.pallas_call(eliminate, out_shape=shape(ROW_TILES * T * COL_TILES, T),...  32.8 us
    all_to_all x1, blocking collectives, shards(): slices = lax.all_to_all(slices, 'col', 0, 0, tiled=True)  15.7 us
    unnamed x22, local copies, waits for them, and re-layouts  13.6 us
    all_to_all x1, waiting for transfers between devices, shards(): lead = lax.all_to_all(lead, ROWS, 0, 0, tiled=True)  8.87 us
    all_to_all x1, starting transfers between devices, shards(): lead = lax.all_to_all(lead, ROWS, 0, 0, tiled=True)  7.33 us
  transfers between devices with their start and end apart: 5, of which 3 were waited for; matrix products, arithmetic and copies ran while one was open for 0% of the time, Pallas kernels for 34%

profile of v2, /device:TPU:16, one launch (start us, length us, event | category | flops | bytes accessed | tf_op | source)
XLA Modules:
  0.0 253.2 jit_solution(8751344113481006808)
XLA Ops:
  6.5 1.7 copy-done.1
  8.2 2.3 copy-done.3
  10.5 0.7 copy-done.4
  11.9 0.7 pack_panel.1
  12.6 35.8 %all_to_all.20.got.moved = f32[16,272,128]{2,1,0:T(8,128)S(1)} all-to-all(f32[16,272,128]{2,1,0:T(8,128)S(1)} %get-tuple-element.9), channel_id=1, replica_groups=mesh['k'=2,'i'=8,'col'=8] {'k','i'}, dimensions={0} | all-to-all | bytes 4456448 | tf_op jit(solution)/shard_map/all_to_all | solution.py:328
  48.4 1.5 add_column.1
  50.7 15.7 %all_to_all.21.moved = f32[8,15,8,128]{3,2,1,0:T(8,128)S(1)} all-to-all(f32[8,15,8,128]{3,2,1,0:T(8,128)S(1)} %pack_slices.1), channel_id=1, replica_groups=mesh['k'=2,'i'=8,'col'=8] {'col'}, dimensions={0} | all-to-all | bytes 983040 | tf_op jit(solution)/shard_map/all_to_all | solution.py:337
  66.4 1.8 add_slices.1
  68.2 7.3 %all-to-all-start.2 = ((f32[16,15,8,128]{3,2,1,0:T(8,128)}), f32[16,15,8,128]{3,2,1,0:T(8,128)S(1)}, u32[]{:S(2)}, u32[]{:S(2)}) async-start(f32[16,15,8,128]{3,2,1,0:T(8,128)} %get-tuple-element.12), calls=%async_computation.2 | async-start | bytes 1966080 | tf_op jit(solution)/shard_map/all_to_all | solution.py:356
  75.6 1.7 copy-done.2
  77.3 0.9 pack_main.1
  78.2 2.0 copy-done
  80.2 8.9 %all-to-all-done.2.lead = f32[16,15,8,128]{3,2,1,0:T(8,128)S(1)} async-done(((f32[16,15,8,128]{3,2,1,0:T(8,128)}), f32[16,15,8,128]{3,2,1,0:T(8,128)S(1)}, u32[]{:S(2)}, u32[]{:S(2)}) %all-to-all-start.2) | async-done | bytes 983072 | tf_op jit(solution)/shard_map/all_to_all | solution.py:356
  89.1 5.8 %all-to-all-start.3 = ((f32[64,128,128]{2,1,0:T(8,128)}), f32[64,128,128]{2,1,0:T(8,128)}, u32[]{:S(2)}, u32[]{:S(2)}) async-start(f32[64,128,128]{2,1,0:T(8,128)} %copy-done), calls=%async_computation.3 | async-start | bytes 8388608 | tf_op jit(solution)/shard_map/all_to_all | solution.py:365
  94.9 46.4 %invert_factor.1.inverse = f32[640,640]{1,0:T(8,128)S(1)} custom-call(f32[16,15,8,128]{3,2,1,0:T(8,128)S(1)} %all-to-all-done.2.lead), custom_call_target="tpu_custom_call" | custom-call | flops 40000000000 | bytes 4194304 | tf_op jit(solution)/shard_map/invert_factor/pallas_call | solution.py:366
  141.3 1.2 copy-done.9
  142.5 4.7 %all-to-all-done.3.moved = f32[64,128,128]{2,1,0:T(8,128)} async-done(((f32[64,128,128]{2,1,0:T(8,128)}), f32[64,128,128]{2,1,0:T(8,128)}, u32[]{:S(2)}, u32[]{:S(2)}) %all-to-all-start.3) | async-done | bytes 4194336 | tf_op jit(solution)/shard_map/all_to_all | solution.py:365
  147.2 2.5 pack_other.1
  149.7 2.1 collective-permute-start
  151.8 51.8 %all-gather.5.cloned.1.call-done = f32[80,12,8,128]{3,2,1,0:T(8,128)} async-done(((f32[5,12,8,128]{3,2,1,0:T(8,128)}), f32[80,12,8,128]{3,2,1,0:T(8,128)}) %all-gather.5.cloned.1.call-update) | async-done | bytes 3932176 | tf_op jit(solution)/shard_map/all_gather | solution.py:355
  203.7 1.9 copy-done.8
  205.5 1.4 copy-done.10
  207.0 32.8 %eliminate.1.start = f32[9216,128]{1,0:T(8,128)} custom-call(f32[9216,128]{1,0:T(8,128)} %bitcast.7, f32[16,5,12,8,128]{4,3,2,1,0:T(8,128)} %bitcast.10, f32[8,6,128,128]{3,2,1,0:T(8,128)S(1)} %bitcast.9, f32[640,640]{1,0:T(8,128)S(1)} %copy-done.10), custom_call_target="tpu_custom_call" | custom-call | flops 24999999488 | bytes 20971520 | tf_op jit(solution)/shard_map/eliminate/pallas_call | solution.py:385
  239.8 6.6 %add_children.1 = f32[9216,128]{1,0:T(8,128)} custom-call(s32[2,48]{1,0:T(2,128)S(1)} %copy-done.5, f32[9216,128]{1,0:T(8,128)} %eliminate.1.start, f32[64,128,128]{2,1,0:T(8,128)} %all-to-all-done.3.moved, f32[4,6,128,128]{3,2,1,0:T(8,128)S(1)} %collective-permute-done.other), custom_call_target="tpu_custom_call", output_to_operand_aliasing={{}: (1, {})} | custom-call | tf_op jit(solution)/shard_map/add_children/pallas_call | solution.py:400
  (21 shorter events, 1.4 us)
Async XLA Ops:
  6.5 145.3 %all-gather.7.cloned.1.call-start = ((), (), s32[]{:S(2)}) async-start(), calls=%async_computation.5 | async-start | bytes 3538944 | tf_op jit(solution)/shard_map/all_gather | solution.py:346
  6.5 1.7 copy-start.1
  8.2 2.3 copy-start.3
  10.5 0.7 copy-start.4
  11.2 0.7 copy-start.6
  12.6 37.5 %copy-start.5 = (s32[2,48]{1,0:T(2,128)S(1)}, s32[2,48]{1,0:T(2,128)}, u32[]{:S(2)}) copy-start(s32[2,48]{1,0:T(2,128)} %maps.13) | copy-start | bytes 1156
  50.0 153.6 %all-gather.5.cloned.1.call-start = ((), (), s32[]{:S(2)}) async-start(), calls=%async_computation.4 | async-start | bytes 4177920 | tf_op jit(solution)/shard_map/all_gather | solution.py:355
  50.7 24.9 %copy-start.7 = (s32[2]{0:T(128)S(1)}, s32[2]{0:T(128)}, u32[]{:S(2)}) copy-start(s32[2]{0:T(128)} %orders.3) | copy-start | bytes 28
  68.2 20.8 %all-to-all-start.2 = ((f32[16,15,8,128]{3,2,1,0:T(8,128)}), f32[16,15,8,128]{3,2,1,0:T(8,128)S(1)}, u32[]{:S(2)}, u32[]{:S(2)}) async-start(f32[16,15,8,128]{3,2,1,0:T(8,128)} %get-tuple-element.12), calls=%async_computation.2 | async-start | bytes 1966080 | tf_op jit(solution)/shard_map/all_to_all | solution.py:356
  75.6 1.7 copy-start.2
  78.2 2.0 copy-start
  89.1 58.2 %all-to-all-start.3 = ((f32[64,128,128]{2,1,0:T(8,128)}), f32[64,128,128]{2,1,0:T(8,128)}, u32[]{:S(2)}, u32[]{:S(2)}) async-start(f32[64,128,128]{2,1,0:T(8,128)} %copy-done), calls=%async_computation.3 | async-start | bytes 8388608 | tf_op jit(solution)/shard_map/all_to_all | solution.py:365
  141.3 1.2 copy-start.9
  149.7 90.1 %collective-permute-start = (f32[4,6,128,128]{3,2,1,0:T(8,128)S(1)}, f32[4,6,128,128]{3,2,1,0:T(8,128)S(1)}, u32[]{:S(2)}, u32[]{:S(2)}) collective-permute-start(f32[4,6,128,128]{3,2,1,0:T(8,128)S(1)} %pack_other.1), channel_id=1, source_target_pairs={{0,64},{64,0},{1,65},{65,1},{2,66},{66,2},{3,67},{67,3},{4,68},{68... | collective-permute-start | bytes 4718600 | tf_op jit(solution)/shard_map/ppermute | solution.py:384
  203.7 1.9 copy-start.8
  205.5 1.4 copy-start.10
Sparse Core Ops, SparseCore 0:
  50.1 28.5 all-gather.6
  81.0 122.6 all-gather.4

commit v3 on v2

v3 whole, which is shorter than its diff:
```python
import jax
import jax.numpy as jnp
from jax import lax
from jax.experimental import pallas as pl
from jax.experimental.pallas import tpu as pltpu
from jax.sharding import Mesh
from jax.sharding import PartitionSpec as P

T = 128
PT = 5
ROW_TILES = 6
COL_TILES = 12
CHILD_TILES = 6
ROWS = ("k", "i")
PIECES = 8 * (COL_TILES + CHILD_TILES)
UPPER = [(b, c) for b in range(PT) for c in range(b, PT)]
GROUP = 32
HIGHEST = lax.Precision.HIGHEST
F32 = jnp.float32
BF16 = jnp.bfloat16

VMEM = pl.BlockSpec(memory_space=pltpu.VMEM)
SMEM = pl.BlockSpec(memory_space=pltpu.SMEM)


def shape(*dims):
    return jax.ShapeDtypeStruct(dims, F32)


def params(mib):
    return pltpu.CompilerParams(vmem_limit_bytes=mib * 2**20)


def place():
    return lax.axis_index("k"), lax.axis_index("i"), lax.axis_index("col")


def offset(maps, child, run):
    return maps[child, 8 * run] - 8 * run


def child_tile(child, order, i, j, g, h):
    tile = child[pl.ds(g * T * CHILD_TILES + h, T, stride=CHILD_TILES), :]
    if g == CHILD_TILES - 1:
        rows = lax.broadcasted_iota(jnp.int32, (T, T), 0) + (8 * g + i) * T
        tile = jnp.where(rows < order, tile, 0.0)
    if h == CHILD_TILES - 1:
        cols = lax.broadcasted_iota(jnp.int32, (T, T), 1) + (8 * h + j) * T
        tile = jnp.where(cols < order, tile, 0.0)
    return tile


def pack_panel(maps, orders, front, child, out, column):
    k, i, j = place()
    order = orders[k]
    cols = lax.broadcasted_iota(jnp.int32, (8, T), 1) + (8 * (CHILD_TILES - 1) + j) * T
    for v in range(16):
        for s in range(COL_TILES):
            out[v, 8 * s:8 * s + 8] = front[pl.ds(8 * v * COL_TILES + s, 8, stride=COL_TILES), :]
        for h in range(CHILD_TILES):
            piece = child[pl.ds(8 * v * CHILD_TILES + h, 8, stride=CHILD_TILES), :]
            if h == CHILD_TILES - 1:
                piece = jnp.where(cols < order, piece, 0.0)
            s = COL_TILES + h
            out[v, 8 * s:8 * s + 8] = piece
    for g in range(CHILD_TILES):
        tile = child_tile(child, order, i, j, g, 0)
        out[(8 * g + i + offset(maps, k, g)) % 16, PIECES:] = tile
    for t in range(ROW_TILES):
        column[t] = front[pl.ds(t * T * COL_TILES, T, stride=COL_TILES), :]


def pack_main(maps, orders, child, out):
    k, i, j = place()
    order = orders[k]
    for g in range(CHILD_TILES):
        to_i = (i + offset(maps, k, g)) % 8
        for h in range(CHILD_TILES):
            to_j = (j + offset(maps, k, h)) % 8
            out[to_i * 8 + to_j] = child_tile(child, order, i, j, g, h)


def pack_slices(maps, orders, got, child, out, main):
    j = lax.axis_index("col")

    pack_main(maps, orders, child, main)

    def piece(source, s):
        return got[source, 8 * s:8 * s + 8]

    for child in range(2):
        for h in range(CHILD_TILES):
            dest = (j + offset(maps, child, h)) % 8
            for b in range(PT):
                out[dest, child * PT + b] = piece(8 * child + b, COL_TILES + h)
    for b in range(PT):
        lead = piece(b, 0) + piece(b, COL_TILES) + piece(8 + b, COL_TILES)
        for dest in range(8):
            out[dest, 2 * PT + b] = lead


def add_slices(maps, got, moved, slab):
    j = lax.axis_index("col")
    for b in range(PT):
        for s in range(COL_TILES):
            slab[b, s] = got[b, 8 * s:8 * s + 8]
    for child in range(2):
        for h in range(CHILD_TILES):
            shift = offset(maps, child, h)
            source = (j - shift) % 8
            s = (8 * h + source + shift) // 8
            for b in range(PT):
                slab[b, s] = slab[b, s] + moved[source, child * PT + b]


def add_column(maps, start, moved, out):
    k, i, j = place()
    row = k * 8 + i
    out[...] = start[...]
    for child in range(2):
        for g in range(CHILD_TILES):
            shift = offset(maps, child, g)
            source = (row - 8 * g - shift) % 16

            @pl.when(source < 8)
            def _():
                t = (8 * g + source + shift) // 16
                out[t] = out[t] + moved[8 * child + source, PIECES:]


def reciprocal(x):
    y = pl.reciprocal(x, approx=True)
    y = y * (2.0 - x * y)
    return y * (2.0 - x * y)


def invert_factor(lead, out, matrix, work):
    for n, (b, c) in enumerate(UPPER):
        for r in range(16):
            matrix[b * T + 8 * r:b * T + 8 * r + 8, c * T:c * T + T] = lead[r, n]
    out[...] = jnp.zeros_like(out)
    sub = lax.broadcasted_iota(jnp.int32, (8, T), 0)
    eye = (
        lax.broadcasted_iota(jnp.int32, (T, T), 0) == lax.broadcasted_iota(jnp.int32, (T, T), 1)
    ).astype(F32)
    for b in range(PT):
        lo, hi = b * T, b * T + T
        work[:, :T] = matrix[lo:hi, lo:hi]
        work[:, T:] = eye
        for base in range(0, T, GROUP):
            rows = [work[base + 8 * q:base + 8 * q + 8, :T] for q in range(GROUP // 8)]
            other = [work[base + 8 * q:base + 8 * q + 8, T:] for q in range(GROUP // 8)]
            inverses = []
            for p in range(GROUP // 8):
                first = base + 8 * p
                after = range(p, GROUP // 8)
                columns = {
                    q: [
                        jnp.broadcast_to(rows[q][:, first + m:first + m + 1], (8, T))
                        for m in range(8)
                    ]
                    for q in after
                }
                pivots = jnp.ones((8, T), F32)
                for m in range(8):
                    pivot = jnp.broadcast_to(columns[p][m][m:m + 1, :], (8, T))
                    pivots = jnp.where(sub == m, pivot, pivots)
                    over = reciprocal(pivot)
                    row = jnp.broadcast_to(rows[p][m:m + 1, :], (8, T))
                    mate = jnp.broadcast_to(other[p][m:m + 1, :], (8, T))
                    for n in range(m + 1, 8):
                        head = jnp.broadcast_to(columns[p][n][m:m + 1, :], (8, T))
                        for q in after:
                            scale = columns[q][m] * over
                            if q == p:
                                scale = jnp.where(sub > m, scale, 0.0)
                            columns[q][n] = columns[q][n] - scale * head
                    for q in after:
                        scale = columns[q][m] * over
                        if q == p:
                            if m == 7:
                                continue
                            scale = jnp.where(sub > m, scale, 0.0)
                        rows[q] = rows[q] - scale * row
                        other[q] = other[q] - scale * mate
                out[lo + first:lo + first + 8, lo:hi] = other[p] * lax.rsqrt(pivots)
                inverses.append(1.0 / pivots)
            if base + GROUP < T:
                scaled = jnp.concatenate([x * y for x, y in zip(rows, inverses)], axis=0)
                both = jnp.concatenate(
                    [jnp.concatenate(rows, axis=0), jnp.concatenate(other, axis=0)], axis=1
                )
                change = jnp.dot(
                    scaled.T[base + GROUP:, :], both,
                    precision=HIGHEST, preferred_element_type=F32,
                )
                work[base + GROUP:, :] = work[base + GROUP:, :] - change
        inverse = out[lo:hi, lo:hi]
        if b > 0:
            out[lo:hi, :lo] = jnp.dot(
                inverse, out[lo:hi, :lo], precision=HIGHEST, preferred_element_type=F32
            )
        if b < PT - 1:
            right = jnp.dot(
                inverse, matrix[lo:hi, hi:], precision=HIGHEST, preferred_element_type=F32
            )
            for n in range(b + 1, PT):
                low, high = n * T, n * T + T
                factor = right[:, low - hi:high - hi]
                matrix[low:high, low:] = matrix[low:high, low:] - lax.dot_general(
                    factor, right[:, low - hi:], (((0,), (0,)), ((), ())),
                    precision=HIGHEST, preferred_element_type=F32,
                )
                out[low:high, :hi] = out[low:high, :hi] - lax.dot_general(
                    factor, out[lo:hi, :hi], (((0,), (0,)), ((), ())),
                    precision=HIGHEST, preferred_element_type=F32,
                )


SPLITS = ((0, 256), (256, 512), (512, 640))
WIDE = 512


def halves(x):
    high = x.astype(BF16)
    return high, (x - high.astype(F32)).astype(BF16)


def product(a, b):
    (a_high, a_low), (b_high, b_low) = a, b
    small = jnp.dot(a_high, b_low, preferred_element_type=F32) + jnp.dot(
        a_low, b_high, preferred_element_type=F32
    )
    return jnp.dot(a_high, b_high, preferred_element_type=F32) + small


def eliminate(
    maps, front, across, down, inverse, moved, other, out,
    pivot_high, pivot_low, inverse_high, inverse_low, upper_high, upper_low, lower,
):
    k, i, j = place()
    row = k * 8 + i
    t = pl.program_id(0)

    @pl.when(t == 0)
    def _():
        for b in range(PT):
            for s in range(COL_TILES):
                tile = across[:, b, s].reshape(T, T)
                high, low = halves(tile)
                pivot_high[b * T:b * T + T, s * T:s * T + T] = high
                pivot_low[b * T:b * T + T, s * T:s * T + T] = low
        high, low = halves(inverse[...])
        inverse_high[...] = high
        inverse_low[...] = low

        def solve_upper(n, carry):
            part = pl.ds(pl.multiple_of(n * WIDE, WIDE), WIDE)
            for lo, hi in SPLITS:
                high, low = halves(product(
                    (inverse_high[lo:hi, :hi], inverse_low[lo:hi, :hi]),
                    (pivot_high[:hi, part], pivot_low[:hi, part]),
                ))
                upper_high[lo:hi, part] = high
                upper_low[lo:hi, part] = low
            return carry

        lax.fori_loop(0, COL_TILES * T // WIDE, solve_upper, 0)

        def solve_lower(t, carry):
            mine = jnp.concatenate([down[b, t] for b in range(PT)], axis=1)
            part = pl.ds(pl.multiple_of(t * T, T), T)
            for lo, hi in SPLITS:
                lower[part, lo:hi] = lax.dot_general(
                    mine[:, :hi], inverse[lo:hi, :hi], (((1,), (1,)), ((), ())),
                    precision=HIGHEST, preferred_element_type=F32,
                )
            return carry

        lax.fori_loop(0, ROW_TILES, solve_lower, 0)

    mine = lower[pl.ds(pl.multiple_of(t * T, T), T), :]
    mine_halves = halves(mine)
    for n in range(COL_TILES * T // WIDE):
        change = product(
            mine_halves,
            (upper_high[:, n * WIDE:n * WIDE + WIDE], upper_low[:, n * WIDE:n * WIDE + WIDE]),
        )
        for s in range(WIDE // T):
            where = pl.ds(n * (WIDE // T) + s, T, stride=COL_TILES)
            out[where, :] = front[where, :] - change[:, s * T:s * T + T]

    add_children(maps, moved, other, out)
    first = jnp.logical_and(t == 0, row < PT)

    @pl.when(first)
    def _():
        for s in range(COL_TILES):
            out[pl.ds(s, T, stride=COL_TILES), :] = jnp.zeros((T, T), F32)

    @pl.when(j < PT)
    def _():
        part = pl.ds(pl.multiple_of(t * T, T), T)
        tile = lower[part, pl.ds(pl.multiple_of(j * T, T), T)]
        x = lax.broadcasted_iota(jnp.int32, (T, T), 0) + (16 * t + row) * T
        y = lax.broadcasted_iota(jnp.int32, (T, T), 1) + j * T
        out[pl.ds(0, T, stride=COL_TILES), :] = jnp.where(x >= y, tile, 0.0)


def pack_other(maps, moved, slices, out, lead):
    k, i, j = place()
    for n, (b, c) in enumerate(UPPER):
        piece = slices[c, 2 * PT + b]
        for v in range(16):
            lead[v, n] = piece
    rank = jnp.int32(0)
    for g in range(CHILD_TILES):
        shift = offset(maps, k, g)
        source = (i - shift) % 8
        leaves = (8 * g + source + shift) // 8 % 2 != k
        here = jnp.minimum(rank, 3)

        @pl.when(leaves)
        def _():
            for h in range(CHILD_TILES):
                out[here, h] = moved[source * 8 + (j - offset(maps, k, h)) % 8]

        rank = rank + leaves.astype(jnp.int32)


def add_children(maps, moved, other, out):
    k, i, j = place()
    t = pl.program_id(0)

    def add(child, tile_of):
        for h in range(CHILD_TILES):
            across = offset(maps, child, h)
            from_j = (j - across) % 8
            where = pl.ds((8 * h + from_j + across) // 8, T, stride=COL_TILES)
            out[where, :] = out[where, :] + tile_of(h, from_j)

    rank = jnp.int32(0)
    for g in range(CHILD_TILES):
        shift = offset(maps, k, g)
        source = (i - shift) % 8
        p = 8 * g + source + shift
        mine = p // 8 % 2 == k

        @pl.when(jnp.logical_and(mine, p // 16 == t))
        def _():
            add(k, lambda h, from_j: moved[source * 8 + from_j])

        far = 1 - k
        far_shift = offset(maps, far, g)
        far_p = 8 * g + (i - far_shift) % 8 + far_shift
        comes = far_p // 8 % 2 == k
        here = jnp.minimum(rank, 3)

        @pl.when(jnp.logical_and(comes, far_p // 16 == t))
        def _():
            add(far, lambda h, from_j: other[here, h])

        rank = rank + comes.astype(jnp.int32)


def shards(front, child_updates, child_maps, child_orders):
    front = front.reshape(ROW_TILES * T * COL_TILES, T)
    child = child_updates.reshape(CHILD_TILES * T * CHILD_TILES, T)
    maps = child_maps
    panel, column = pl.pallas_call(
        pack_panel,
        out_shape=(shape(16, PIECES + T, T), shape(ROW_TILES, T, T)),
        in_specs=[SMEM, SMEM, VMEM, VMEM],
        out_specs=[VMEM, VMEM],
        compiler_params=params(24),
        name="pack_panel",
    )(maps, child_orders, front, child)
    panel = lax.all_to_all(panel, ROWS, 0, 0, tiled=True)
    slices, main = pl.pallas_call(
        pack_slices,
        out_shape=(shape(8, 3 * PT, 8, T), shape(64, T, T)),
        in_specs=[SMEM, SMEM, VMEM, VMEM],
        out_specs=[VMEM, VMEM],
        compiler_params=params(24),
        name="pack_slices",
    )(maps, child_orders, panel, child)
    slices = lax.all_to_all(slices, "col", 0, 0, tiled=True)
    column = pl.pallas_call(
        add_column,
        out_shape=shape(ROW_TILES, T, T),
        in_specs=[SMEM, VMEM, VMEM],
        out_specs=VMEM,
        compiler_params=params(24),
        name="add_column",
    )(maps, column, panel)
    down = lax.all_gather(column, "col")
    slab = pl.pallas_call(
        add_slices,
        out_shape=shape(PT, COL_TILES, 8, T),
        in_specs=[SMEM, VMEM, VMEM],
        out_specs=VMEM,
        compiler_params=params(16),
        name="add_slices",
    )(maps, panel, slices)
    across = lax.all_gather(slab, ROWS)
    main = lax.all_to_all(main, ("i", "col"), 0, 0, tiled=True)
    other, lead = pl.pallas_call(
        pack_other,
        out_shape=(shape(4, CHILD_TILES, T, T), shape(16, len(UPPER), 8, T)),
        in_specs=[SMEM, VMEM, VMEM],
        out_specs=[VMEM, VMEM],
        compiler_params=params(24),
        name="pack_other",
    )(maps, main, slices)
    lead = lax.all_to_all(lead, ROWS, 0, 0, tiled=True)
    other = lax.ppermute(other, "k", [(0, 1), (1, 0)])
    inverse = pl.pallas_call(
        invert_factor,
        out_shape=shape(PT * T, PT * T),
        in_specs=[VMEM],
        out_specs=VMEM,
        scratch_shapes=[pltpu.VMEM((PT * T, PT * T), F32), pltpu.VMEM((T, 2 * T), F32)],
        compiler_params=params(32),
        cost_estimate=pl.CostEstimate(flops=40 * 10**9, bytes_accessed=4 * 2**20, transcendentals=0),
        name="invert_factor",
    )(lead)
    block = pl.BlockSpec((T * COL_TILES, T), lambda t: (t, 0))
    out = pl.pallas_call(
        eliminate,
        out_shape=shape(ROW_TILES * T * COL_TILES, T),
        grid=(ROW_TILES,),
        in_specs=[SMEM, block] + [VMEM] * 5,
        out_specs=block,
        scratch_shapes=[
            pltpu.VMEM((PT * T, COL_TILES * T), BF16),
            pltpu.VMEM((PT * T, COL_TILES * T), BF16),
            pltpu.VMEM((PT * T, PT * T), BF16),
            pltpu.VMEM((PT * T, PT * T), BF16),
            pltpu.VMEM((PT * T, COL_TILES * T), BF16),
            pltpu.VMEM((PT * T, COL_TILES * T), BF16),
            pltpu.VMEM((ROW_TILES * T, PT * T), F32),
        ],
        compiler_params=params(40),
        cost_estimate=pl.CostEstimate(flops=15 * 10**9, bytes_accessed=20 * 2**20, transcendentals=0),
        name="eliminate",
    )(maps, front, across, down, inverse, main, other)
    return out.reshape(ROW_TILES, 1, T, COL_TILES, 1, T)


def solution(mesh):
    split = Mesh(mesh.devices.reshape(2, 8, 8), ("k", "i", "col"))
    tiles = P(None, ROWS, None, None, "col", None)
    return jax.shard_map(
        shards, mesh=split, in_specs=(tiles, tiles, P(), P()), out_specs=tiles, check_vma=False
    )
```

time: 254 us -> 245 us (0.965); the launches traced: 253 us -> 241 us
  Pallas kernels: 93.8 us -> 59.3 us
  waiting for transfers between devices: 65.4 us -> 83.3 us
  blocking collectives: 51.6 us -> 55.2 us
  local copies, waits for them, and re-layouts: 13.6 us -> 16.8 us
    all_gather x1, waiting for transfers between devices: 51.8 us -> 0.92 us  [shards(): across = lax.all_gather(slab, ROWS)]
    all_to_all x1, waiting for transfers between devices: 4.68 us -> 52.4 us  [shards(): main = lax.all_to_all(main, ('i', 'col'), 0, 0, tiled=True)]
    pallas_call x1, Pallas kernels: 46.4 us -> 27.6 us  [shards(): pl.pallas_call(invert_factor, out_shape=shape(PT * T, PT * T), in_specs=[...]
    all_to_all x1, waiting for transfers between devices: 8.87 us -> 23.1 us  [shards(): lead = lax.all_to_all(lead, ROWS, 0, 0, tiled=True)]
    pallas_call x1, Pallas kernels: 32.8 us -> 23.7 us  [shards(): pl.pallas_call(eliminate, out_shape=shape(ROW_TILES * T * COL_TILES, T),...]
    ppermute x1, waiting for transfers between devices: 0.01 us -> 6.84 us  [shards(): other = lax.ppermute(other, 'k', [(0, 1), (1, 0)])]
    pallas_call x5 -> x3, Pallas kernels: 12.3 us -> 5.75 us  [the longest x1 3.43 us: shards(): pl.pallas_call(pack_other, out_shape=(shape(4, CHILD_TILES, T, T), shape(...]
    all_to_all x1, blocking collectives: 15.7 us -> 19.4 us  [shards(): slices = lax.all_to_all(slices, 'col', 0, 0, tiled=True)]
  transfers between devices with their start and end apart: 5 -> 5, of which waited for: 3 -> 4; matrix products, arithmetic and copies ran while one was open for 0% -> 0% of each run, Pallas kernels for 34% -> 14%
where the time goes in v3:
time: 245 us; the launch traced here: 241 us
  waiting for transfers between devices  83.3 us (34%)
  Pallas kernels  59.3 us (24%)
  blocking collectives  55.2 us (23%)
  local copies, waits for them, and re-layouts  16.8 us (7%)
  between operations  13.5 us (6%)
  starting transfers between devices  13.2 us (5%)
    all_to_all x1, waiting for transfers between devices, shards(): main = lax.all_to_all(main, ('i', 'col'), 0, 0, tiled=True)  52.4 us
    all_to_all x1, blocking collectives, shards(): panel = lax.all_to_all(panel, ROWS, 0, 0, tiled=True)  35.8 us
    pallas_call x1, Pallas kernels, shards(): pl.pallas_call(invert_factor, out_shape=shape(PT * T, PT * T), in_specs=[...  27.6 us
    pallas_call x1, Pallas kernels, shards(): pl.pallas_call(eliminate, out_shape=shape(ROW_TILES * T * COL_TILES, T),...  23.7 us
    all_to_all x1, waiting for transfers between devices, shards(): lead = lax.all_to_all(lead, ROWS, 0, 0, tiled=True)  23.1 us
    all_to_all x1, blocking collectives, shards(): slices = lax.all_to_all(slices, 'col', 0, 0, tiled=True)  19.4 us
    unnamed x26, local copies, waits for them, and re-layouts  16.8 us
    all_to_all x1, starting transfers between devices, shards(): lead = lax.all_to_all(lead, ROWS, 0, 0, tiled=True)  7.13 us
  transfers between devices with their start and end apart: 5, of which 4 were waited for; matrix products, arithmetic and copies ran while one was open for 0% of the time, Pallas kernels for 14%

profile of v3, /device:TPU:16, one launch (start us, length us, event | category | flops | bytes accessed | tf_op | source)
XLA Modules:
  0.0 241.2 jit_solution(10321917500474530995)
XLA Ops:
  6.5 1.7 copy-done
  8.2 2.3 copy-done.2
  11.9 0.7 pack_panel.1
  12.6 35.8 %all_to_all.20.got.moved = f32[16,272,128]{2,1,0:T(8,128)S(1)} all-to-all(f32[16,272,128]{2,1,0:T(8,128)S(1)} %get-tuple-element.11), channel_id=1, replica_groups=mesh['k'=2,'i'=8,'col'=8] {'k','i'}, dimensions={0} | all-to-all | bytes 4456448 | tf_op jit(solution)/shard_map/all_to_all | solution.py:378
  48.4 1.6 add_column.1
  50.1 1.7 copy-done.1
  51.7 1.0 pack_slices.1
  52.7 2.0 copy-done.3
  54.7 19.4 %all_to_all.21.moved.slices = f32[8,15,8,128]{3,2,1,0:T(8,128)S(1)} all-to-all(f32[8,15,8,128]{3,2,1,0:T(8,128)S(1)} %get-tuple-element.12), channel_id=1, replica_groups=mesh['k'=2,'i'=8,'col'=8] {'col'}, dimensions={0} | all-to-all | bytes 983040 | tf_op jit(solution)/shard_map/all_to_all | solution.py:387
  74.1 5.7 %all-to-all-start.2 = ((f32[64,128,128]{2,1,0:T(8,128)}), f32[64,128,128]{2,1,0:T(8,128)}, u32[]{:S(2)}, u32[]{:S(2)}) async-start(f32[64,128,128]{2,1,0:T(8,128)} %copy-done.3), calls=%async_computation.2 | async-start | bytes 8388608 | tf_op jit(solution)/shard_map/all_to_all | solution.py:406
  79.8 1.4 add_slices.1
  81.2 52.4 %all-to-all-done.2.moved = f32[64,128,128]{2,1,0:T(8,128)} async-done(((f32[64,128,128]{2,1,0:T(8,128)}), f32[64,128,128]{2,1,0:T(8,128)}, u32[]{:S(2)}, u32[]{:S(2)}) %all-to-all-start.2) | async-done | bytes 4194336 | tf_op jit(solution)/shard_map/all_to_all | solution.py:406
  133.6 3.4 %pack_other.1 = (f32[4,6,128,128]{3,2,1,0:T(8,128)S(1)}, f32[16,15,8,128]{3,2,1,0:T(8,128)}) custom-call(s32[2,48]{1,0:T(2,128)S(1)} %copy-done.5, f32[64,128,128]{2,1,0:T(8,128)} %all-to-all-done.2.moved, f32[8,15,8,128]{3,2,1,0:T(8,128)S(1)} %all_to_all.21.moved.slices), custom_call_target="tpu_custom_call" | custom-call | tf_op jit(solution)/shard_map/pack_other/pallas_call | solution.py:407
  137.0 1.2 copy-done.10
  138.2 7.1 %all-to-all-start.3 = ((f32[16,15,8,128]{3,2,1,0:T(8,128)}), f32[16,15,8,128]{3,2,1,0:T(8,128)S(1)}, u32[]{:S(2)}, u32[]{:S(2)}) async-start(f32[16,15,8,128]{3,2,1,0:T(8,128)} %get-tuple-element.15), calls=%async_computation.3 | async-start | bytes 1966080 | tf_op jit(solution)/shard_map/all_to_all | solution.py:415
  145.7 23.1 %all-to-all-done.3.lead = f32[16,15,8,128]{3,2,1,0:T(8,128)S(1)} async-done(((f32[16,15,8,128]{3,2,1,0:T(8,128)}), f32[16,15,8,128]{3,2,1,0:T(8,128)S(1)}, u32[]{:S(2)}, u32[]{:S(2)}) %all-to-all-start.3) | async-done | bytes 983072 | tf_op jit(solution)/shard_map/all_to_all | solution.py:415
  168.8 27.6 %invert_factor.1.inverse = f32[640,640]{1,0:T(8,128)S(1)} custom-call(f32[16,15,8,128]{3,2,1,0:T(8,128)S(1)} %all-to-all-done.3.lead), custom_call_target="tpu_custom_call" | custom-call | flops 40000000000 | bytes 4194304 | tf_op jit(solution)/shard_map/invert_factor/pallas_call | solution.py:417
  196.4 1.2 copy-done.11
  197.5 6.8 %collective-permute-done.other = f32[4,6,128,128]{3,2,1,0:T(8,128)S(1)} collective-permute-done((f32[4,6,128,128]{3,2,1,0:T(8,128)}, f32[4,6,128,128]{3,2,1,0:T(8,128)S(1)}, u32[]{:S(2)}, u32[]{:S(2)}) %collective-permute-start) | collective-permute-done | bytes 1572896 | tf_op jit(solution)/shard_map/ppermute | solution.py:416
  204.4 0.9 all-gather.5.cloned.1.call-done
  205.3 2.1 copy-done.8
  207.4 1.9 copy-done.9
  209.3 1.4 copy-done.12
  210.7 23.7 %eliminate.1 = f32[9216,128]{1,0:T(8,128)} custom-call(s32[2,48]{1,0:T(2,128)S(1)} %copy-done.5, f32[9216,128]{1,0:T(8,128)} %bitcast.7, f32[16,5,12,8,128]{4,3,2,1,0:T(8,128)S(1)} %bitcast.9, f32[8,6,128,128]{3,2,1,0:T(8,128)S(1)} %bitcast.10, f32[640,640]{1,0:T(8,128)S(1)} %copy-done.12, f32[64,128,128]{2,1,0:T(8,128)} %all-to-all-done.2.moved, ...), custom_call_target="tpu_custom_call" | custom-call | flops 15000000512 | bytes 20971520 | tf_op jit(solution)/shard_map/eliminate/pallas_call | solution.py:428
  (23 shorter events, 1.8 us)
Async XLA Ops:
  6.5 191.0 %all-gather.7.cloned.1.call-start = ((), (), s32[]{:S(2)}) async-start(), calls=%async_computation.5 | async-start | bytes 3538944 | tf_op jit(solution)/shard_map/all_gather | solution.py:396
  6.5 1.7 copy-start
  8.2 2.3 copy-start.2
  10.5 0.7 copy-start.4
  11.2 0.7 copy-start.6
  12.6 37.4 %copy-start.5 = (s32[2,48]{1,0:T(2,128)S(1)}, s32[2,48]{1,0:T(2,128)}, u32[]{:S(2)}) copy-start(s32[2,48]{1,0:T(2,128)} %maps.11) | copy-start | bytes 1156
  12.6 37.4 %copy-start.7 = (s32[2]{0:T(128)S(1)}, s32[2]{0:T(128)}, u32[]{:S(2)}) copy-start(s32[2]{0:T(128)} %orders.3) | copy-start | bytes 28
  50.0 1.7 copy-start.1
  52.7 2.0 copy-start.3
  74.1 59.5 %all-to-all-start.2 = ((f32[64,128,128]{2,1,0:T(8,128)}), f32[64,128,128]{2,1,0:T(8,128)}, u32[]{:S(2)}, u32[]{:S(2)}) async-start(f32[64,128,128]{2,1,0:T(8,128)} %copy-done.3), calls=%async_computation.2 | async-start | bytes 8388608 | tf_op jit(solution)/shard_map/all_to_all | solution.py:406
  79.7 125.5 %all-gather.5.cloned.1.call-start = ((), (), s32[]{:S(2)}) async-start(), calls=%async_computation.4 | async-start | bytes 4177920 | tf_op jit(solution)/shard_map/all_gather | solution.py:405
  137.0 1.2 copy-start.10
  138.2 30.5 %all-to-all-start.3 = ((f32[16,15,8,128]{3,2,1,0:T(8,128)}), f32[16,15,8,128]{3,2,1,0:T(8,128)S(1)}, u32[]{:S(2)}, u32[]{:S(2)}) async-start(f32[16,15,8,128]{3,2,1,0:T(8,128)} %get-tuple-element.15), calls=%async_computation.3 | async-start | bytes 1966080 | tf_op jit(solution)/shard_map/all_to_all | solution.py:415
  145.4 59.0 %collective-permute-start = (f32[4,6,128,128]{3,2,1,0:T(8,128)}, f32[4,6,128,128]{3,2,1,0:T(8,128)S(1)}, u32[]{:S(2)}, u32[]{:S(2)}) collective-permute-start(f32[4,6,128,128]{3,2,1,0:T(8,128)} %copy-done.10), channel_id=1, source_target_pairs={{0,64},{64,0},{1,65},{65,1},{2,66},{66,2},{3,67},{67,3},{4,68},{68... | collective-permute-start | bytes 4718600 | tf_op jit(solution)/shard_map/ppermute | solution.py:416
  196.3 1.2 copy-start.11
  205.3 2.1 copy-start.8
  207.4 1.9 copy-start.9
  209.3 1.4 copy-start.12
Sparse Core Ops, SparseCore 0:
  50.1 32.5 all-gather.6
  84.9 120.3 all-gather.4

commit v4 on v3

--- a/solution.py
+++ b/solution.py
@@ -12,7 +12,7 @@
 COL_TILES = 12
 CHILD_TILES = 6
 ROWS = ("k", "i")
-PIECES = 8 * (COL_TILES + CHILD_TILES)
+PIECES = COL_TILES + CHILD_TILES
 UPPER = [(b, c) for b in range(PT) for c in range(b, PT)]
 GROUP = 32
 HIGHEST = lax.Precision.HIGHEST
@@ -20,6 +20,7 @@
 BF16 = jnp.bfloat16
 
 VMEM = pl.BlockSpec(memory_space=pltpu.VMEM)
+ANY = pl.BlockSpec(memory_space=pl.ANY)
 SMEM = pl.BlockSpec(memory_space=pltpu.SMEM)
 
 
@@ -50,24 +51,30 @@
     return tile
 
 
-def pack_panel(maps, orders, front, child, out, column):
+def pack_panel(maps, orders, front, child, moved, out, column):
     k, i, j = place()
     order = orders[k]
     cols = lax.broadcasted_iota(jnp.int32, (8, T), 1) + (8 * (CHILD_TILES - 1) + j) * T
     for v in range(16):
         for s in range(COL_TILES):
-            out[v, 8 * s:8 * s + 8] = front[pl.ds(8 * v * COL_TILES + s, 8, stride=COL_TILES), :]
+            out[v, s] = front[pl.ds(8 * v * COL_TILES + s, 8, stride=COL_TILES), :]
         for h in range(CHILD_TILES):
             piece = child[pl.ds(8 * v * CHILD_TILES + h, 8, stride=CHILD_TILES), :]
             if h == CHILD_TILES - 1:
                 piece = jnp.where(cols < order, piece, 0.0)
-            s = COL_TILES + h
-            out[v, 8 * s:8 * s + 8] = piece
-    for g in range(CHILD_TILES):
-        tile = child_tile(child, order, i, j, g, 0)
-        out[(8 * g + i + offset(maps, k, g)) % 16, PIECES:] = tile
+            out[v, COL_TILES + h] = piece
+    row = k * 8 + i
     for t in range(ROW_TILES):
         column[t] = front[pl.ds(t * T * COL_TILES, T, stride=COL_TILES), :]
+    for source_child in range(2):
+        for g in range(CHILD_TILES):
+            shift = offset(maps, source_child, g)
+            source = (row - 8 * g - shift) % 16
+
+            @pl.when(source < 8)
+            def _():
+                t = (8 * g + source + shift) // 16
+                column[t] = column[t] + moved[8 * source_child + source]
 
 
 def pack_main(maps, orders, child, out):
@@ -80,30 +87,28 @@
             out[to_i * 8 + to_j] = child_tile(child, order, i, j, g, h)
 
 
-def pack_slices(maps, orders, got, child, out, main):
+def pack_slices(maps, got, out):
     j = lax.axis_index("col")
-
-    pack_main(maps, orders, child, main)
-
-    def piece(source, s):
-        return got[source, 8 * s:8 * s + 8]
-
     for child in range(2):
         for h in range(CHILD_TILES):
             dest = (j + offset(maps, child, h)) % 8
             for b in range(PT):
-                out[dest, child * PT + b] = piece(8 * child + b, COL_TILES + h)
+                out[dest, child * PT + b] = got[8 * child + b, COL_TILES + h]
     for b in range(PT):
-        lead = piece(b, 0) + piece(b, COL_TILES) + piece(8 + b, COL_TILES)
+        lead = got[b, 0] + got[b, COL_TILES] + got[8 + b, COL_TILES]
         for dest in range(8):
             out[dest, 2 * PT + b] = lead
 
 
-def add_slices(maps, got, moved, slab):
+def add_slices(maps, got, moved, other, slab, lead):
     j = lax.axis_index("col")
+    for n, (b, c) in enumerate(UPPER):
+        piece = moved[c, 2 * PT + b]
+        for v in range(16):
+            lead[v, n] = piece
     for b in range(PT):
         for s in range(COL_TILES):
-            slab[b, s] = got[b, 8 * s:8 * s + 8]
+            slab[b, s] = got[b, s]
     for child in range(2):
         for h in range(CHILD_TILES):
             shift = offset(maps, child, h)
@@ -111,21 +116,6 @@
             s = (8 * h + source + shift) // 8
             for b in range(PT):
                 slab[b, s] = slab[b, s] + moved[source, child * PT + b]
-
-
-def add_column(maps, start, moved, out):
-    k, i, j = place()
-    row = k * 8 + i
-    out[...] = start[...]
-    for child in range(2):
-        for g in range(CHILD_TILES):
-            shift = offset(maps, child, g)
-            source = (row - 8 * g - shift) % 16
-
-            @pl.when(source < 8)
-            def _():
-                t = (8 * g + source + shift) // 16
-                out[t] = out[t] + moved[8 * child + source, PIECES:]
 
 
 def reciprocal(x):
@@ -234,25 +224,53 @@
     return jnp.dot(a_high, b_high, preferred_element_type=F32) + small
 
 
+def solve_rows(down, inverse, lower, inverse_high, inverse_low):
+    high, low = halves(inverse[...])
+    inverse_high[...] = high
+    inverse_low[...] = low
+
+    def solve(t, carry):
+        mine = jnp.concatenate([down[b, t] for b in range(PT)], axis=1)
+        part = pl.ds(pl.multiple_of(t * T, T), T)
+        for lo, hi in SPLITS:
+            lower[part, lo:hi] = lax.dot_general(
+                mine[:, :hi], inverse[lo:hi, :hi], (((1,), (1,)), ((), ())),
+                precision=HIGHEST, preferred_element_type=F32,
+            )
+        return carry
+
+    lax.fori_loop(0, ROW_TILES, solve, 0)
+
+
 def eliminate(
-    maps, front, across, down, inverse, moved, other, out,
-    pivot_high, pivot_low, inverse_high, inverse_low, upper_high, upper_low, lower,
+    maps, front, across_far, lower, inverse_high, inverse_low, moved_far, other_far, out,
+    pivot_high, pivot_low, upper_high, upper_low, across, moved, other, across_sem, sems,
 ):
     k, i, j = place()
     row = k * 8 + i
     t = pl.program_id(0)
 
+    def child_copies():
+        return (
+            pltpu.make_async_copy(moved_far, moved, sems.at[0]),
+            pltpu.make_async_copy(other_far, other, sems.at[1]),
+        )
+
     @pl.when(t == 0)
     def _():
+        arrivals = [
+            pltpu.make_async_copy(across_far.at[:, b], across.at[:, b], across_sem.at[b])
+            for b in range(PT)
+        ]
+        for copy in (*arrivals, *child_copies()):
+            copy.start()
         for b in range(PT):
+            arrivals[b].wait()
             for s in range(COL_TILES):
                 tile = across[:, b, s].reshape(T, T)
                 high, low = halves(tile)
                 pivot_high[b * T:b * T + T, s * T:s * T + T] = high
                 pivot_low[b * T:b * T + T, s * T:s * T + T] = low
-        high, low = halves(inverse[...])
-        inverse_high[...] = high
-        inverse_low[...] = low
 
         def solve_upper(n, carry):
             part = pl.ds(pl.multiple_of(n * WIDE, WIDE), WIDE)
@@ -267,20 +285,7 @@
 
         lax.fori_loop(0, COL_TILES * T // WIDE, solve_upper, 0)
 
-        def solve_lower(t, carry):
-            mine = jnp.concatenate([down[b, t] for b in range(PT)], axis=1)
-            part = pl.ds(pl.multiple_of(t * T, T), T)
-            for lo, hi in SPLITS:
-                lower[part, lo:hi] = lax.dot_general(
-                    mine[:, :hi], inverse[lo:hi, :hi], (((1,), (1,)), ((), ())),
-                    precision=HIGHEST, preferred_element_type=F32,
-                )
-            return carry
-
-        lax.fori_loop(0, ROW_TILES, solve_lower, 0)
-
-    mine = lower[pl.ds(pl.multiple_of(t * T, T), T), :]
-    mine_halves = halves(mine)
+    mine_halves = halves(lower[...])
     for n in range(COL_TILES * T // WIDE):
         change = product(
             mine_halves,
@@ -290,6 +295,11 @@
             where = pl.ds(n * (WIDE // T) + s, T, stride=COL_TILES)
             out[where, :] = front[where, :] - change[:, s * T:s * T + T]
 
+    @pl.when(t == 0)
+    def _():
+        for copy in child_copies():
+            copy.wait()
+
     add_children(maps, moved, other, out)
     first = jnp.logical_and(t == 0, row < PT)
 
@@ -300,19 +310,18 @@
 
     @pl.when(j < PT)
     def _():
-        part = pl.ds(pl.multiple_of(t * T, T), T)
-        tile = lower[part, pl.ds(pl.multiple_of(j * T, T), T)]
+        tile = lower[:, pl.ds(pl.multiple_of(j * T, T), T)]
         x = lax.broadcasted_iota(jnp.int32, (T, T), 0) + (16 * t + row) * T
         y = lax.broadcasted_iota(jnp.int32, (T, T), 1) + j * T
         out[pl.ds(0, T, stride=COL_TILES), :] = jnp.where(x >= y, tile, 0.0)
 
 
-def pack_other(maps, moved, slices, out, lead):
+def pack_other(maps, orders, moved, child, out, column):
     k, i, j = place()
-    for n, (b, c) in enumerate(UPPER):
-        piece = slices[c, 2 * PT + b]
-        for v in range(16):
-            lead[v, n] = piece
+    order = orders[k]
+    for g in range(CHILD_TILES):
+        tile = child_tile(child, order, i, j, g, 0)
+        column[(8 * g + i + offset(maps, k, g)) % 16] = tile
     rank = jnp.int32(0)
     for g in range(CHILD_TILES):
         shift = offset(maps, k, g)
@@ -367,83 +376,96 @@
     front = front.reshape(ROW_TILES * T * COL_TILES, T)
     child = child_updates.reshape(CHILD_TILES * T * CHILD_TILES, T)
     maps = child_maps
+    main = pl.pallas_call(
+        pack_main,
+        out_shape=shape(64, T, T),
+        in_specs=[SMEM, SMEM, VMEM],
+        out_specs=VMEM,
+        compiler_params=params(16),
+        name="pack_main",
+    )(maps, child_orders, child)
+    main = lax.all_to_all(main, ("i", "col"), 0, 0, tiled=True)
+    other, column = pl.pallas_call(
+        pack_other,
+        out_shape=(shape(4, CHILD_TILES, T, T), shape(16, T, T)),
+        in_specs=[SMEM, SMEM, VMEM, VMEM],
+        out_specs=[VMEM, VMEM],
+        compiler_params=params(20),
+        name="pack_other",
+    )(maps, child_orders, main, child)
+    column = lax.all_to_all(column, ROWS, 0, 0, tiled=True)
+    other = lax.ppermute(other, "k", [(0, 1), (1, 0)])
     panel, column = pl.pallas_call(
         pack_panel,
-        out_shape=(shape(16, PIECES + T, T), shape(ROW_TILES, T, T)),
-        in_specs=[SMEM, SMEM, VMEM, VMEM],
+        out_shape=(shape(16, PIECES, 8, T), shape(ROW_TILES, T, T)),
+        in_specs=[SMEM, SMEM, VMEM, VMEM, VMEM],
         out_specs=[VMEM, VMEM],
-        compiler_params=params(24),
+        compiler_params=params(20),
         name="pack_panel",
-    )(maps, child_orders, front, child)
+    )(maps, child_orders, front, child, column)
+    down = lax.all_gather(column, "col")
     panel = lax.all_to_all(panel, ROWS, 0, 0, tiled=True)
-    slices, main = pl.pallas_call(
+    slices = pl.pallas_call(
         pack_slices,
-        out_shape=(shape(8, 3 * PT, 8, T), shape(64, T, T)),
-        in_specs=[SMEM, SMEM, VMEM, VMEM],
-        out_specs=[VMEM, VMEM],
-        compiler_params=params(24),
-        name="pack_slices",
-    )(maps, child_orders, panel, child)
-    slices = lax.all_to_all(slices, "col", 0, 0, tiled=True)
-    column = pl.pallas_call(
-        add_column,
-        out_shape=shape(ROW_TILES, T, T),
-        in_specs=[SMEM, VMEM, VMEM],
-        out_specs=VMEM,
-        compiler_params=params(24),
-        name="add_column",
-    )(maps, column, panel)
-    down = lax.all_gather(column, "col")
-    slab = pl.pallas_call(
-        add_slices,
-        out_shape=shape(PT, COL_TILES, 8, T),
-        in_specs=[SMEM, VMEM, VMEM],
+        out_shape=shape(8, 3 * PT, 8, T),
+        in_specs=[SMEM, VMEM],
         out_specs=VMEM,
         compiler_params=params(16),
+        name="pack_slices",
+    )(maps, panel)
+    slices = lax.all_to_all(slices, "col", 0, 0, tiled=True)
+    slab, lead = pl.pallas_call(
+        add_slices,
+        out_shape=(shape(PT, COL_TILES, 8, T), shape(16, len(UPPER), 8, T)),
+        in_specs=[SMEM, VMEM, VMEM, ANY],
+        out_specs=[VMEM, VMEM],
+        compiler_params=params(16),
         name="add_slices",
-    )(maps, panel, slices)
+    )(maps, panel, slices, other)
     across = lax.all_gather(slab, ROWS)
-    main = lax.all_to_all(main, ("i", "col"), 0, 0, tiled=True)
-    other, lead = pl.pallas_call(
-        pack_other,
-        out_shape=(shape(4, CHILD_TILES, T, T), shape(16, len(UPPER), 8, T)),
-        in_specs=[SMEM, VMEM, VMEM],
-        out_specs=[VMEM, VMEM],
-        compiler_params=params(24),
-        name="pack_other",
-    )(maps, main, slices)
     lead = lax.all_to_all(lead, ROWS, 0, 0, tiled=True)
-    other = lax.ppermute(other, "k", [(0, 1), (1, 0)])
     inverse = pl.pallas_call(
         invert_factor,
         out_shape=shape(PT * T, PT * T),
         in_specs=[VMEM],
         out_specs=VMEM,
         scratch_shapes=[pltpu.VMEM((PT * T, PT * T), F32), pltpu.VMEM((T, 2 * T), F32)],
-        compiler_params=params(32),
-        cost_estimate=pl.CostEstimate(flops=40 * 10**9, bytes_accessed=4 * 2**20, transcendentals=0),
+        compiler_params=params(16),
+        cost_estimate=pl.CostEstimate(flops=25 * 10**9, bytes_accessed=4 * 2**20, transcendentals=0),
         name="invert_factor",
     )(lead)
+    square = jax.ShapeDtypeStruct((PT * T, PT * T), BF16)
+    lower, inverse_high, inverse_low = pl.pallas_call(
+        solve_rows,
+        out_shape=(shape(ROW_TILES * T, PT * T), square, square),
+        in_specs=[VMEM, VMEM],
+        out_specs=[VMEM] * 3,
+        compiler_params=params(20),
+        cost_estimate=pl.CostEstimate(flops=5 * 10**9, bytes_accessed=8 * 2**20, transcendentals=0),
+        name="solve_rows",
+    )(down, inverse)
     block = pl.BlockSpec((T * COL_TILES, T), lambda t: (t, 0))
     out = pl.pallas_call(
         eliminate,
         out_shape=shape(ROW_TILES * T * COL_TILES, T),
         grid=(ROW_TILES,),
-        in_specs=[SMEM, block] + [VMEM] * 5,
+        in_specs=[SMEM, block, ANY, pl.BlockSpec((T, PT * T), lambda t: (t, 0)), VMEM, VMEM, ANY, ANY],
         out_specs=block,
         scratch_shapes=[
             pltpu.VMEM((PT * T, COL_TILES * T), BF16),
             pltpu.VMEM((PT * T, COL_TILES * T), BF16),
-            pltpu.VMEM((PT * T, PT * T), BF16),
-            pltpu.VMEM((PT * T, PT * T), BF16),
             pltpu.VMEM((PT * T, COL_TILES * T), BF16),
             pltpu.VMEM((PT * T, COL_TILES * T), BF16),
-            pltpu.VMEM((ROW_TILES * T, PT * T), F32),
+            pltpu.VMEM((16, PT, COL_TILES, 8, T), F32),
+            pltpu.VMEM((64, T, T), F32),
+            pltpu.VMEM((4, CHILD_TILES, T, T), F32),
+            pltpu.SemaphoreType.DMA((PT,)),
+            pltpu.SemaphoreType.DMA((2,)),
         ],
-        compiler_params=params(40),
-        cost_estimate=pl.CostEstimate(flops=15 * 10**9, bytes_accessed=20 * 2**20, transcendentals=0),
+        compiler_params=params(58),
+        cost_estimate=pl.CostEstimate(flops=12 * 10**9, bytes_accessed=20 * 2**20, transcendentals=0),
         name="eliminate",
-    )(maps, front, across, down, inverse, main, other)
+    )(maps, front, across, lower, inverse_high, inverse_low, main, other)
     return out.reshape(ROW_TILES, 1, T, COL_TILES, 1, T)
 
 

time: 245 us -> 256 us (1.045)
  blocking collectives: 55.2 us -> 153 us
  waiting for transfers between devices: 83.3 us -> 9.9 us
  starting transfers between devices: 13.2 us -> 5.82 us
  local copies, waits for them, and re-layouts: 16.8 us -> 10.1 us
    all_to_all x1 -> x3, blocking collectives: 19.4 us -> 105 us  [the longest x1 60.5 us: shards(): main = lax.all_to_all(main, ('i', 'col'), 0, 0, tiled=True)]
    all_to_all x2 -> x1, waiting for transfers between devices: 75.5 us -> 9.85 us  [shards(): slices = lax.all_to_all(slices, 'col', 0, 0, tiled=True)]
    all_to_all x1, blocking collectives: 35.8 us -> 48.4 us  [shards(): panel = lax.all_to_all(panel, ROWS, 0, 0, tiled=True)]
    all_to_all x2 -> x1, starting transfers between devices: 12.8 us -> 3.48 us  [shards(): slices = lax.all_to_all(slices, 'col', 0, 0, tiled=True)]
    pallas_call x4 -> x5, Pallas kernels: 4.58 us -> 12.6 us  [the longest x1 7.2 us: shards(): pl.pallas_call(solve_rows, out_shape=(shape(ROW_TILES * T, PT * T), squar...]
    ppermute x1, waiting for transfers between devices: 6.84 us -> 0.01 us  [shards(): other = lax.ppermute(other, 'k', [(0, 1), (1, 0)])]
    unnamed x26 -> x32, local copies, waits for them, and re-layouts: 16.8 us -> 10.1 us
    pallas_call x1, Pallas kernels: 23.7 us -> 18.9 us  [shards(): pl.pallas_call(eliminate, out_shape=shape(ROW_TILES * T * COL_TILES, T),...]
  transfers between devices with their start and end apart: 5 -> 4, of which waited for: 4 -> 1; matrix products, arithmetic and copies ran while one was open for 0% -> 0% of each run, Pallas kernels for 14% -> 15%
where the time goes in v4:
time: 256 us; the launch traced here: 254 us
  blocking collectives  153 us (60%)
  Pallas kernels  61.5 us (24%)
  between operations  13.5 us (5%)
  local copies, waits for them, and re-layouts  10.1 us (4%)
  waiting for transfers between devices  9.9 us (4%)
  starting transfers between devices  5.82 us (2%)
    all_to_all x1, blocking collectives, shards(): main = lax.all_to_all(main, ('i', 'col'), 0, 0, tiled=True)  60.5 us
    all_to_all x1, blocking collectives, shards(): panel = lax.all_to_all(panel, ROWS, 0, 0, tiled=True)  48.4 us
    pallas_call x1, Pallas kernels, shards(): pl.pallas_call(invert_factor, out_shape=shape(PT * T, PT * T), in_specs=[...  27.5 us
    all_to_all x1, blocking collectives, shards(): lead = lax.all_to_all(lead, ROWS, 0, 0, tiled=True)  23.2 us
    all_to_all x1, blocking collectives, shards(): column = lax.all_to_all(column, ROWS, 0, 0, tiled=True)  21.2 us
    pallas_call x1, Pallas kernels, shards(): pl.pallas_call(eliminate, out_shape=shape(ROW_TILES * T * COL_TILES, T),...  18.9 us
    unnamed x32, local copies, waits for them, and re-layouts  10.1 us
    all_to_all x1, waiting for transfers between devices, shards(): slices = lax.all_to_all(slices, 'col', 0, 0, tiled=True)  9.85 us
  transfers between devices with their start and end apart: 4, of which 1 were waited for; matrix products, arithmetic and copies ran while one was open for 0% of the time, Pallas kernels for 15%

profile of v4, /device:TPU:16, one launch (start us, length us, event | category | flops | bytes accessed | tf_op | source)
XLA Modules:
  0.0 254.2 jit_solution(530881476865220768)
XLA Ops:
  6.5 1.7 copy-done
  8.2 0.7 copy-done.6
  8.9 0.7 copy-done.8
  9.5 0.9 pack_main.1
  10.5 60.5 %all_to_all.25.moved.moved_far = f32[64,128,128]{2,1,0:T(8,128)S(1)} all-to-all(f32[64,128,128]{2,1,0:T(8,128)S(1)} %pack_main.1), channel_id=1, replica_groups=mesh['k'=2,'i'=8,'col'=8] {'i','col'}, dimensions={0} | all-to-all | bytes 8388608 | tf_op jit(solution)/shard_map/all_to_all | solution.py:387
  71.0 2.5 pack_other.1
  73.5 21.2 %all_to_all.26.moved = f32[16,128,128]{2,1,0:T(8,128)S(1)} all-to-all(f32[16,128,128]{2,1,0:T(8,128)S(1)} %get-tuple-element.14), channel_id=1, replica_groups=mesh['k'=2,'i'=8,'col'=8] {'k','i'}, dimensions={0} | all-to-all | bytes 2097152 | tf_op jit(solution)/shard_map/all_to_all | solution.py:396
  94.7 1.6 pack_panel.1
  96.4 1.1 copy-done.4
  97.5 2.3 collective-permute-start
  99.7 48.4 %all_to_all.27.got = f32[16,18,8,128]{3,2,1,0:T(8,128)S(1)} all-to-all(f32[16,18,8,128]{3,2,1,0:T(8,128)} %copy-done.4), channel_id=1, replica_groups=mesh['k'=2,'i'=8,'col'=8] {'k','i'}, dimensions={0} | all-to-all | bytes 2359296 | tf_op jit(solution)/shard_map/all_to_all | solution.py:407
  148.2 1.4 pack_slices.1
  149.6 3.5 %all-to-all-start.3 = ((f32[8,15,8,128]{3,2,1,0:T(8,128)}), f32[8,15,8,128]{3,2,1,0:T(8,128)S(1)}, u32[]{:S(2)}, u32[]{:S(2)}) async-start(f32[8,15,8,128]{3,2,1,0:T(8,128)} %pack_slices.1), calls=%async_computation.3 | async-start | bytes 983040 | tf_op jit(solution)/shard_map/all_to_all | solution.py:416
  153.1 9.8 %all-to-all-done.3.moved = f32[8,15,8,128]{3,2,1,0:T(8,128)S(1)} async-done(((f32[8,15,8,128]{3,2,1,0:T(8,128)}), f32[8,15,8,128]{3,2,1,0:T(8,128)S(1)}, u32[]{:S(2)}, u32[]{:S(2)}) %all-to-all-start.3) | async-done | bytes 491552 | tf_op jit(solution)/shard_map/all_to_all | solution.py:416
  163.0 1.4 add_slices.1
  164.4 0.9 copy-done.5
  165.4 23.2 %all_to_all.28.lead = f32[16,15,8,128]{3,2,1,0:T(8,128)S(1)} all-to-all(f32[16,15,8,128]{3,2,1,0:T(8,128)} %copy-done.5), channel_id=1, replica_groups=mesh['k'=2,'i'=8,'col'=8] {'k','i'}, dimensions={0} | all-to-all | bytes 1966080 | tf_op jit(solution)/shard_map/all_to_all | solution.py:426
  188.6 27.5 %invert_factor.1.inverse = f32[640,640]{1,0:T(8,128)S(1)} custom-call(f32[16,15,8,128]{3,2,1,0:T(8,128)S(1)} %all_to_all.28.lead), custom_call_target="tpu_custom_call" | custom-call | flops 24999999488 | bytes 4194304 | tf_op jit(solution)/shard_map/invert_factor/pallas_call | solution.py:427
  216.2 1.9 copy-done.10
  218.1 7.2 %solve_rows.1 = (f32[768,640]{1,0:T(8,128)S(1)}, bf16[640,640]{1,0:T(8,128)(2,1)S(1)}, bf16[640,640]{1,0:T(8,128)(2,1)S(1)}) custom-call(f32[8,6,128,128]{3,2,1,0:T(8,128)S(1)} %bitcast.12, f32[640,640]{1,0:T(8,128)S(1)} %invert_factor.1.inverse), custom_call_target="tpu_custom_call" | custom-call | flops 5000000000 | bytes 8388608 | tf_op jit(solution)/shard_map/solve_rows/pallas_call | solution.py:438
  225.3 1.3 copy-done.11
  226.5 0.9 copy-done.12
  227.5 1.0 copy-done.13
  228.4 18.9 %eliminate.1 = f32[9216,128]{1,0:T(8,128)} custom-call(s32[2,48]{1,0:T(2,128)} %maps.11, f32[9216,128]{1,0:T(8,128)} %bitcast.8, f32[16,5,12,8,128]{4,3,2,1,0:T(8,128)} %bitcast.13, f32[768,640]{1,0:T(8,128)} %copy-done.11, bf16[640,640]{1,0:T(8,128)(2,1)} %copy-done.12, bf16[640,640]{1,0:T(8,128)(2,1)} %copy-done.13, f32[64,128,128]{2,1,0:T(8,128)} %copy-done.2, ...), custom_call_target="tpu_custom_call" | custom-call | flops 12000000000 | bytes 20971520 | tf_op jit(solution)/shard_map/eliminate/pallas_call | solution.py:448
  (31 shorter events, 0.2 us)
Async XLA Ops:
  6.5 209.6 %all-gather.7.cloned.1.call-start = ((), (), s32[]{:S(2)}) async-start(), calls=%async_computation.6 | async-start | bytes 3538944 | tf_op jit(solution)/shard_map/all_gather | solution.py:406
  6.5 1.7 copy-start
  8.2 0.7 copy-start.6
  8.9 0.7 copy-start.8
  10.5 60.5 %copy-start.1 = (f32[6,1,128,6,1,128]{5,4,3,2,1,0:T(1,128)S(1)}, f32[6,1,128,6,1,128]{5,4,3,2,1,0:T(1,128)}, u32[]{:S(2)}) copy-start(f32[6,1,128,6,1,128]{5,4,3,2,1,0:T(1,128)} %param.5) | copy-start | bytes 7077892
  10.5 60.5 %copy-start.7 = (s32[2,48]{1,0:T(2,128)S(1)}, s32[2,48]{1,0:T(2,128)}, u32[]{:S(2)}) copy-start(s32[2,48]{1,0:T(2,128)} %maps.11) | copy-start | bytes 1156
  10.5 60.5 %copy-start.9 = (s32[2]{0:T(128)S(1)}, s32[2]{0:T(128)}, u32[]{:S(2)}) copy-start(s32[2]{0:T(128)} %orders.5) | copy-start | bytes 28
  10.5 84.2 %slice-start = ((s8[4718592]{0:T(1024)(128)(4,1)}), s8[4194304]{0:T(1024)(128)(4,1)S(1)}, s32[]{:S(2)}) async-start(s8[4718592]{0:T(1024)(128)(4,1)} %bitcast.9), calls=%async_computation.7 | async-start | bytes 8388608
  71.0 2.5 copy-start.2
  71.0 23.7 %slice-start.1 = ((s8[4718592]{0:T(1024)(128)(4,1)}), s8[524288]{0:T(1024)(128)(4,1)S(1)}, s32[]{:S(2)}) async-start(s8[4718592]{0:T(1024)(128)(4,1)} %bitcast.9), calls=%async_computation.8 | async-start | bytes 1048576
  96.4 1.1 copy-start.4
  97.5 55.7 %collective-permute-start = (f32[4,6,128,128]{3,2,1,0:T(8,128)}, f32[4,6,128,128]{3,2,1,0:T(8,128)S(1)}, u32[]{:S(2)}, u32[]{:S(2)}) collective-permute-start(f32[4,6,128,128]{3,2,1,0:T(8,128)} %get-tuple-element.16), channel_id=1, source_target_pairs={{0,64},{64,0},{1,65},{65,1},{2,66},{66,2},{3,67},{67,3},{4,68},{68... | collective-permute-start | bytes 4718600 | tf_op jit(solution)/shard_map/ppermute | solution.py:397
  149.6 13.4 %all-to-all-start.3 = ((f32[8,15,8,128]{3,2,1,0:T(8,128)}), f32[8,15,8,128]{3,2,1,0:T(8,128)S(1)}, u32[]{:S(2)}, u32[]{:S(2)}) async-start(f32[8,15,8,128]{3,2,1,0:T(8,128)} %pack_slices.1), calls=%async_computation.3 | async-start | bytes 983040 | tf_op jit(solution)/shard_map/all_to_all | solution.py:416
  153.1 75.4 %all-gather.5.cloned.1.call-start = ((), (), s32[]{:S(2)}) async-start(), calls=%async_computation.5 | async-start | bytes 4177920 | tf_op jit(solution)/shard_map/all_gather | solution.py:425
  153.1 35.5 %copy-start.3 = (f32[4,6,128,128]{3,2,1,0:T(8,128)}, f32[4,6,128,128]{3,2,1,0:T(8,128)S(1)}, u32[]{:S(2)}) copy-start(f32[4,6,128,128]{3,2,1,0:T(8,128)S(1)} %collective-permute-done.other.other_far) | copy-start | bytes 4718596
  164.4 0.9 copy-start.5
  216.2 1.9 copy-start.10
  225.2 1.3 copy-start.11
  226.5 0.9 copy-start.12
  227.4 1.0 copy-start.13
Sparse Core Ops, SparseCore 0:
  97.6 26.6 all-gather.6
  165.5 51.4 all-gather.4

commit v5 on v4

--- a/solution.py
+++ b/solution.py
@@ -12,7 +12,6 @@
 COL_TILES = 12
 CHILD_TILES = 6
 ROWS = ("k", "i")
-PIECES = COL_TILES + CHILD_TILES
 UPPER = [(b, c) for b in range(PT) for c in range(b, PT)]
 GROUP = 32
 HIGHEST = lax.Precision.HIGHEST
@@ -51,32 +50,6 @@
     return tile
 
 
-def pack_panel(maps, orders, front, child, moved, out, column):
-    k, i, j = place()
-    order = orders[k]
-    cols = lax.broadcasted_iota(jnp.int32, (8, T), 1) + (8 * (CHILD_TILES - 1) + j) * T
-    for v in range(16):
-        for s in range(COL_TILES):
-            out[v, s] = front[pl.ds(8 * v * COL_TILES + s, 8, stride=COL_TILES), :]
-        for h in range(CHILD_TILES):
-            piece = child[pl.ds(8 * v * CHILD_TILES + h, 8, stride=CHILD_TILES), :]
-            if h == CHILD_TILES - 1:
-                piece = jnp.where(cols < order, piece, 0.0)
-            out[v, COL_TILES + h] = piece
-    row = k * 8 + i
-    for t in range(ROW_TILES):
-        column[t] = front[pl.ds(t * T * COL_TILES, T, stride=COL_TILES), :]
-    for source_child in range(2):
-        for g in range(CHILD_TILES):
-            shift = offset(maps, source_child, g)
-            source = (row - 8 * g - shift) % 16
-
-            @pl.when(source < 8)
-            def _():
-                t = (8 * g + source + shift) // 16
-                column[t] = column[t] + moved[8 * source_child + source]
-
-
 def pack_main(maps, orders, child, out):
     k, i, j = place()
     order = orders[k]
@@ -87,35 +60,67 @@
             out[to_i * 8 + to_j] = child_tile(child, order, i, j, g, h)
 
 
-def pack_slices(maps, got, out):
-    j = lax.axis_index("col")
-    for child in range(2):
-        for h in range(CHILD_TILES):
-            dest = (j + offset(maps, child, h)) % 8
-            for b in range(PT):
-                out[dest, child * PT + b] = got[8 * child + b, COL_TILES + h]
-    for b in range(PT):
-        lead = got[b, 0] + got[b, COL_TILES] + got[8 + b, COL_TILES]
-        for dest in range(8):
-            out[dest, 2 * PT + b] = lead
-
-
-def add_slices(maps, got, moved, other, slab, lead):
-    j = lax.axis_index("col")
+def add_column(maps, front, moved, other, out):
+    k, i, j = place()
+    for t in range(ROW_TILES):
+        out[t] = front[pl.ds(t * T * COL_TILES, T, stride=COL_TILES), :]
+    rank = jnp.int32(0)
+    for g in range(CHILD_TILES):
+        shift = offset(maps, k, g)
+        source = (i - shift) % 8
+        p = 8 * g + source + shift
+
+        @pl.when(p // 8 % 2 == k)
+        def _():
+            out[p // 16] = out[p // 16] + moved[source * 8 + j]
+
+        far_shift = offset(maps, 1 - k, g)
+        far_p = 8 * g + (i - far_shift) % 8 + far_shift
+        comes = far_p // 8 % 2 == k
+        here = jnp.minimum(rank, 3)
+
+        @pl.when(comes)
+        def _():
+            out[far_p // 16] = out[far_p // 16] + other[here]
+
+        rank = rank + comes.astype(jnp.int32)
+
+
+def pack_rows(maps, front_far, moved_far, other, out, tiles, front, moved, sems):
+    k, i, j = place()
+
+    @pl.when(jnp.logical_and(k == 0, i < PT))
+    def _():
+        copies = (
+            pltpu.make_async_copy(front_far.at[pl.ds(0, T * COL_TILES)], front, sems.at[0]),
+            pltpu.make_async_copy(moved_far.at[pl.ds(i * 8, 8)], moved, sems.at[1]),
+        )
+        for copy in copies:
+            copy.start()
+        for copy in copies:
+            copy.wait()
+        for s in range(COL_TILES):
+            tiles[s] = front[pl.ds(s, T, stride=COL_TILES), :]
+        for child in range(2):
+            for h in range(CHILD_TILES):
+                shift = offset(maps, child, h)
+                from_j = (j - shift) % 8
+                s = (8 * h + from_j + shift) // 8
+                if child == 0:
+                    tile = moved[from_j]
+                else:
+                    tile = other[0 if h == 0 else 3 + h]
+                tiles[s] = tiles[s] + tile
+        for v in range(16):
+            for s in range(COL_TILES):
+                out[v, s] = tiles[s, 8 * v:8 * v + 8]
+
+
+def pack_lead(got, out):
     for n, (b, c) in enumerate(UPPER):
-        piece = moved[c, 2 * PT + b]
+        piece = got[c, b]
         for v in range(16):
-            lead[v, n] = piece
-    for b in range(PT):
-        for s in range(COL_TILES):
-            slab[b, s] = got[b, s]
-    for child in range(2):
-        for h in range(CHILD_TILES):
-            shift = offset(maps, child, h)
-            source = (j - shift) % 8
-            s = (8 * h + source + shift) // 8
-            for b in range(PT):
-                slab[b, s] = slab[b, s] + moved[source, child * PT + b]
+            out[v, n] = piece
 
 
 def reciprocal(x):
@@ -243,7 +248,8 @@
 
 
 def eliminate(
-    maps, front, across_far, lower, inverse_high, inverse_low, moved_far, other_far, out,
+    maps, front, across_far, lower, inverse_high, inverse_low,
+    moved_far, near, rest, out,
     pivot_high, pivot_low, upper_high, upper_low, across, moved, other, across_sem, sems,
 ):
     k, i, j = place()
@@ -253,7 +259,13 @@
     def child_copies():
         return (
             pltpu.make_async_copy(moved_far, moved, sems.at[0]),
-            pltpu.make_async_copy(other_far, other, sems.at[1]),
+            pltpu.make_async_copy(near.at[pl.ds(0, 4)], other.at[:, 0], sems.at[1]),
+            pltpu.make_async_copy(
+                near.at[pl.ds(4, CHILD_TILES - 1)], other.at[0, pl.ds(1, CHILD_TILES - 1)], sems.at[2]
+            ),
+            pltpu.make_async_copy(
+                rest, other.at[pl.ds(1, 3), pl.ds(1, CHILD_TILES - 1)], sems.at[3]
+            ),
         )
 
     @pl.when(t == 0)
@@ -301,9 +313,8 @@
             copy.wait()
 
     add_children(maps, moved, other, out)
-    first = jnp.logical_and(t == 0, row < PT)
-
-    @pl.when(first)
+
+    @pl.when(jnp.logical_and(t == 0, row < PT))
     def _():
         for s in range(COL_TILES):
             out[pl.ds(s, T, stride=COL_TILES), :] = jnp.zeros((T, T), F32)
@@ -316,12 +327,8 @@
         out[pl.ds(0, T, stride=COL_TILES), :] = jnp.where(x >= y, tile, 0.0)
 
 
-def pack_other(maps, orders, moved, child, out, column):
+def pack_other(maps, moved, near, rest):
     k, i, j = place()
-    order = orders[k]
-    for g in range(CHILD_TILES):
-        tile = child_tile(child, order, i, j, g, 0)
-        column[(8 * g + i + offset(maps, k, g)) % 16] = tile
     rank = jnp.int32(0)
     for g in range(CHILD_TILES):
         shift = offset(maps, k, g)
@@ -331,8 +338,19 @@
 
         @pl.when(leaves)
         def _():
-            for h in range(CHILD_TILES):
-                out[here, h] = moved[source * 8 + (j - offset(maps, k, h)) % 8]
+            near[here] = moved[source * 8 + j]
+
+        @pl.when(jnp.logical_and(leaves, rank == 0))
+        def _():
+            for h in range(1, CHILD_TILES):
+                near[3 + h] = moved[source * 8 + (j - offset(maps, k, h)) % 8]
+
+        @pl.when(jnp.logical_and(leaves, rank > 0))
+        def _():
+            for h in range(1, CHILD_TILES):
+                rest[jnp.maximum(here - 1, 0), h - 1] = moved[
+                    source * 8 + (j - offset(maps, k, h)) % 8
+                ]
 
         rank = rank + leaves.astype(jnp.int32)
 
@@ -385,44 +403,52 @@
         name="pack_main",
     )(maps, child_orders, child)
     main = lax.all_to_all(main, ("i", "col"), 0, 0, tiled=True)
-    other, column = pl.pallas_call(
+    swap = [(0, 1), (1, 0)]
+    near, rest = pl.pallas_call(
         pack_other,
-        out_shape=(shape(4, CHILD_TILES, T, T), shape(16, T, T)),
-        in_specs=[SMEM, SMEM, VMEM, VMEM],
-        out_specs=[VMEM, VMEM],
-        compiler_params=params(20),
+        out_shape=(shape(3 + CHILD_TILES, T, T), shape(3, CHILD_TILES - 1, T, T)),
+        in_specs=[SMEM, VMEM],
+        out_specs=[VMEM] * 2,
+        compiler_params=params(16),
         name="pack_other",
-    )(maps, child_orders, main, child)
-    column = lax.all_to_all(column, ROWS, 0, 0, tiled=True)
-    other = lax.ppermute(other, "k", [(0, 1), (1, 0)])
-    panel, column = pl.pallas_call(
-        pack_panel,
-        out_shape=(shape(16, PIECES, 8, T), shape(ROW_TILES, T, T)),
-        in_specs=[SMEM, SMEM, VMEM, VMEM, VMEM],
-        out_specs=[VMEM, VMEM],
-        compiler_params=params(20),
-        name="pack_panel",
-    )(maps, child_orders, front, child, column)
-    down = lax.all_gather(column, "col")
-    panel = lax.all_to_all(panel, ROWS, 0, 0, tiled=True)
-    slices = pl.pallas_call(
-        pack_slices,
-        out_shape=shape(8, 3 * PT, 8, T),
-        in_specs=[SMEM, VMEM],
+    )(maps, main)
+    near = lax.ppermute(near, "k", swap)
+    rest = lax.ppermute(rest, "k", swap)
+    column = pl.pallas_call(
+        add_column,
+        out_shape=shape(ROW_TILES, T, T),
+        in_specs=[SMEM, VMEM, VMEM, VMEM],
         out_specs=VMEM,
         compiler_params=params(16),
-        name="pack_slices",
-    )(maps, panel)
-    slices = lax.all_to_all(slices, "col", 0, 0, tiled=True)
-    slab, lead = pl.pallas_call(
-        add_slices,
-        out_shape=(shape(PT, COL_TILES, 8, T), shape(16, len(UPPER), 8, T)),
-        in_specs=[SMEM, VMEM, VMEM, ANY],
-        out_specs=[VMEM, VMEM],
+        name="add_column",
+    )(maps, front, main, near)
+    down = lax.all_gather(column, "col")
+    rows = pl.pallas_call(
+        pack_rows,
+        out_shape=shape(16, COL_TILES, 8, T),
+        in_specs=[SMEM, ANY, ANY, VMEM],
+        out_specs=VMEM,
+        scratch_shapes=[
+            pltpu.VMEM((COL_TILES, T, T), F32),
+            pltpu.VMEM((T * COL_TILES, T), F32),
+            pltpu.VMEM((8, T, T), F32),
+            pltpu.SemaphoreType.DMA((2,)),
+        ],
+        compiler_params=params(58),
+        name="pack_rows",
+    )(maps, front, main, near)
+    rows = lax.all_to_all(rows, ROWS, 0, 0, tiled=True)
+    slab = rows[:PT]
+    across = lax.all_gather(slab, ROWS)
+    lead = lax.all_gather(slab[:, 0], "col")
+    lead = pl.pallas_call(
+        pack_lead,
+        out_shape=shape(16, len(UPPER), 8, T),
+        in_specs=[VMEM],
+        out_specs=VMEM,
         compiler_params=params(16),
-        name="add_slices",
-    )(maps, panel, slices, other)
-    across = lax.all_gather(slab, ROWS)
+        name="pack_lead",
+    )(lead)
     lead = lax.all_to_all(lead, ROWS, 0, 0, tiled=True)
     inverse = pl.pallas_call(
         invert_factor,
@@ -449,7 +475,7 @@
         eliminate,
         out_shape=shape(ROW_TILES * T * COL_TILES, T),
         grid=(ROW_TILES,),
-        in_specs=[SMEM, block, ANY, pl.BlockSpec((T, PT * T), lambda t: (t, 0)), VMEM, VMEM, ANY, ANY],
+        in_specs=[SMEM, block, ANY, pl.BlockSpec((T, PT * T), lambda t: (t, 0))] + [VMEM] * 2 + [ANY] * 3,
         out_specs=block,
         scratch_shapes=[
             pltpu.VMEM((PT * T, COL_TILES * T), BF16),
@@ -460,12 +486,12 @@
             pltpu.VMEM((64, T, T), F32),
             pltpu.VMEM((4, CHILD_TILES, T, T), F32),
             pltpu.SemaphoreType.DMA((PT,)),
-            pltpu.SemaphoreType.DMA((2,)),
+            pltpu.SemaphoreType.DMA((4,)),
         ],
         compiler_params=params(58),
         cost_estimate=pl.CostEstimate(flops=12 * 10**9, bytes_accessed=20 * 2**20, transcendentals=0),
         name="eliminate",
-    )(maps, front, across, lower, inverse_high, inverse_low, main, other)
+    )(maps, front, across, lower, inverse_high, inverse_low, main, near, rest)
     return out.reshape(ROW_TILES, 1, T, COL_TILES, 1, T)
 
 

time: 256 us -> 224 us (0.88)
  blocking collectives: 153 us -> 91.6 us
  waiting for transfers between devices: 9.9 us -> 38.4 us
    all_to_all x3 -> x1, blocking collectives: 92.8 us -> 18.5 us  [shards(): rows = lax.all_to_all(rows, ROWS, 0, 0, tiled=True)]
    ppermute x1 -> x2, waiting for transfers between devices: 0.01 us -> 15.9 us  [the longest x1 15.9 us: shards(): near = lax.ppermute(near, 'k', swap)]
    all_gather x0 -> x1, blocking collectives: none -> 12.8 us  [shards(): lead = lax.all_gather(slab[:, 0], 'col')]
    all_to_all x1, waiting for transfers between devices: 9.85 us -> 18.2 us  [shards(): lead = lax.all_to_all(lead, ROWS, 0, 0, tiled=True)]
    all_gather x1, waiting for transfers between devices: 0.01 us -> 4.32 us  [shards(): across = lax.all_gather(slab, ROWS)]
    unnamed x32 -> x28, local copies, waits for them, and re-layouts: 10.1 us -> 10.6 us
  transfers between devices with their start and end apart: 4 -> 5, of which waited for: 1 -> 3; matrix products, arithmetic and copies ran while one was open for 0% -> 0% of each run, Pallas kernels for 15% -> 17%
where the time goes in v5:
time: 224 us; the launch traced here: 222 us
  blocking collectives  91.6 us (41%)
  Pallas kernels  60.4 us (27%)
  waiting for transfers between devices  38.4 us (17%)
  between operations  13.5 us (6%)
  local copies, waits for them, and re-layouts  11.3 us (5%)
  starting transfers between devices  7.03 us (3%)
    all_to_all x1, blocking collectives, shards(): main = lax.all_to_all(main, ('i', 'col'), 0, 0, tiled=True)  60.4 us
    pallas_call x1, Pallas kernels, shards(): pl.pallas_call(invert_factor, out_shape=shape(PT * T, PT * T), in_specs=[...  27.5 us
    pallas_call x1, Pallas kernels, shards(): pl.pallas_call(eliminate, out_shape=shape(ROW_TILES * T * COL_TILES, T),...  19.1 us
    all_to_all x1, blocking collectives, shards(): rows = lax.all_to_all(rows, ROWS, 0, 0, tiled=True)  18.5 us
    all_to_all x1, waiting for transfers between devices, shards(): lead = lax.all_to_all(lead, ROWS, 0, 0, tiled=True)  18.2 us
    ppermute x1, waiting for transfers between devices, shards(): near = lax.ppermute(near, 'k', swap)  15.9 us
    all_gather x1, blocking collectives, shards(): lead = lax.all_gather(slab[:, 0], 'col')  12.8 us
    unnamed x28, local copies, waits for them, and re-layouts  10.6 us
  transfers between devices with their start and end apart: 5, of which 3 were waited for; matrix products, arithmetic and copies ran while one was open for 0% of the time, Pallas kernels for 17%

profile of v5, /device:TPU:16, one launch (start us, length us, event | category | flops | bytes accessed | tf_op | source)
XLA Modules:
  0.0 222.3 jit_solution(8273178636759032202)
XLA Ops:
  6.5 1.7 copy-done.1
  9.5 0.9 pack_main.1
  10.5 60.4 %all_to_all.15.moved.moved_far = f32[64,128,128]{2,1,0:T(8,128)S(1)} all-to-all(f32[64,128,128]{2,1,0:T(8,128)S(1)} %pack_main.1), channel_id=1, replica_groups=mesh['k'=2,'i'=8,'col'=8] {'i','col'}, dimensions={0} | all-to-all | bytes 8388608 | tf_op jit(solution)/shard_map/all_to_all | solution.py:405
  70.8 0.9 pack_other.1
  71.7 0.7 collective-permute-start
  72.4 15.9 %collective-permute-done.other.near = f32[9,128,128]{2,1,0:T(8,128)S(1)} collective-permute-done((f32[9,128,128]{2,1,0:T(8,128)S(1)}, f32[9,128,128]{2,1,0:T(8,128)S(1)}, u32[]{:S(2)}, u32[]{:S(2)}) %collective-permute-start) | collective-permute-done | bytes 589856 | tf_op jit(solution)/shard_map/ppermute | solution.py:415
  88.3 1.7 add_column.1
  90.1 2.0 pack_rows.1
  92.1 18.5 %all_to_all.16 = f32[16,12,8,128]{3,2,1,0:T(8,128)S(1)} all-to-all(f32[16,12,8,128]{3,2,1,0:T(8,128)} %pack_rows.1), channel_id=1, replica_groups=mesh['k'=2,'i'=8,'col'=8] {'k','i'}, dimensions={0} | all-to-all | bytes 1572864 | tf_op jit(solution)/shard_map/all_to_all | solution.py:440
  110.6 0.7 slice.9
  111.3 12.8 %all-gather.2 = f32[40,1,8,128]{3,2,1,0:T(8,128)S(1)} all-gather(f32[5,1,8,128]{3,2,1,0:T(8,128)S(1)} %slice.10), channel_id=4, replica_groups=mesh['k'=2,'i'=8,'col'=8] {'col'}, dimensions={0}, use_global_device_ids=true | all-gather | bytes 184320 | tf_op jit(solution)/shard_map/all_gather | solution.py:443
  124.1 1.0 pack_lead.1
  125.1 5.9 %all-to-all-start.2 = ((f32[16,15,8,128]{3,2,1,0:T(8,128)}), f32[16,15,8,128]{3,2,1,0:T(8,128)S(1)}, u32[]{:S(2)}, u32[]{:S(2)}) async-start(f32[16,15,8,128]{3,2,1,0:T(8,128)} %pack_lead.1), calls=%async_computation.2 | async-start | bytes 1966080 | tf_op jit(solution)/shard_map/all_to_all | solution.py:452
  131.4 18.2 %all-to-all-done.2.lead = f32[16,15,8,128]{3,2,1,0:T(8,128)S(1)} async-done(((f32[16,15,8,128]{3,2,1,0:T(8,128)}), f32[16,15,8,128]{3,2,1,0:T(8,128)S(1)}, u32[]{:S(2)}, u32[]{:S(2)}) %all-to-all-start.2) | async-done | bytes 983072 | tf_op jit(solution)/shard_map/all_to_all | solution.py:452
  149.5 27.5 %invert_factor.1.inverse = f32[640,640]{1,0:T(8,128)S(1)} custom-call(f32[16,15,8,128]{3,2,1,0:T(8,128)S(1)} %all-to-all-done.2.lead), custom_call_target="tpu_custom_call" | custom-call | flops 24999999488 | bytes 4194304 | tf_op jit(solution)/shard_map/invert_factor/pallas_call | solution.py:453
  177.1 1.2 copy-done.7
  178.3 1.9 copy-done.5
  180.2 1.4 copy-done.8
  181.6 7.2 %solve_rows.1 = (f32[768,640]{1,0:T(8,128)S(1)}, bf16[640,640]{1,0:T(8,128)(2,1)S(1)}, bf16[640,640]{1,0:T(8,128)(2,1)S(1)}) custom-call(f32[8,6,128,128]{3,2,1,0:T(8,128)S(1)} %bitcast.13, f32[640,640]{1,0:T(8,128)S(1)} %copy-done.8), custom_call_target="tpu_custom_call" | custom-call | flops 5000000000 | bytes 8388608 | tf_op jit(solution)/shard_map/solve_rows/pallas_call | solution.py:464
  188.8 1.3 copy-done.6
  190.1 0.9 copy-done.9
  191.0 0.9 copy-done.10
  191.9 4.3 %all-gather.6.cloned.1.call-done = f32[80,12,8,128]{3,2,1,0:T(8,128)} async-done(((f32[5,12,8,128]{3,2,1,0:T(8,128)}), f32[80,12,8,128]{3,2,1,0:T(8,128)}) %all-gather.6.cloned.1.call-update) | async-done | bytes 3932176 | tf_op jit(solution)/shard_map/all_gather | solution.py:442
  196.3 19.1 %eliminate.1 = f32[9216,128]{1,0:T(8,128)} custom-call(s32[2,48]{1,0:T(2,128)} %maps.9, f32[9216,128]{1,0:T(8,128)} %bitcast.7, f32[16,5,12,8,128]{4,3,2,1,0:T(8,128)} %bitcast.14, f32[768,640]{1,0:T(8,128)} %copy-done.6, bf16[640,640]{1,0:T(8,128)(2,1)} %copy-done.9, bf16[640,640]{1,0:T(8,128)(2,1)} %copy-done.10, f32[64,128,128]{2,1,0:T(8,128)} %copy-done, ...), custom_call_target="tpu_custom_call" | custom-call | flops 12000000000 | bytes 20971520 | tf_op jit(solution)/shard_map/eliminate/pallas_call | solution.py:474
  (30 shorter events, 1.8 us)
Async XLA Ops:
  6.5 171.7 %all-gather.8.cloned.1.call-start = ((), (), s32[]{:S(2)}) async-start(), calls=%async_computation.4 | async-start | bytes 3538944 | tf_op jit(solution)/shard_map/all_gather | solution.py:425
  6.5 1.7 copy-start.1
  8.2 0.7 copy-start.3
  8.9 0.7 copy-start.4
  9.5 78.7 %slice-start = ((s8[4718592]{0:T(1024)(128)(4,1)}), s8[4194304]{0:T(1024)(128)(4,1)S(1)}, s32[]{:S(2)}) async-start(s8[4718592]{0:T(1024)(128)(4,1)} %bitcast.8), calls=%async_computation.5 | async-start | bytes 8388608
  10.5 77.8 %slice-start.1 = ((s8[4718592]{0:T(1024)(128)(4,1)}), s8[524288]{0:T(1024)(128)(4,1)S(1)}, s32[]{:S(2)}) async-start(s8[4718592]{0:T(1024)(128)(4,1)} %bitcast.8), calls=%async_computation.6 | async-start | bytes 1048576
  70.8 17.4 %copy-start = (f32[64,128,128]{2,1,0:T(8,128)}, f32[64,128,128]{2,1,0:T(8,128)S(1)}, u32[]{:S(2)}) copy-start(f32[64,128,128]{2,1,0:T(8,128)S(1)} %all_to_all.15.moved.moved_far) | copy-start | bytes 12582916
  71.7 16.6 %collective-permute-start = (f32[9,128,128]{2,1,0:T(8,128)S(1)}, f32[9,128,128]{2,1,0:T(8,128)S(1)}, u32[]{:S(2)}, u32[]{:S(2)}) collective-permute-start(f32[9,128,128]{2,1,0:T(8,128)S(1)} %get-tuple-element.10), channel_id=1, source_target_pairs={{0,64},{64,0},{1,65},{65,1},{2,66},{66,2},{3,67},{67,3},{4,68},{68... | collective-permute-start | bytes 1769480 | tf_op jit(solution)/shard_map/ppermute | solution.py:415
  88.3 1.7 copy-start.2
  90.0 106.2 %all-gather.6.cloned.1.call-start = ((), (), s32[]{:S(2)}) async-start(), calls=%async_computation.3 | async-start | bytes 4177920 | tf_op jit(solution)/shard_map/all_gather | solution.py:442
  125.1 24.5 %all-to-all-start.2 = ((f32[16,15,8,128]{3,2,1,0:T(8,128)}), f32[16,15,8,128]{3,2,1,0:T(8,128)S(1)}, u32[]{:S(2)}, u32[]{:S(2)}) async-start(f32[16,15,8,128]{3,2,1,0:T(8,128)} %pack_lead.1), calls=%async_computation.2 | async-start | bytes 1966080 | tf_op jit(solution)/shard_map/all_to_all | solution.py:452
  131.0 60.9 %collective-permute-start.1 = (f32[3,5,128,128]{3,2,1,0:T(8,128)S(1)}, f32[3,5,128,128]{3,2,1,0:T(8,128)S(1)}, u32[]{:S(2)}, u32[]{:S(2)}) collective-permute-start(f32[3,5,128,128]{3,2,1,0:T(8,128)S(1)} %get-tuple-element.14), channel_id=1, source_target_pairs={{0,64},{64,0},{1,65},{65,1},{2,66},{66,2},{3,67},{67,3},{4,68},{68... | collective-permute-start | bytes 2949128 | tf_op jit(solution)/shard_map/ppermute | solution.py:416
  177.1 1.2 copy-start.7
  178.3 1.9 copy-start.5
  180.2 1.4 copy-start.8
  188.8 1.3 copy-start.6
  190.1 0.9 copy-start.9
  191.0 0.9 copy-start.10
  191.9 4.3 %copy-start.11 = (f32[3,5,128,128]{3,2,1,0:T(8,128)}, f32[3,5,128,128]{3,2,1,0:T(8,128)S(1)}, u32[]{:S(2)}) copy-start(f32[3,5,128,128]{3,2,1,0:T(8,128)S(1)} %collective-permute-done.1.rest) | copy-start | bytes 2949124
Sparse Core Ops, SparseCore 0:
  90.1 27.4 all-gather.7
  119.9 76.3 all-gather.5

commit v6 on v5

--- a/solution.py
+++ b/solution.py
@@ -60,10 +60,17 @@
             out[to_i * 8 + to_j] = child_tile(child, order, i, j, g, h)
 
 
-def add_column(maps, front, moved, other, out):
+def add_column(maps, front, moved, other, lead, out):
     k, i, j = place()
+
+    def tile(t):
+        return pl.ds(pl.multiple_of(t * T, T), T)
+
+    for b in range(PT):
+        first = ROW_TILES * T + 8 * b
+        out[first:first + 8, :] = lead[b] + lead[8 + b]
     for t in range(ROW_TILES):
-        out[t] = front[pl.ds(t * T * COL_TILES, T, stride=COL_TILES), :]
+        out[t * T:t * T + T, :] = front[pl.ds(t * T * COL_TILES, T, stride=COL_TILES), :]
     rank = jnp.int32(0)
     for g in range(CHILD_TILES):
         shift = offset(maps, k, g)
@@ -72,7 +79,7 @@
 
         @pl.when(p // 8 % 2 == k)
         def _():
-            out[p // 16] = out[p // 16] + moved[source * 8 + j]
+            out[tile(p // 16), :] = out[tile(p // 16), :] + moved[source * 8 + j]
 
         far_shift = offset(maps, 1 - k, g)
         far_p = 8 * g + (i - far_shift) % 8 + far_shift
@@ -81,7 +88,7 @@
 
         @pl.when(comes)
         def _():
-            out[far_p // 16] = out[far_p // 16] + other[here]
+            out[tile(far_p // 16), :] = out[tile(far_p // 16), :] + other[here]
 
         rank = rank + comes.astype(jnp.int32)
 
@@ -116,11 +123,39 @@
                 out[v, s] = tiles[s, 8 * v:8 * v + 8]
 
 
-def pack_lead(got, out):
+def take_slab(rows, other, out):
+    for b in range(PT):
+        out[b] = rows[b]
+
+
+def pack_lead(far, out, got, sem):
+    copy = pltpu.make_async_copy(
+        far.at[pl.ds(0, PT), pl.ds(ROW_TILES * T, 8 * PT)], got, sem
+    )
+    copy.start()
+    copy.wait()
     for n, (b, c) in enumerate(UPPER):
-        piece = got[c, b]
+        piece = got[c, 8 * b:8 * b + 8]
         for v in range(16):
             out[v, n] = piece
+
+
+SPLITS = ((0, 256), (256, 512), (512, 640))
+WIDE = 512
+
+
+def halves(x):
+    high = x.astype(BF16)
+    return high, (x - high.astype(F32)).astype(BF16)
+
+
+def product(a, b, over=0):
+    (a_high, a_low), (b_high, b_low) = a, b
+
+    def dot(x, y):
+        return lax.dot_general(x, y, (((1,), (over,)), ((), ())), preferred_element_type=F32)
+
+    return dot(a_high, b_high) + (dot(a_high, b_low) + dot(a_low, b_high))
 
 
 def reciprocal(x):
@@ -129,7 +164,9 @@
     return y * (2.0 - x * y)
 
 
-def invert_factor(lead, out, matrix, work):
+def invert_factor(lead, far, lower, inverse_high, inverse_low, out, matrix, work, down, sem):
+    copy = pltpu.make_async_copy(far.at[pl.ds(0, PT), pl.ds(0, ROW_TILES * T)], down, sem)
+    copy.start()
     for n, (b, c) in enumerate(UPPER):
         for r in range(16):
             matrix[b * T + 8 * r:b * T + 8 * r + 8, c * T:c * T + T] = lead[r, n]
@@ -212,35 +249,19 @@
                 )
 
 
-SPLITS = ((0, 256), (256, 512), (512, 640))
-WIDE = 512
-
-
-def halves(x):
-    high = x.astype(BF16)
-    return high, (x - high.astype(F32)).astype(BF16)
-
-
-def product(a, b):
-    (a_high, a_low), (b_high, b_low) = a, b
-    small = jnp.dot(a_high, b_low, preferred_element_type=F32) + jnp.dot(
-        a_low, b_high, preferred_element_type=F32
-    )
-    return jnp.dot(a_high, b_high, preferred_element_type=F32) + small
-
-
-def solve_rows(down, inverse, lower, inverse_high, inverse_low):
-    high, low = halves(inverse[...])
+    high, low = halves(out[...])
     inverse_high[...] = high
     inverse_low[...] = low
+    copy.wait()
 
     def solve(t, carry):
-        mine = jnp.concatenate([down[b, t] for b in range(PT)], axis=1)
         part = pl.ds(pl.multiple_of(t * T, T), T)
+        mine_high, mine_low = halves(jnp.concatenate([down[b, part, :] for b in range(PT)], axis=1))
         for lo, hi in SPLITS:
-            lower[part, lo:hi] = lax.dot_general(
-                mine[:, :hi], inverse[lo:hi, :hi], (((1,), (1,)), ((), ())),
-                precision=HIGHEST, preferred_element_type=F32,
+            lower[part, lo:hi] = product(
+                (mine_high[:, :hi], mine_low[:, :hi]),
+                (inverse_high[lo:hi, :hi], inverse_low[lo:hi, :hi]),
+                1,
             )
         return carry
 
@@ -327,8 +348,12 @@
         out[pl.ds(0, T, stride=COL_TILES), :] = jnp.where(x >= y, tile, 0.0)
 
 
-def pack_other(maps, moved, near, rest):
+def pack_other(maps, moved, child, front, near, rest, lead):
     k, i, j = place()
+    tile = child[pl.ds(0, T, stride=CHILD_TILES), :]
+    tile = tile + jnp.where(k == 0, front[pl.ds(0, T, stride=COL_TILES), :], 0.0)
+    for v in range(16):
+        lead[v] = tile[8 * v:8 * v + 8]
     rank = jnp.int32(0)
     for g in range(CHILD_TILES):
         shift = offset(maps, k, g)
@@ -404,24 +429,27 @@
     )(maps, child_orders, child)
     main = lax.all_to_all(main, ("i", "col"), 0, 0, tiled=True)
     swap = [(0, 1), (1, 0)]
-    near, rest = pl.pallas_call(
+    near, rest, lead = pl.pallas_call(
         pack_other,
-        out_shape=(shape(3 + CHILD_TILES, T, T), shape(3, CHILD_TILES - 1, T, T)),
-        in_specs=[SMEM, VMEM],
-        out_specs=[VMEM] * 2,
+        out_shape=(
+            shape(3 + CHILD_TILES, T, T), shape(3, CHILD_TILES - 1, T, T), shape(16, 8, T)
+        ),
+        in_specs=[SMEM, VMEM, VMEM, VMEM],
+        out_specs=[VMEM] * 3,
         compiler_params=params(16),
         name="pack_other",
-    )(maps, main)
+    )(maps, main, child, front)
+    lead = lax.all_to_all(lead, ROWS, 0, 0, tiled=True)
     near = lax.ppermute(near, "k", swap)
     rest = lax.ppermute(rest, "k", swap)
     column = pl.pallas_call(
         add_column,
-        out_shape=shape(ROW_TILES, T, T),
-        in_specs=[SMEM, VMEM, VMEM, VMEM],
+        out_shape=shape(ROW_TILES * T + 8 * PT, T),
+        in_specs=[SMEM, VMEM, VMEM, VMEM, VMEM],
         out_specs=VMEM,
         compiler_params=params(16),
         name="add_column",
-    )(maps, front, main, near)
+    )(maps, front, main, near, lead)
     down = lax.all_gather(column, "col")
     rows = pl.pallas_call(
         pack_rows,
@@ -438,38 +466,42 @@
         name="pack_rows",
     )(maps, front, main, near)
     rows = lax.all_to_all(rows, ROWS, 0, 0, tiled=True)
-    slab = rows[:PT]
+    slab = pl.pallas_call(
+        take_slab,
+        out_shape=shape(PT, COL_TILES, 8, T),
+        in_specs=[VMEM, ANY],
+        out_specs=VMEM,
+        compiler_params=params(16),
+        name="take_slab",
+    )(rows, rest)
     across = lax.all_gather(slab, ROWS)
-    lead = lax.all_gather(slab[:, 0], "col")
     lead = pl.pallas_call(
         pack_lead,
         out_shape=shape(16, len(UPPER), 8, T),
-        in_specs=[VMEM],
+        in_specs=[ANY],
         out_specs=VMEM,
-        compiler_params=params(16),
+        scratch_shapes=[pltpu.VMEM((PT, 8 * PT, T), F32), pltpu.SemaphoreType.DMA],
+        compiler_params=params(58),
         name="pack_lead",
-    )(lead)
+    )(down)
     lead = lax.all_to_all(lead, ROWS, 0, 0, tiled=True)
-    inverse = pl.pallas_call(
-        invert_factor,
-        out_shape=shape(PT * T, PT * T),
-        in_specs=[VMEM],
-        out_specs=VMEM,
-        scratch_shapes=[pltpu.VMEM((PT * T, PT * T), F32), pltpu.VMEM((T, 2 * T), F32)],
-        compiler_params=params(16),
-        cost_estimate=pl.CostEstimate(flops=25 * 10**9, bytes_accessed=4 * 2**20, transcendentals=0),
-        name="invert_factor",
-    )(lead)
     square = jax.ShapeDtypeStruct((PT * T, PT * T), BF16)
     lower, inverse_high, inverse_low = pl.pallas_call(
-        solve_rows,
+        invert_factor,
         out_shape=(shape(ROW_TILES * T, PT * T), square, square),
-        in_specs=[VMEM, VMEM],
+        in_specs=[VMEM, ANY],
         out_specs=[VMEM] * 3,
-        compiler_params=params(20),
-        cost_estimate=pl.CostEstimate(flops=5 * 10**9, bytes_accessed=8 * 2**20, transcendentals=0),
-        name="solve_rows",
-    )(down, inverse)
+        scratch_shapes=[
+            pltpu.VMEM((PT * T, PT * T), F32),
+            pltpu.VMEM((PT * T, PT * T), F32),
+            pltpu.VMEM((T, 2 * T), F32),
+            pltpu.VMEM((PT, ROW_TILES * T, T), F32),
+            pltpu.SemaphoreType.DMA,
+        ],
+        compiler_params=params(58),
+        cost_estimate=pl.CostEstimate(flops=30 * 10**9, bytes_accessed=8 * 2**20, transcendentals=0),
+        name="invert_factor",
+    )(lead, down)
     block = pl.BlockSpec((T * COL_TILES, T), lambda t: (t, 0))
     out = pl.pallas_call(
         eliminate,

time: 224 us -> 217 us (0.969)
  waiting for transfers between devices: 38.4 us -> 23.3 us
  blocking collectives: 91.6 us -> 103 us
  local copies, waits for them, and re-layouts: 11.3 us -> 3.02 us
  starting transfers between devices: 7.03 us -> 9.28 us
    all_to_all x1 -> x2, blocking collectives: 18.5 us -> 42.5 us  [shards(): lead = lax.all_to_all(lead, ROWS, 0, 0, tiled=True)]
    ppermute x1, waiting for transfers between devices: 15.9 us -> 0.01 us  [shards(): near = lax.ppermute(near, 'k', swap)]
    ppermute x1, waiting for transfers between devices: 0.01 us -> 15.7 us  [shards(): rest = lax.ppermute(rest, 'k', swap)]
    all_gather x1 -> x0, blocking collectives: 12.8 us -> none  [shards(): lead = lax.all_gather(slab[:, 0], 'col')]
    all_to_all x1, waiting for transfers between devices: 18.2 us -> 7.56 us  [shards(): rows = lax.all_to_all(rows, ROWS, 0, 0, tiled=True)]
    unnamed x28 -> x16, local copies, waits for them, and re-layouts: 10.6 us -> 3.02 us
    all_gather x1, waiting for transfers between devices: 4.32 us -> 0.02 us  [shards(): across = lax.all_gather(slab, ROWS)]
  transfers between devices with their start and end apart: 5 -> 5, of which waited for: 3 -> 2; matrix products, arithmetic and copies ran while one was open for 0% -> 0% of each run, Pallas kernels for 17% -> 18%
where the time goes in v6:
time: 217 us; the launch traced here: 214 us
  blocking collectives  103 us (47%)
  Pallas kernels  62.1 us (29%)
  waiting for transfers between devices  23.3 us (11%)
  between operations  13.5 us (6%)
  starting transfers between devices  9.28 us (4%)
  local copies, waits for them, and re-layouts  3.02 us (1%)
    all_to_all x1, blocking collectives, shards(): main = lax.all_to_all(main, ('i', 'col'), 0, 0, tiled=True)  60.4 us
    all_to_all x2, blocking collectives, shards(): lead = lax.all_to_all(lead, ROWS, 0, 0, tiled=True)  42.5 us
    pallas_call x1, Pallas kernels, shards(): pl.pallas_call(invert_factor, out_shape=(shape(ROW_TILES * T, PT * T), sq...  34.9 us
    pallas_call x1, Pallas kernels, shards(): pl.pallas_call(eliminate, out_shape=shape(ROW_TILES * T * COL_TILES, T),...  19.1 us
    ppermute x1, waiting for transfers between devices, shards(): rest = lax.ppermute(rest, 'k', swap)  15.7 us
    all_to_all x1, starting transfers between devices, shards(): rows = lax.all_to_all(rows, ROWS, 0, 0, tiled=True)  7.84 us
    all_to_all x1, waiting for transfers between devices, shards(): rows = lax.all_to_all(rows, ROWS, 0, 0, tiled=True)  7.56 us
  transfers between devices with their start and end apart: 5, of which 2 were waited for; matrix products, arithmetic and copies ran while one was open for 0% of the time, Pallas kernels for 18%

profile of v6, /device:TPU:16, one launch (start us, length us, event | category | flops | bytes accessed | tf_op | source)
XLA Modules:
  0.0 214.1 jit_solution(9275683661779464056)
XLA Ops:
  6.5 1.7 copy-done.1
  8.2 0.7 copy-done.4
  8.9 0.7 copy-done.5
  9.5 0.9 pack_main.1
  10.5 60.4 %all_to_all.20.moved.moved_far = f32[64,128,128]{2,1,0:T(8,128)S(1)} all-to-all(f32[64,128,128]{2,1,0:T(8,128)S(1)} %pack_main.1), channel_id=1, replica_groups=mesh['k'=2,'i'=8,'col'=8] {'i','col'}, dimensions={0} | all-to-all | bytes 8388608 | tf_op jit(solution)/shard_map/all_to_all | solution.py:430
  70.9 0.9 pack_other.1
  71.7 0.7 collective-permute-start
  72.4 18.4 %all_to_all.21.lead = f32[16,8,128]{2,1,0:T(8,128)S(1)} all-to-all(f32[16,8,128]{2,1,0:T(8,128)S(1)} %get-tuple-element.13), channel_id=1, replica_groups=mesh['k'=2,'i'=8,'col'=8] {'k','i'}, dimensions={0} | all-to-all | bytes 131072 | tf_op jit(solution)/shard_map/all_to_all | solution.py:442
  90.8 1.7 add_column.1
  92.6 0.0 all-gather.7.cloned.1.call-update
  92.6 0.7 collective-permute-start.1
  93.3 2.0 pack_rows.1
  95.3 7.8 %all-to-all-start.1 = ((f32[16,12,8,128]{3,2,1,0:T(8,128)}), f32[16,12,8,128]{3,2,1,0:T(8,128)S(1)}, u32[]{:S(2)}, u32[]{:S(2)}) async-start(f32[16,12,8,128]{3,2,1,0:T(8,128)} %pack_rows.1), calls=%async_computation.1 | async-start | bytes 1572864 | tf_op jit(solution)/shard_map/all_to_all | solution.py:468
  103.1 0.0 all-gather.5.cloned.1.call-start
  103.2 15.7 %collective-permute-done.1.other.rest = f32[3,5,128,128]{3,2,1,0:T(8,128)S(1)} collective-permute-done((f32[3,5,128,128]{3,2,1,0:T(8,128)S(1)}, f32[3,5,128,128]{3,2,1,0:T(8,128)S(1)}, u32[]{:S(2)}, u32[]{:S(2)}) %collective-permute-start.1) | collective-permute-done | bytes 983072 | tf_op jit(solution)/shard_map/ppermute | solution.py:444
  118.8 7.6 %all-to-all-done.1.rows = f32[16,12,8,128]{3,2,1,0:T(8,128)S(1)} async-done(((f32[16,12,8,128]{3,2,1,0:T(8,128)}), f32[16,12,8,128]{3,2,1,0:T(8,128)S(1)}, u32[]{:S(2)}, u32[]{:S(2)}) %all-to-all-start.1) | async-done | bytes 786464 | tf_op jit(solution)/shard_map/all_to_all | solution.py:468
  126.4 0.7 take_slab.1
  127.1 0.0 all-gather.5.cloned.1.call-update
  127.1 0.0 all-gather.7.cloned.1.call-done
  127.2 1.9 pack_lead.1
  129.1 24.1 %all_to_all.22.lead = f32[16,15,8,128]{3,2,1,0:T(8,128)} all-to-all(f32[16,15,8,128]{3,2,1,0:T(8,128)} %pack_lead.1), channel_id=1, replica_groups=mesh['k'=2,'i'=8,'col'=8] {'k','i'}, dimensions={0} | all-to-all | bytes 1966080 | tf_op jit(solution)/shard_map/all_to_all | solution.py:487
  153.2 34.9 %invert_factor.1 = (f32[768,640]{1,0:T(8,128)}, bf16[640,640]{1,0:T(8,128)(2,1)}, bf16[640,640]{1,0:T(8,128)(2,1)}) custom-call(f32[16,15,8,128]{3,2,1,0:T(8,128)} %all_to_all.22.lead, f32[8,808,128]{2,1,0:T(8,128)} %bitcast.14), custom_call_target="tpu_custom_call" | custom-call | flops 30000001024 | bytes 8388608 | tf_op jit(solution)/shard_map/invert_factor/pallas_call | solution.py:489
  188.1 0.0 all-gather.5.cloned.1.call-done
  188.1 19.1 %eliminate.1 = f32[9216,128]{1,0:T(8,128)} custom-call(s32[2,48]{1,0:T(2,128)} %maps.9, f32[9216,128]{1,0:T(8,128)} %bitcast.6, f32[16,5,12,8,128]{4,3,2,1,0:T(8,128)} %bitcast.15, f32[768,640]{1,0:T(8,128)} %get-tuple-element.14.lower, bf16[640,640]{1,0:T(8,128)(2,1)} %get-tuple-element.15.inverse_high, bf16[640,640]{1,0:T(8,128)(2,1)} %get-tuple-element.16.inverse_low, ...), custom_call_target="tpu_custom_call" | custom-call | flops 12000000000 | bytes 20971520 | tf_op jit(solution)/shard_map/eliminate/pallas_call | solution.py:506
  (16 shorter events, 0.0 us)
Async XLA Ops:
  6.5 120.6 %all-gather.7.cloned.1.call-start = ((), (), s32[]{:S(2)}) async-start(), calls=%async_computation.5 | async-start | bytes 3723264 | tf_op jit(solution)/shard_map/all_gather | solution.py:453
  6.5 1.7 copy-start.1
  8.2 0.7 copy-start.4
  8.9 0.7 copy-start.5
  9.5 61.3 %slice-start = ((s8[4718592]{0:T(1024)(128)(4,1)}), s8[4194304]{0:T(1024)(128)(4,1)S(1)}, s32[]{:S(2)}) async-start(s8[4718592]{0:T(1024)(128)(4,1)} %bitcast.7), calls=%async_computation.6 | async-start | bytes 8388608
  10.5 60.4 %slice-start.1 = ((s8[4718592]{0:T(1024)(128)(4,1)}), s8[524288]{0:T(1024)(128)(4,1)S(1)}, s32[]{:S(2)}) async-start(s8[4718592]{0:T(1024)(128)(4,1)} %bitcast.7), calls=%async_computation.7 | async-start | bytes 1048576
  70.8 20.0 %copy-start = (f32[64,128,128]{2,1,0:T(8,128)}, f32[64,128,128]{2,1,0:T(8,128)S(1)}, u32[]{:S(2)}) copy-start(f32[64,128,128]{2,1,0:T(8,128)S(1)} %all_to_all.20.moved.moved_far) | copy-start | bytes 12582916
  71.7 19.1 %collective-permute-start = (f32[9,128,128]{2,1,0:T(8,128)S(1)}, f32[9,128,128]{2,1,0:T(8,128)S(1)}, u32[]{:S(2)}, u32[]{:S(2)}) collective-permute-start(f32[9,128,128]{2,1,0:T(8,128)S(1)} %get-tuple-element.11), channel_id=1, source_target_pairs={{0,64},{64,0},{1,65},{65,1},{2,66},{66,2},{3,67},{67,3},{4,68},{68... | collective-permute-start | bytes 1769480 | tf_op jit(solution)/shard_map/ppermute | solution.py:443
  90.8 1.7 copy-start.2
  92.6 26.3 %collective-permute-start.1 = (f32[3,5,128,128]{3,2,1,0:T(8,128)S(1)}, f32[3,5,128,128]{3,2,1,0:T(8,128)S(1)}, u32[]{:S(2)}, u32[]{:S(2)}) collective-permute-start(f32[3,5,128,128]{3,2,1,0:T(8,128)S(1)} %get-tuple-element.12), channel_id=1, source_target_pairs={{0,64},{64,0},{1,65},{65,1},{2,66},{66,2},{3,67},{67,3},{4,68},{68... | collective-permute-start | bytes 2949128 | tf_op jit(solution)/shard_map/ppermute | solution.py:444
  95.3 31.1 %all-to-all-start.1 = ((f32[16,12,8,128]{3,2,1,0:T(8,128)}), f32[16,12,8,128]{3,2,1,0:T(8,128)S(1)}, u32[]{:S(2)}, u32[]{:S(2)}) async-start(f32[16,12,8,128]{3,2,1,0:T(8,128)} %pack_rows.1), calls=%async_computation.1 | async-start | bytes 1572864 | tf_op jit(solution)/shard_map/all_to_all | solution.py:468
  103.1 85.0 %all-gather.5.cloned.1.call-start = ((), (), s32[]{:S(2)}) async-start(), calls=%async_computation.4 | async-start | bytes 4177920 | tf_op jit(solution)/shard_map/all_gather | solution.py:477
  118.8 34.4 %copy-start.3 = (f32[3,5,128,128]{3,2,1,0:T(8,128)}, f32[3,5,128,128]{3,2,1,0:T(8,128)S(1)}, u32[]{:S(2)}) copy-start(f32[3,5,128,128]{3,2,1,0:T(8,128)S(1)} %collective-permute-done.1.other.rest) | copy-start | bytes 2949124
Sparse Core Ops, SparseCore 0:
  92.7 27.9 all-gather.6
  127.3 54.6 all-gather.4

commit v7 on v6

--- a/solution.py
+++ b/solution.py
@@ -14,6 +14,7 @@
 ROWS = ("k", "i")
 UPPER = [(b, c) for b in range(PT) for c in range(b, PT)]
 GROUP = 32
+BLOCK = 2
 HIGHEST = lax.Precision.HIGHEST
 F32 = jnp.float32
 BF16 = jnp.bfloat16
@@ -164,9 +165,30 @@
     return y * (2.0 - x * y)
 
 
-def invert_factor(lead, far, lower, inverse_high, inverse_low, out, matrix, work, down, sem):
-    copy = pltpu.make_async_copy(far.at[pl.ds(0, PT), pl.ds(0, ROW_TILES * T)], down, sem)
-    copy.start()
+def split_rows(far, down_high, down_low, down, sems):
+    copies = [
+        pltpu.make_async_copy(far.at[b, pl.ds(0, ROW_TILES * T)], down.at[b], sems.at[b])
+        for b in range(PT)
+    ]
+    for copy in copies:
+        copy.start()
+    for b in range(PT):
+        copies[b].wait()
+        high, low = halves(down[b])
+        down_high[:, b * T:b * T + T] = high
+        down_low[:, b * T:b * T + T] = low
+
+
+def invert_factor(
+    lead, high_far, low_far, lower, inverse_high, inverse_low,
+    out, matrix, work, down_high, down_low, sems,
+):
+    copies = (
+        pltpu.make_async_copy(high_far, down_high, sems.at[0]),
+        pltpu.make_async_copy(low_far, down_low, sems.at[1]),
+    )
+    for copy in copies:
+        copy.start()
     for n, (b, c) in enumerate(UPPER):
         for r in range(16):
             matrix[b * T + 8 * r:b * T + 8 * r + 8, c * T:c * T + T] = lead[r, n]
@@ -194,27 +216,35 @@
                     for q in after
                 }
                 pivots = jnp.ones((8, T), F32)
-                for m in range(8):
-                    pivot = jnp.broadcast_to(columns[p][m][m:m + 1, :], (8, T))
-                    pivots = jnp.where(sub == m, pivot, pivots)
-                    over = reciprocal(pivot)
-                    row = jnp.broadcast_to(rows[p][m:m + 1, :], (8, T))
-                    mate = jnp.broadcast_to(other[p][m:m + 1, :], (8, T))
-                    for n in range(m + 1, 8):
-                        head = jnp.broadcast_to(columns[p][n][m:m + 1, :], (8, T))
-                        for q in after:
-                            scale = columns[q][m] * over
-                            if q == p:
-                                scale = jnp.where(sub > m, scale, 0.0)
-                            columns[q][n] = columns[q][n] - scale * head
+                for m in range(0, 8, 2):
+                    heads = [
+                        [jnp.broadcast_to(columns[p][n][r:r + 1, :], (8, T)) for r in (m, m + 1)]
+                        for n in range(8)
+                    ]
+                    (one, side), (_, two) = heads[m], heads[m + 1]
+                    over = reciprocal(one * two - side * side)
+                    step = side * reciprocal(one)
+                    pivots = jnp.where(sub == m, one, pivots)
+                    pivots = jnp.where(sub == m + 1, two - side * step, pivots)
+                    row, mate = [
+                        [jnp.broadcast_to(x[p][r:r + 1, :], (8, T)) for r in (m, m + 1)]
+                        for x in (rows, other)
+                    ]
                     for q in after:
-                        scale = columns[q][m] * over
+                        left, right = columns[q][m], columns[q][m + 1]
+                        low = (left * two - right * side) * over
+                        high = (right * one - left * side) * over
                         if q == p:
-                            if m == 7:
-                                continue
-                            scale = jnp.where(sub > m, scale, 0.0)
-                        rows[q] = rows[q] - scale * row
-                        other[q] = other[q] - scale * mate
+                            low = jnp.where(
+                                sub > m + 1, low, jnp.where(sub == m + 1, step, 0.0)
+                            )
+                            high = jnp.where(sub > m + 1, high, 0.0)
+                        for n in range(m + 2, 8):
+                            columns[q][n] = columns[q][n] - (
+                                low * heads[n][0] + high * heads[n][1]
+                            )
+                        rows[q] = rows[q] - (low * row[0] + high * row[1])
+                        other[q] = other[q] - (low * mate[0] + high * mate[1])
                 out[lo + first:lo + first + 8, lo:hi] = other[p] * lax.rsqrt(pivots)
                 inverses.append(1.0 / pivots)
             if base + GROUP < T:
@@ -252,26 +282,20 @@
     high, low = halves(out[...])
     inverse_high[...] = high
     inverse_low[...] = low
-    copy.wait()
-
-    def solve(t, carry):
-        part = pl.ds(pl.multiple_of(t * T, T), T)
-        mine_high, mine_low = halves(jnp.concatenate([down[b, part, :] for b in range(PT)], axis=1))
-        for lo, hi in SPLITS:
-            lower[part, lo:hi] = product(
-                (mine_high[:, :hi], mine_low[:, :hi]),
-                (inverse_high[lo:hi, :hi], inverse_low[lo:hi, :hi]),
-                1,
-            )
-        return carry
-
-    lax.fori_loop(0, ROW_TILES, solve, 0)
+    for copy in copies:
+        copy.wait()
+    for lo, hi in SPLITS:
+        lower[:, lo:hi] = product(
+            (down_high[:, :hi], down_low[:, :hi]),
+            (inverse_high[lo:hi, :hi], inverse_low[lo:hi, :hi]),
+            1,
+        )
 
 
 def eliminate(
     maps, front, across_far, lower, inverse_high, inverse_low,
     moved_far, near, rest, out,
-    pivot_high, pivot_low, upper_high, upper_low, across, moved, other, across_sem, sems,
+    pivot_high, pivot_low, upper, across, moved, other, across_sem, sems,
 ):
     k, i, j = place()
     row = k * 8 + i
@@ -305,28 +329,31 @@
                 pivot_high[b * T:b * T + T, s * T:s * T + T] = high
                 pivot_low[b * T:b * T + T, s * T:s * T + T] = low
 
-        def solve_upper(n, carry):
-            part = pl.ds(pl.multiple_of(n * WIDE, WIDE), WIDE)
+        for n in range(COL_TILES * T // WIDE):
+            part = slice(n * WIDE, n * WIDE + WIDE)
             for lo, hi in SPLITS:
-                high, low = halves(product(
-                    (inverse_high[lo:hi, :hi], inverse_low[lo:hi, :hi]),
-                    (pivot_high[:hi, part], pivot_low[:hi, part]),
+                first, second = inverse_high[lo:hi, :hi], inverse_low[lo:hi, :hi]
+                high, low = halves(jnp.dot(
+                    jnp.concatenate([first, first, second], axis=1),
+                    jnp.concatenate(
+                        [pivot_high[:hi, part], pivot_low[:hi, part], pivot_high[:hi, part]], axis=0
+                    ),
+                    preferred_element_type=F32,
                 ))
-                upper_high[lo:hi, part] = high
-                upper_low[lo:hi, part] = low
-            return carry
-
-        lax.fori_loop(0, COL_TILES * T // WIDE, solve_upper, 0)
-
-    mine_halves = halves(lower[...])
+                upper[lo:hi, part] = high
+                upper[PT * T + lo:PT * T + hi, part] = low
+                upper[2 * PT * T + lo:2 * PT * T + hi, part] = high
+
+    first, second = halves(lower[...])
+    mine = jnp.concatenate([first, first, second], axis=1)
     for n in range(COL_TILES * T // WIDE):
-        change = product(
-            mine_halves,
-            (upper_high[:, n * WIDE:n * WIDE + WIDE], upper_low[:, n * WIDE:n * WIDE + WIDE]),
+        change = jnp.dot(
+            mine, upper[:, n * WIDE:n * WIDE + WIDE], preferred_element_type=F32
         )
-        for s in range(WIDE // T):
-            where = pl.ds(n * (WIDE // T) + s, T, stride=COL_TILES)
-            out[where, :] = front[where, :] - change[:, s * T:s * T + T]
+        for r in range(BLOCK):
+            for s in range(WIDE // T):
+                where = pl.ds(r * T * COL_TILES + n * (WIDE // T) + s, T, stride=COL_TILES)
+                out[where, :] = front[where, :] - change[r * T:r * T + T, s * T:s * T + T]
 
     @pl.when(t == 0)
     def _():
@@ -342,10 +369,11 @@
 
     @pl.when(j < PT)
     def _():
-        tile = lower[:, pl.ds(pl.multiple_of(j * T, T), T)]
-        x = lax.broadcasted_iota(jnp.int32, (T, T), 0) + (16 * t + row) * T
-        y = lax.broadcasted_iota(jnp.int32, (T, T), 1) + j * T
-        out[pl.ds(0, T, stride=COL_TILES), :] = jnp.where(x >= y, tile, 0.0)
+        for r in range(BLOCK):
+            tile = lower[r * T:r * T + T, pl.ds(pl.multiple_of(j * T, T), T)]
+            x = lax.broadcasted_iota(jnp.int32, (T, T), 0) + (16 * (BLOCK * t + r) + row) * T
+            y = lax.broadcasted_iota(jnp.int32, (T, T), 1) + j * T
+            out[pl.ds(r * T * COL_TILES, T, stride=COL_TILES), :] = jnp.where(x >= y, tile, 0.0)
 
 
 def pack_other(maps, moved, child, front, near, rest, lead):
@@ -384,11 +412,12 @@
     k, i, j = place()
     t = pl.program_id(0)
 
-    def add(child, tile_of):
+    def add(child, p, tile_of):
         for h in range(CHILD_TILES):
             across = offset(maps, child, h)
             from_j = (j - across) % 8
-            where = pl.ds((8 * h + from_j + across) // 8, T, stride=COL_TILES)
+            first = p // 16 % BLOCK * (T * COL_TILES) + (8 * h + from_j + across) // 8
+            where = pl.ds(first, T, stride=COL_TILES)
             out[where, :] = out[where, :] + tile_of(h, from_j)
 
     rank = jnp.int32(0)
@@ -398,9 +427,9 @@
         p = 8 * g + source + shift
         mine = p // 8 % 2 == k
 
-        @pl.when(jnp.logical_and(mine, p // 16 == t))
-        def _():
-            add(k, lambda h, from_j: moved[source * 8 + from_j])
+        @pl.when(jnp.logical_and(mine, p // 16 // BLOCK == t))
+        def _():
+            add(k, p, lambda h, from_j: moved[source * 8 + from_j])
 
         far = 1 - k
         far_shift = offset(maps, far, g)
@@ -408,9 +437,9 @@
         comes = far_p // 8 % 2 == k
         here = jnp.minimum(rank, 3)
 
-        @pl.when(jnp.logical_and(comes, far_p // 16 == t))
-        def _():
-            add(far, lambda h, from_j: other[here, h])
+        @pl.when(jnp.logical_and(comes, far_p // 16 // BLOCK == t))
+        def _():
+            add(far, far_p, lambda h, from_j: other[here, h])
 
         rank = rank + comes.astype(jnp.int32)
 
@@ -485,35 +514,47 @@
         name="pack_lead",
     )(down)
     lead = lax.all_to_all(lead, ROWS, 0, 0, tiled=True)
+    tall = jax.ShapeDtypeStruct((ROW_TILES * T, PT * T), BF16)
+    halved = pl.pallas_call(
+        split_rows,
+        out_shape=(tall, tall),
+        in_specs=[ANY],
+        out_specs=[VMEM] * 2,
+        scratch_shapes=[
+            pltpu.VMEM((PT, ROW_TILES * T, T), F32), pltpu.SemaphoreType.DMA((PT,)),
+        ],
+        compiler_params=params(40),
+        name="split_rows",
+    )(down)
     square = jax.ShapeDtypeStruct((PT * T, PT * T), BF16)
     lower, inverse_high, inverse_low = pl.pallas_call(
         invert_factor,
         out_shape=(shape(ROW_TILES * T, PT * T), square, square),
-        in_specs=[VMEM, ANY],
+        in_specs=[VMEM, ANY, ANY],
         out_specs=[VMEM] * 3,
         scratch_shapes=[
             pltpu.VMEM((PT * T, PT * T), F32),
             pltpu.VMEM((PT * T, PT * T), F32),
             pltpu.VMEM((T, 2 * T), F32),
-            pltpu.VMEM((PT, ROW_TILES * T, T), F32),
-            pltpu.SemaphoreType.DMA,
+            pltpu.VMEM((ROW_TILES * T, PT * T), BF16),
+            pltpu.VMEM((ROW_TILES * T, PT * T), BF16),
+            pltpu.SemaphoreType.DMA((2,)),
         ],
         compiler_params=params(58),
         cost_estimate=pl.CostEstimate(flops=30 * 10**9, bytes_accessed=8 * 2**20, transcendentals=0),
         name="invert_factor",
-    )(lead, down)
-    block = pl.BlockSpec((T * COL_TILES, T), lambda t: (t, 0))
+    )(lead, *halved)
+    block = pl.BlockSpec((BLOCK * T * COL_TILES, T), lambda t: (t, 0))
     out = pl.pallas_call(
         eliminate,
         out_shape=shape(ROW_TILES * T * COL_TILES, T),
-        grid=(ROW_TILES,),
-        in_specs=[SMEM, block, ANY, pl.BlockSpec((T, PT * T), lambda t: (t, 0))] + [VMEM] * 2 + [ANY] * 3,
+        grid=(ROW_TILES // BLOCK,),
+        in_specs=[SMEM, block, ANY, pl.BlockSpec((BLOCK * T, PT * T), lambda t: (t, 0))] + [VMEM] * 2 + [ANY] * 3,
         out_specs=block,
         scratch_shapes=[
             pltpu.VMEM((PT * T, COL_TILES * T), BF16),
             pltpu.VMEM((PT * T, COL_TILES * T), BF16),
-            pltpu.VMEM((PT * T, COL_TILES * T), BF16),
-            pltpu.VMEM((PT * T, COL_TILES * T), BF16),
+            pltpu.VMEM((3 * PT * T, COL_TILES * T), BF16),
             pltpu.VMEM((16, PT, COL_TILES, 8, T), F32),
             pltpu.VMEM((64, T, T), F32),
             pltpu.VMEM((4, CHILD_TILES, T, T), F32),

time: 217 us -> 210 us (0.968)
  blocking collectives: 103 us -> 78.7 us
  waiting for transfers between devices: 23.3 us -> 37.4 us
  starting transfers between devices: 9.28 us -> 16 us
  Pallas kernels: 62.1 us -> 56.2 us
    all_to_all x2 -> x1, blocking collectives: 42.5 us -> 18.4 us  [shards(): lead = lax.all_to_all(lead, ROWS, 0, 0, tiled=True)]
    all_to_all x0 -> x1, waiting for transfers between devices: none -> 13.9 us  [shards(): lead = lax.all_to_all(lead, ROWS, 0, 0, tiled=True)]
    all_to_all x0 -> x1, starting transfers between devices: none -> 6.7 us  [shards(): lead = lax.all_to_all(lead, ROWS, 0, 0, tiled=True)]
    pallas_call x1, Pallas kernels: 34.9 us -> 29.2 us  [shards(): pl.pallas_call(invert_factor, out_shape=(shape(ROW_TILES * T, PT * T), sq...]
    unnamed x16 -> x22, local copies, waits for them, and re-layouts: 3.02 us -> 4.92 us
  transfers between devices with their start and end apart: 5 -> 6, of which waited for: 2 -> 4; matrix products, arithmetic and copies ran while one was open for 0% -> 0% of each run, Pallas kernels for 18% -> 17%
where the time goes in v7:
time: 210 us; the launch traced here: 207 us
  blocking collectives  78.7 us (37%)
  Pallas kernels  56.2 us (27%)
  waiting for transfers between devices  37.4 us (18%)
  starting transfers between devices  16 us (8%)
  between operations  13.5 us (6%)
  local copies, waits for them, and re-layouts  4.92 us (2%)
    all_to_all x1, blocking collectives, shards(): main = lax.all_to_all(main, ('i', 'col'), 0, 0, tiled=True)  60.4 us
    pallas_call x1, Pallas kernels, shards(): pl.pallas_call(invert_factor, out_shape=(shape(ROW_TILES * T, PT * T), sq...  29.2 us
    all_to_all x1, blocking collectives, shards(): lead = lax.all_to_all(lead, ROWS, 0, 0, tiled=True)  18.4 us
    pallas_call x1, Pallas kernels, shards(): pl.pallas_call(eliminate, out_shape=shape(ROW_TILES * T * COL_TILES, T),...  17.1 us
    ppermute x1, waiting for transfers between devices, shards(): rest = lax.ppermute(rest, 'k', swap)  15.7 us
    all_to_all x1, waiting for transfers between devices, shards(): lead = lax.all_to_all(lead, ROWS, 0, 0, tiled=True)  13.9 us
    all_to_all x1, starting transfers between devices, shards(): rows = lax.all_to_all(rows, ROWS, 0, 0, tiled=True)  7.81 us
    all_to_all x1, waiting for transfers between devices, shards(): rows = lax.all_to_all(rows, ROWS, 0, 0, tiled=True)  7.63 us
  transfers between devices with their start and end apart: 6, of which 4 were waited for; matrix products, arithmetic and copies ran while one was open for 0% of the time, Pallas kernels for 17%

profile of v7, /device:TPU:16, one launch (start us, length us, event | category | flops | bytes accessed | tf_op | source)
XLA Modules:
  0.0 206.7 jit_solution(8207658363321082058)
XLA Ops:
  6.5 1.7 copy-done.2
  8.2 0.7 copy-done.5
  8.9 0.7 copy-done.6
  9.5 0.9 pack_main.1
  10.5 60.4 %all_to_all.20.moved.moved_far = f32[64,128,128]{2,1,0:T(8,128)S(1)} all-to-all(f32[64,128,128]{2,1,0:T(8,128)S(1)} %pack_main.1), channel_id=1, replica_groups=mesh['k'=2,'i'=8,'col'=8] {'i','col'}, dimensions={0} | all-to-all | bytes 8388608 | tf_op jit(solution)/shard_map/all_to_all | solution.py:459
  70.9 0.9 pack_other.1
  71.8 0.7 collective-permute-start
  72.4 18.4 %all_to_all.21.lead = f32[16,8,128]{2,1,0:T(8,128)S(1)} all-to-all(f32[16,8,128]{2,1,0:T(8,128)S(1)} %get-tuple-element.15), channel_id=1, replica_groups=mesh['k'=2,'i'=8,'col'=8] {'k','i'}, dimensions={0} | all-to-all | bytes 131072 | tf_op jit(solution)/shard_map/all_to_all | solution.py:471
  90.8 1.7 add_column.1
  92.5 0.8 collective-permute-start.1
  93.3 2.0 pack_rows.1
  95.3 7.8 %all-to-all-start.1 = ((f32[16,12,8,128]{3,2,1,0:T(8,128)}), f32[16,12,8,128]{3,2,1,0:T(8,128)S(1)}, u32[]{:S(2)}, u32[]{:S(2)}) async-start(f32[16,12,8,128]{3,2,1,0:T(8,128)} %pack_rows.1), calls=%async_computation.1 | async-start | bytes 1572864 | tf_op jit(solution)/shard_map/all_to_all | solution.py:497
  103.1 15.7 %collective-permute-done.1.other.rest = f32[3,5,128,128]{3,2,1,0:T(8,128)S(1)} collective-permute-done((f32[3,5,128,128]{3,2,1,0:T(8,128)S(1)}, f32[3,5,128,128]{3,2,1,0:T(8,128)S(1)}, u32[]{:S(2)}, u32[]{:S(2)}) %collective-permute-start.1) | collective-permute-done | bytes 983072 | tf_op jit(solution)/shard_map/ppermute | solution.py:473
  118.8 7.6 %all-to-all-done.1.rows = f32[16,12,8,128]{3,2,1,0:T(8,128)S(1)} async-done(((f32[16,12,8,128]{3,2,1,0:T(8,128)}), f32[16,12,8,128]{3,2,1,0:T(8,128)S(1)}, u32[]{:S(2)}, u32[]{:S(2)}) %all-to-all-start.1) | async-done | bytes 786464 | tf_op jit(solution)/shard_map/all_to_all | solution.py:497
  126.4 0.7 take_slab.1
  127.2 2.1 pack_lead.1
  129.3 6.7 %all-to-all-start.3 = ((f32[16,15,8,128]{3,2,1,0:T(8,128)}), f32[16,15,8,128]{3,2,1,0:T(8,128)}, u32[]{:S(2)}, u32[]{:S(2)}) async-start(f32[16,15,8,128]{3,2,1,0:T(8,128)} %pack_lead.1), calls=%async_computation.3 | async-start | bytes 1966080 | tf_op jit(solution)/shard_map/all_to_all | solution.py:516
  136.0 1.6 split_rows.1
  137.6 0.9 copy-done.7
  138.5 1.0 copy-done.8
  139.5 13.9 %all-to-all-done.3.lead = f32[16,15,8,128]{3,2,1,0:T(8,128)} async-done(((f32[16,15,8,128]{3,2,1,0:T(8,128)}), f32[16,15,8,128]{3,2,1,0:T(8,128)}, u32[]{:S(2)}, u32[]{:S(2)}) %all-to-all-start.3) | async-done | bytes 983072 | tf_op jit(solution)/shard_map/all_to_all | solution.py:516
  153.3 29.2 %invert_factor.1 = (f32[768,640]{1,0:T(8,128)}, bf16[640,640]{1,0:T(8,128)(2,1)}, bf16[640,640]{1,0:T(8,128)(2,1)}) custom-call(f32[16,15,8,128]{3,2,1,0:T(8,128)} %all-to-all-done.3.lead, bf16[768,640]{1,0:T(8,128)(2,1)} %copy-done.7, bf16[768,640]{1,0:T(8,128)(2,1)} %copy-done.8), custom_call_target="tpu_custom_call" | custom-call | flops 30000001024 | bytes 8388608 | tf_op jit(solution)/shard_map/invert_factor/pallas_call | solution.py:530
  182.6 0.2 all-gather.5.cloned.1.call-done
  182.7 17.1 %eliminate.1 = f32[9216,128]{1,0:T(8,128)} custom-call(s32[2,48]{1,0:T(2,128)} %maps.9, f32[9216,128]{1,0:T(8,128)} %bitcast.6, f32[16,5,12,8,128]{4,3,2,1,0:T(8,128)} %bitcast.15, f32[768,640]{1,0:T(8,128)} %get-tuple-element.18.lower, bf16[640,640]{1,0:T(8,128)(2,1)} %get-tuple-element.19.inverse_high, bf16[640,640]{1,0:T(8,128)(2,1)} %get-tuple-element.20.inverse_low, ...), custom_call_target="tpu_custom_call" | custom-call | flops 12000000000 | bytes 20971520 | tf_op jit(solution)/shard_map/eliminate/pallas_call | solution.py:548
  (24 shorter events, 0.1 us)
Async XLA Ops:
  6.5 120.7 %all-gather.7.cloned.1.call-start = ((), (), s32[]{:S(2)}) async-start(), calls=%async_computation.5 | async-start | bytes 3723264 | tf_op jit(solution)/shard_map/all_gather | solution.py:482
  6.5 1.7 copy-start.2
  8.2 0.7 copy-start.5
  8.9 0.7 copy-start.6
  9.5 61.3 %slice-start = ((s8[4718592]{0:T(1024)(128)(4,1)}), s8[4194304]{0:T(1024)(128)(4,1)S(1)}, s32[]{:S(2)}) async-start(s8[4718592]{0:T(1024)(128)(4,1)} %bitcast.7), calls=%async_computation.6 | async-start | bytes 8388608
  10.5 60.4 %slice-start.1 = ((s8[4718592]{0:T(1024)(128)(4,1)}), s8[524288]{0:T(1024)(128)(4,1)S(1)}, s32[]{:S(2)}) async-start(s8[4718592]{0:T(1024)(128)(4,1)} %bitcast.7), calls=%async_computation.7 | async-start | bytes 1048576
  70.8 20.0 %copy-start = (f32[64,128,128]{2,1,0:T(8,128)}, f32[64,128,128]{2,1,0:T(8,128)S(1)}, u32[]{:S(2)}) copy-start(f32[64,128,128]{2,1,0:T(8,128)S(1)} %all_to_all.20.moved.moved_far) | copy-start | bytes 12582916
  71.8 19.0 %collective-permute-start = (f32[9,128,128]{2,1,0:T(8,128)S(1)}, f32[9,128,128]{2,1,0:T(8,128)S(1)}, u32[]{:S(2)}, u32[]{:S(2)}) collective-permute-start(f32[9,128,128]{2,1,0:T(8,128)S(1)} %get-tuple-element.13), channel_id=1, source_target_pairs={{0,64},{64,0},{1,65},{65,1},{2,66},{66,2},{3,67},{67,3},{4,68},{68... | collective-permute-start | bytes 1769480 | tf_op jit(solution)/shard_map/ppermute | solution.py:472
  90.8 1.7 copy-start.3
  92.5 26.3 %collective-permute-start.1 = (f32[3,5,128,128]{3,2,1,0:T(8,128)S(1)}, f32[3,5,128,128]{3,2,1,0:T(8,128)S(1)}, u32[]{:S(2)}, u32[]{:S(2)}) collective-permute-start(f32[3,5,128,128]{3,2,1,0:T(8,128)S(1)} %get-tuple-element.14), channel_id=1, source_target_pairs={{0,64},{64,0},{1,65},{65,1},{2,66},{66,2},{3,67},{67,3},{4,68},{68... | collective-permute-start | bytes 2949128 | tf_op jit(solution)/shard_map/ppermute | solution.py:473
  95.3 31.1 %all-to-all-start.1 = ((f32[16,12,8,128]{3,2,1,0:T(8,128)}), f32[16,12,8,128]{3,2,1,0:T(8,128)S(1)}, u32[]{:S(2)}, u32[]{:S(2)}) async-start(f32[16,12,8,128]{3,2,1,0:T(8,128)} %pack_rows.1), calls=%async_computation.1 | async-start | bytes 1572864 | tf_op jit(solution)/shard_map/all_to_all | solution.py:497
  103.1 79.7 %all-gather.5.cloned.1.call-start = ((), (), s32[]{:S(2)}) async-start(), calls=%async_computation.4 | async-start | bytes 4177920 | tf_op jit(solution)/shard_map/all_gather | solution.py:506
  118.8 8.4 %copy-start.4 = (f32[3,5,128,128]{3,2,1,0:T(8,128)}, f32[3,5,128,128]{3,2,1,0:T(8,128)S(1)}, u32[]{:S(2)}) copy-start(f32[3,5,128,128]{3,2,1,0:T(8,128)S(1)} %collective-permute-done.1.other.rest) | copy-start | bytes 2949124
  127.2 8.8 %copy-start.1 = (f32[6464,128]{1,0:T(8,128)S(1)}, f32[6464,128]{1,0:T(8,128)}, u32[]{:S(2)}) copy-start(f32[6464,128]{1,0:T(8,128)} %all-gather.7.cloned.1.call-done) | copy-start | bytes 9928708
  129.3 24.1 %all-to-all-start.3 = ((f32[16,15,8,128]{3,2,1,0:T(8,128)}), f32[16,15,8,128]{3,2,1,0:T(8,128)}, u32[]{:S(2)}, u32[]{:S(2)}) async-start(f32[16,15,8,128]{3,2,1,0:T(8,128)} %pack_lead.1), calls=%async_computation.3 | async-start | bytes 1966080 | tf_op jit(solution)/shard_map/all_to_all | solution.py:516
  137.6 1.0 copy-start.7
  138.5 1.0 copy-start.8
Sparse Core Ops, SparseCore 0:
  92.7 28.0 all-gather.6
  127.3 55.4 all-gather.4

commit v8 on v7

--- a/solution.py
+++ b/solution.py
@@ -51,14 +51,31 @@
     return tile
 
 
-def pack_main(maps, orders, child, out):
+def pack_main(maps, orders, far, out, child, tiles, came, went):
     k, i, j = place()
     order = orders[k]
+    size = T * CHILD_TILES
+    arrivals = [
+        pltpu.make_async_copy(
+            far.at[pl.ds(g * size, size)], child.at[pl.ds(g * size, size)], came.at[g]
+        )
+        for g in range(CHILD_TILES)
+    ]
+    for copy in arrivals:
+        copy.start()
+    sent = []
     for g in range(CHILD_TILES):
+        arrivals[g].wait()
         to_i = (i + offset(maps, k, g)) % 8
         for h in range(CHILD_TILES):
+            n = g * CHILD_TILES + h
             to_j = (j + offset(maps, k, h)) % 8
-            out[to_i * 8 + to_j] = child_tile(child, order, i, j, g, h)
+            tiles[n] = child_tile(child, order, i, j, g, h)
+            copy = pltpu.make_async_copy(tiles.at[n], out.at[to_i * 8 + to_j], went.at[n])
+            copy.start()
+            sent.append(copy)
+    for copy in sent:
+        copy.wait()
 
 
 def add_column(maps, front, moved, other, lead, out):
@@ -451,9 +468,15 @@
     main = pl.pallas_call(
         pack_main,
         out_shape=shape(64, T, T),
-        in_specs=[SMEM, SMEM, VMEM],
-        out_specs=VMEM,
-        compiler_params=params(16),
+        in_specs=[SMEM, SMEM, ANY],
+        out_specs=ANY,
+        scratch_shapes=[
+            pltpu.VMEM((CHILD_TILES * T * CHILD_TILES, T), F32),
+            pltpu.VMEM((CHILD_TILES * CHILD_TILES, T, T), F32),
+            pltpu.SemaphoreType.DMA((CHILD_TILES,)),
+            pltpu.SemaphoreType.DMA((CHILD_TILES * CHILD_TILES,)),
+        ],
+        compiler_params=params(58),
         name="pack_main",
     )(maps, child_orders, child)
     main = lax.all_to_all(main, ("i", "col"), 0, 0, tiled=True)

time: 210 us -> 210 us (level)
  local copies, waits for them, and re-layouts: 4.92 us -> 1.94 us
  Pallas kernels: 56.2 us -> 58.8 us
    unnamed x22 -> x20, local copies, waits for them, and re-layouts: 4.92 us -> 1.94 us
    pallas_call x1, Pallas kernels: 0.92 us -> 3.57 us  [shards(): pl.pallas_call(pack_main, out_shape=shape(64, T, T), in_specs=[SMEM, SMEM...]
where the time goes in v8:
time: 210 us; the launch traced here: 207 us
  blocking collectives  79.1 us (38%)
  Pallas kernels  58.8 us (28%)
  waiting for transfers between devices  37.3 us (18%)
  starting transfers between devices  16 us (8%)
  between operations  13.6 us (6%)
    all_to_all x1, blocking collectives, shards(): main = lax.all_to_all(main, ('i', 'col'), 0, 0, tiled=True)  60.7 us
    pallas_call x1, Pallas kernels, shards(): pl.pallas_call(invert_factor, out_shape=(shape(ROW_TILES * T, PT * T), sq...  29.2 us
    all_to_all x1, blocking collectives, shards(): lead = lax.all_to_all(lead, ROWS, 0, 0, tiled=True)  18.4 us
    pallas_call x1, Pallas kernels, shards(): pl.pallas_call(eliminate, out_shape=shape(ROW_TILES * T * COL_TILES, T),...  17.1 us
    ppermute x1, waiting for transfers between devices, shards(): rest = lax.ppermute(rest, 'k', swap)  15.7 us
    all_to_all x1, waiting for transfers between devices, shards(): lead = lax.all_to_all(lead, ROWS, 0, 0, tiled=True)  13.9 us
    all_to_all x1, starting transfers between devices, shards(): rows = lax.all_to_all(rows, ROWS, 0, 0, tiled=True)  7.84 us
    all_to_all x1, waiting for transfers between devices, shards(): rows = lax.all_to_all(rows, ROWS, 0, 0, tiled=True)  7.62 us
  transfers between devices with their start and end apart: 6, of which 4 were waited for; matrix products, arithmetic and copies ran while one was open for 0% of the time, Pallas kernels for 17%

profile of v8, /device:TPU:16, one launch (start us, length us, event | category | flops | bytes accessed | tf_op | source)
XLA Modules:
  0.0 206.7 jit_solution(10488271522081254292)
XLA Ops:
  6.5 3.6 %pack_main.1 = f32[64,128,128]{2,1,0:T(8,128)} custom-call(s32[2,48]{1,0:T(2,128)} %maps.9, s32[2]{0:T(128)} %orders.1, f32[4608,128]{1,0:T(8,128)} %bitcast.13), custom_call_target="tpu_custom_call" | custom-call | tf_op jit(solution)/shard_map/pack_main/pallas_call | solution.py:468
  10.2 60.7 %all_to_all.20.moved.moved_far = f32[64,128,128]{2,1,0:T(8,128)S(1)} all-to-all(f32[64,128,128]{2,1,0:T(8,128)} %pack_main.1), channel_id=1, replica_groups=mesh['k'=2,'i'=8,'col'=8] {'i','col'}, dimensions={0} | all-to-all | bytes 8388608 | tf_op jit(solution)/shard_map/all_to_all | solution.py:482
  70.9 0.9 pack_other.1
  71.8 0.7 collective-permute-start
  72.5 18.4 %all_to_all.21.lead = f32[16,8,128]{2,1,0:T(8,128)S(1)} all-to-all(f32[16,8,128]{2,1,0:T(8,128)S(1)} %get-tuple-element.15), channel_id=1, replica_groups=mesh['k'=2,'i'=8,'col'=8] {'k','i'}, dimensions={0} | all-to-all | bytes 131072 | tf_op jit(solution)/shard_map/all_to_all | solution.py:494
  90.8 1.7 add_column.1
  92.5 0.0 all-gather.7.cloned.1.call-update
  92.6 0.7 collective-permute-start.1
  93.3 2.0 pack_rows.1
  95.3 7.8 %all-to-all-start.1 = ((f32[16,12,8,128]{3,2,1,0:T(8,128)}), f32[16,12,8,128]{3,2,1,0:T(8,128)S(1)}, u32[]{:S(2)}, u32[]{:S(2)}) async-start(f32[16,12,8,128]{3,2,1,0:T(8,128)} %pack_rows.1), calls=%async_computation.1 | async-start | bytes 1572864 | tf_op jit(solution)/shard_map/all_to_all | solution.py:520
  103.1 0.0 all-gather.5.cloned.1.call-start
  103.2 15.7 %collective-permute-done.1.other.rest = f32[3,5,128,128]{3,2,1,0:T(8,128)S(1)} collective-permute-done((f32[3,5,128,128]{3,2,1,0:T(8,128)S(1)}, f32[3,5,128,128]{3,2,1,0:T(8,128)S(1)}, u32[]{:S(2)}, u32[]{:S(2)}) %collective-permute-start.1) | collective-permute-done | bytes 983072 | tf_op jit(solution)/shard_map/ppermute | solution.py:496
  118.8 7.6 %all-to-all-done.1.rows = f32[16,12,8,128]{3,2,1,0:T(8,128)S(1)} async-done(((f32[16,12,8,128]{3,2,1,0:T(8,128)}), f32[16,12,8,128]{3,2,1,0:T(8,128)S(1)}, u32[]{:S(2)}, u32[]{:S(2)}) %all-to-all-start.1) | async-done | bytes 786464 | tf_op jit(solution)/shard_map/all_to_all | solution.py:520
  126.4 0.7 take_slab.1
  127.2 0.0 all-gather.7.cloned.1.call-done
  127.2 2.1 pack_lead.1
  129.3 6.7 %all-to-all-start.3 = ((f32[16,15,8,128]{3,2,1,0:T(8,128)}), f32[16,15,8,128]{3,2,1,0:T(8,128)}, u32[]{:S(2)}, u32[]{:S(2)}) async-start(f32[16,15,8,128]{3,2,1,0:T(8,128)} %pack_lead.1), calls=%async_computation.3 | async-start | bytes 1966080 | tf_op jit(solution)/shard_map/all_to_all | solution.py:539
  136.0 1.6 split_rows.1
  137.6 0.9 copy-done.6
  138.6 1.0 copy-done.7
  139.5 13.9 %all-to-all-done.3.lead = f32[16,15,8,128]{3,2,1,0:T(8,128)} async-done(((f32[16,15,8,128]{3,2,1,0:T(8,128)}), f32[16,15,8,128]{3,2,1,0:T(8,128)}, u32[]{:S(2)}, u32[]{:S(2)}) %all-to-all-start.3) | async-done | bytes 983072 | tf_op jit(solution)/shard_map/all_to_all | solution.py:539
  153.4 29.2 %invert_factor.1 = (f32[768,640]{1,0:T(8,128)}, bf16[640,640]{1,0:T(8,128)(2,1)}, bf16[640,640]{1,0:T(8,128)(2,1)}) custom-call(f32[16,15,8,128]{3,2,1,0:T(8,128)} %all-to-all-done.3.lead, bf16[768,640]{1,0:T(8,128)(2,1)} %copy-done.6, bf16[768,640]{1,0:T(8,128)(2,1)} %copy-done.7), custom_call_target="tpu_custom_call" | custom-call | flops 30000001024 | bytes 8388608 | tf_op jit(solution)/shard_map/invert_factor/pallas_call | solution.py:553
  182.6 0.2 all-gather.5.cloned.1.call-done
  182.8 17.1 %eliminate.1 = f32[9216,128]{1,0:T(8,128)} custom-call(s32[2,48]{1,0:T(2,128)} %maps.9, f32[9216,128]{1,0:T(8,128)} %bitcast.6, f32[16,5,12,8,128]{4,3,2,1,0:T(8,128)} %bitcast.15, f32[768,640]{1,0:T(8,128)} %get-tuple-element.18.lower, bf16[640,640]{1,0:T(8,128)(2,1)} %get-tuple-element.19.inverse_high, bf16[640,640]{1,0:T(8,128)(2,1)} %get-tuple-element.20.inverse_low, ...), custom_call_target="tpu_custom_call" | custom-call | flops 12000000000 | bytes 20971520 | tf_op jit(solution)/shard_map/eliminate/pallas_call | solution.py:571
  (22 shorter events, 0.1 us)
Async XLA Ops:
  6.5 120.7 %all-gather.7.cloned.1.call-start = ((), (), s32[]{:S(2)}) async-start(), calls=%async_computation.5 | async-start | bytes 3723264 | tf_op jit(solution)/shard_map/all_gather | solution.py:505
  6.5 64.3 %slice-start = ((s8[4718592]{0:T(1024)(128)(4,1)}), s8[524288]{0:T(1024)(128)(4,1)S(1)}, s32[]{:S(2)}) async-start(s8[4718592]{0:T(1024)(128)(4,1)} %bitcast.7), calls=%async_computation.6 | async-start | bytes 1048576
  10.1 60.7 %slice-start.1 = ((s8[4718592]{0:T(1024)(128)(4,1)}), s8[4194304]{0:T(1024)(128)(4,1)S(1)}, s32[]{:S(2)}) async-start(s8[4718592]{0:T(1024)(128)(4,1)} %bitcast.7), calls=%async_computation.7 | async-start | bytes 8388608
  10.1 60.7 %copy-start.2 = (f32[6,1,128,6,1,128]{5,4,3,2,1,0:T(1,128)S(1)}, f32[6,1,128,6,1,128]{5,4,3,2,1,0:T(1,128)}, u32[]{:S(2)}) copy-start(f32[6,1,128,6,1,128]{5,4,3,2,1,0:T(1,128)} %param.5) | copy-start | bytes 7077892
  10.1 60.7 %copy-start.5 = (s32[2,48]{1,0:T(2,128)S(1)}, s32[2,48]{1,0:T(2,128)}, u32[]{:S(2)}) copy-start(s32[2,48]{1,0:T(2,128)} %maps.9) | copy-start | bytes 1156
  70.9 20.0 %copy-start = (f32[64,128,128]{2,1,0:T(8,128)}, f32[64,128,128]{2,1,0:T(8,128)S(1)}, u32[]{:S(2)}) copy-start(f32[64,128,128]{2,1,0:T(8,128)S(1)} %all_to_all.20.moved.moved_far) | copy-start | bytes 12582916
  71.8 19.0 %collective-permute-start = (f32[9,128,128]{2,1,0:T(8,128)S(1)}, f32[9,128,128]{2,1,0:T(8,128)S(1)}, u32[]{:S(2)}, u32[]{:S(2)}) collective-permute-start(f32[9,128,128]{2,1,0:T(8,128)S(1)} %get-tuple-element.13), channel_id=1, source_target_pairs={{0,64},{64,0},{1,65},{65,1},{2,66},{66,2},{3,67},{67,3},{4,68},{68... | collective-permute-start | bytes 1769480 | tf_op jit(solution)/shard_map/ppermute | solution.py:495
  90.8 1.7 copy-start.3
  92.6 26.3 %collective-permute-start.1 = (f32[3,5,128,128]{3,2,1,0:T(8,128)S(1)}, f32[3,5,128,128]{3,2,1,0:T(8,128)S(1)}, u32[]{:S(2)}, u32[]{:S(2)}) collective-permute-start(f32[3,5,128,128]{3,2,1,0:T(8,128)S(1)} %get-tuple-element.14), channel_id=1, source_target_pairs={{0,64},{64,0},{1,65},{65,1},{2,66},{66,2},{3,67},{67,3},{4,68},{68... | collective-permute-start | bytes 2949128 | tf_op jit(solution)/shard_map/ppermute | solution.py:496
  95.3 31.2 %all-to-all-start.1 = ((f32[16,12,8,128]{3,2,1,0:T(8,128)}), f32[16,12,8,128]{3,2,1,0:T(8,128)S(1)}, u32[]{:S(2)}, u32[]{:S(2)}) async-start(f32[16,12,8,128]{3,2,1,0:T(8,128)} %pack_rows.1), calls=%async_computation.1 | async-start | bytes 1572864 | tf_op jit(solution)/shard_map/all_to_all | solution.py:520
  103.1 79.6 %all-gather.5.cloned.1.call-start = ((), (), s32[]{:S(2)}) async-start(), calls=%async_computation.4 | async-start | bytes 4177920 | tf_op jit(solution)/shard_map/all_gather | solution.py:529
  118.8 8.4 %copy-start.4 = (f32[3,5,128,128]{3,2,1,0:T(8,128)}, f32[3,5,128,128]{3,2,1,0:T(8,128)S(1)}, u32[]{:S(2)}) copy-start(f32[3,5,128,128]{3,2,1,0:T(8,128)S(1)} %collective-permute-done.1.other.rest) | copy-start | bytes 2949124
  127.2 8.8 %copy-start.1 = (f32[6464,128]{1,0:T(8,128)S(1)}, f32[6464,128]{1,0:T(8,128)}, u32[]{:S(2)}) copy-start(f32[6464,128]{1,0:T(8,128)} %all-gather.7.cloned.1.call-done) | copy-start | bytes 9928708
  129.3 24.1 %all-to-all-start.3 = ((f32[16,15,8,128]{3,2,1,0:T(8,128)}), f32[16,15,8,128]{3,2,1,0:T(8,128)}, u32[]{:S(2)}, u32[]{:S(2)}) async-start(f32[16,15,8,128]{3,2,1,0:T(8,128)} %pack_lead.1), calls=%async_computation.3 | async-start | bytes 1966080 | tf_op jit(solution)/shard_map/all_to_all | solution.py:539
  137.6 1.0 copy-start.6
  138.6 1.0 copy-start.7
Sparse Core Ops, SparseCore 0:
  92.7 27.9 all-gather.6
  127.3 55.4 all-gather.4

commit v9 on v7

--- a/solution.py
+++ b/solution.py
@@ -14,7 +14,7 @@
 ROWS = ("k", "i")
 UPPER = [(b, c) for b in range(PT) for c in range(b, PT)]
 GROUP = 32
-BLOCK = 2
+BLOCK = 3
 HIGHEST = lax.Precision.HIGHEST
 F32 = jnp.float32
 BF16 = jnp.bfloat16
@@ -124,7 +124,7 @@
                 out[v, s] = tiles[s, 8 * v:8 * v + 8]
 
 
-def take_slab(rows, other, out):
+def take_slab(rows, other, lead, out):
     for b in range(PT):
         out[b] = rows[b]
 
@@ -495,15 +495,6 @@
         name="pack_rows",
     )(maps, front, main, near)
     rows = lax.all_to_all(rows, ROWS, 0, 0, tiled=True)
-    slab = pl.pallas_call(
-        take_slab,
-        out_shape=shape(PT, COL_TILES, 8, T),
-        in_specs=[VMEM, ANY],
-        out_specs=VMEM,
-        compiler_params=params(16),
-        name="take_slab",
-    )(rows, rest)
-    across = lax.all_gather(slab, ROWS)
     lead = pl.pallas_call(
         pack_lead,
         out_shape=shape(16, len(UPPER), 8, T),
@@ -513,6 +504,15 @@
         compiler_params=params(58),
         name="pack_lead",
     )(down)
+    slab = pl.pallas_call(
+        take_slab,
+        out_shape=shape(PT, COL_TILES, 8, T),
+        in_specs=[VMEM, ANY, ANY],
+        out_specs=VMEM,
+        compiler_params=params(16),
+        name="take_slab",
+    )(rows, rest, lead)
+    across = lax.all_gather(slab, ROWS)
     lead = lax.all_to_all(lead, ROWS, 0, 0, tiled=True)
     tall = jax.ShapeDtypeStruct((ROW_TILES * T, PT * T), BF16)
     halved = pl.pallas_call(

time: 210 us -> 212 us (level)
  Pallas kernels: 56.2 us -> 59.1 us
    all_gather x1, waiting for transfers between devices: 0.02 us -> 16.8 us  [shards(): down = lax.all_gather(column, 'col')]
    ppermute x1, waiting for transfers between devices: 15.7 us -> 0.01 us  [shards(): rest = lax.ppermute(rest, 'k', swap)]
    all_to_all x1, waiting for transfers between devices: 7.63 us -> 3.88 us  [shards(): rows = lax.all_to_all(rows, ROWS, 0, 0, tiled=True)]
    unnamed x22 -> x24, local copies, waits for them, and re-layouts: 4.92 us -> 6.12 us
where the time goes in v9:
time: 212 us; the launch traced here: 210 us
  blocking collectives  78.8 us (37%)
  Pallas kernels  59.1 us (28%)
  waiting for transfers between devices  35.6 us (17%)
  starting transfers between devices  16.6 us (8%)
  between operations  13.5 us (6%)
  local copies, waits for them, and re-layouts  6.12 us (3%)
    all_to_all x1, blocking collectives, shards(): main = lax.all_to_all(main, ('i', 'col'), 0, 0, tiled=True)  60.4 us
    pallas_call x1, Pallas kernels, shards(): pl.pallas_call(invert_factor, out_shape=(shape(ROW_TILES * T, PT * T), sq...  29.3 us
    all_to_all x1, blocking collectives, shards(): lead = lax.all_to_all(lead, ROWS, 0, 0, tiled=True)  18.4 us
    pallas_call x1, Pallas kernels, shards(): pl.pallas_call(eliminate, out_shape=shape(ROW_TILES * T * COL_TILES, T),...  17.3 us
    all_gather x1, waiting for transfers between devices, shards(): down = lax.all_gather(column, 'col')  16.8 us
    all_to_all x1, waiting for transfers between devices, shards(): lead = lax.all_to_all(lead, ROWS, 0, 0, tiled=True)  12.8 us
    all_to_all x1, starting transfers between devices, shards(): rows = lax.all_to_all(rows, ROWS, 0, 0, tiled=True)  8.47 us
    all_to_all x1, starting transfers between devices, shards(): lead = lax.all_to_all(lead, ROWS, 0, 0, tiled=True)  6.77 us
  transfers between devices with their start and end apart: 6, of which 4 were waited for; matrix products, arithmetic and copies ran while one was open for 0% of the time, Pallas kernels for 17%

profile of v9, /device:TPU:16, one launch (start us, length us, event | category | flops | bytes accessed | tf_op | source)
XLA Modules:
  0.0 209.7 jit_solution(15922878066380511501)
XLA Ops:
  6.5 1.7 copy-done.2
  8.2 0.7 copy-done.5
  8.9 0.7 copy-done.7
  9.5 0.9 pack_main.1
  10.5 60.4 %all_to_all.20.moved.moved_far = f32[64,128,128]{2,1,0:T(8,128)S(1)} all-to-all(f32[64,128,128]{2,1,0:T(8,128)S(1)} %pack_main.1), channel_id=1, replica_groups=mesh['k'=2,'i'=8,'col'=8] {'i','col'}, dimensions={0} | all-to-all | bytes 8388608 | tf_op jit(solution)/shard_map/all_to_all | solution.py:459
  70.9 2.3 %pack_other.1 = (f32[9,128,128]{2,1,0:T(8,128)S(1)}, f32[3,5,128,128]{3,2,1,0:T(8,128)}, f32[16,8,128]{2,1,0:T(8,128)S(1)}) custom-call(s32[2,48]{1,0:T(2,128)S(1)} %copy-done.6, f32[64,128,128]{2,1,0:T(8,128)S(1)} %all_to_all.20.moved.moved_far, f32[4608,128]{1,0:T(8,128)S(1)} %bitcast.14, f32[9216,128]{1,0:T(8,128)S(1)} %bitcast.9), custom_call_target="tpu_custom_call" | custom-call | tf_op jit(solution)/shard_map/pack_other/pallas_call | solution.py:461
  73.8 18.4 %all_to_all.21.lead = f32[16,8,128]{2,1,0:T(8,128)S(1)} all-to-all(f32[16,8,128]{2,1,0:T(8,128)S(1)} %get-tuple-element.15), channel_id=1, replica_groups=mesh['k'=2,'i'=8,'col'=8] {'k','i'}, dimensions={0} | all-to-all | bytes 131072 | tf_op jit(solution)/shard_map/all_to_all | solution.py:471
  92.2 1.7 add_column.1
  94.0 0.7 collective-permute-start.1
  94.7 2.0 pack_rows.1
  96.7 8.5 %all-to-all-start.1 = ((f32[16,12,8,128]{3,2,1,0:T(8,128)}), f32[16,12,8,128]{3,2,1,0:T(8,128)}, u32[]{:S(2)}, u32[]{:S(2)}) async-start(f32[16,12,8,128]{3,2,1,0:T(8,128)} %pack_rows.1), calls=%async_computation.1 | async-start | bytes 1572864 | tf_op jit(solution)/shard_map/all_to_all | solution.py:497
  105.3 16.8 %all-gather.5.cloned.1.call-done = f32[6464,128]{1,0:T(8,128)} async-done(((f32[808,128]{1,0:T(8,128)}), f32[6464,128]{1,0:T(8,128)}) %all-gather.5.cloned.1.call-update) | async-done | bytes 3309584 | tf_op jit(solution)/shard_map/all_gather | solution.py:482
  122.1 2.1 %pack_lead.1.lead = f32[16,15,8,128]{3,2,1,0:T(8,128)} custom-call(f32[8,808,128]{2,1,0:T(8,128)} %bitcast.11), custom_call_target="tpu_custom_call" | custom-call | tf_op jit(solution)/shard_map/pack_lead/pallas_call | solution.py:498
  124.2 3.9 %all-to-all-done.1.rows = f32[16,12,8,128]{3,2,1,0:T(8,128)} async-done(((f32[16,12,8,128]{3,2,1,0:T(8,128)}), f32[16,12,8,128]{3,2,1,0:T(8,128)}, u32[]{:S(2)}, u32[]{:S(2)}) %all-to-all-start.1) | async-done | bytes 786464 | tf_op jit(solution)/shard_map/all_to_all | solution.py:497
  128.1 1.2 copy-done.3
  129.3 1.9 take_slab.1
  131.2 6.8 %all-to-all-start.3 = ((f32[16,15,8,128]{3,2,1,0:T(8,128)}), f32[16,15,8,128]{3,2,1,0:T(8,128)}, u32[]{:S(2)}, u32[]{:S(2)}) async-start(f32[16,15,8,128]{3,2,1,0:T(8,128)} %pack_lead.1.lead), calls=%async_computation.3 | async-start | bytes 1966080 | tf_op jit(solution)/shard_map/all_to_all | solution.py:516
  138.0 1.6 split_rows.1
  139.6 0.9 copy-done.8
  140.5 1.0 copy-done.9
  141.5 12.8 %all-to-all-done.3.lead = f32[16,15,8,128]{3,2,1,0:T(8,128)} async-done(((f32[16,15,8,128]{3,2,1,0:T(8,128)}), f32[16,15,8,128]{3,2,1,0:T(8,128)}, u32[]{:S(2)}, u32[]{:S(2)}) %all-to-all-start.3) | async-done | bytes 983072 | tf_op jit(solution)/shard_map/all_to_all | solution.py:516
  154.2 29.3 %invert_factor.1 = (f32[768,640]{1,0:T(8,128)}, bf16[640,640]{1,0:T(8,128)(2,1)}, bf16[640,640]{1,0:T(8,128)(2,1)}) custom-call(f32[16,15,8,128]{3,2,1,0:T(8,128)} %all-to-all-done.3.lead, bf16[768,640]{1,0:T(8,128)(2,1)} %copy-done.8, bf16[768,640]{1,0:T(8,128)(2,1)} %copy-done.9), custom_call_target="tpu_custom_call" | custom-call | flops 30000001024 | bytes 8388608 | tf_op jit(solution)/shard_map/invert_factor/pallas_call | solution.py:530
  183.5 2.0 all-gather.7.cloned.1.call-done
  185.6 17.3 %eliminate.1 = f32[9216,128]{1,0:T(8,128)} custom-call(s32[2,48]{1,0:T(2,128)} %maps.9, f32[9216,128]{1,0:T(8,128)} %bitcast.6, f32[16,5,12,8,128]{4,3,2,1,0:T(8,128)} %bitcast.15, f32[768,640]{1,0:T(8,128)} %get-tuple-element.18.lower, bf16[640,640]{1,0:T(8,128)(2,1)} %get-tuple-element.19.inverse_high, bf16[640,640]{1,0:T(8,128)(2,1)} %get-tuple-element.20.inverse_low, ...), custom_call_target="tpu_custom_call" | custom-call | flops 12000000000 | bytes 20971520 | tf_op jit(solution)/shard_map/eliminate/pallas_call | solution.py:548
  (26 shorter events, 0.7 us)
Async XLA Ops:
  6.5 115.5 %all-gather.5.cloned.1.call-start = ((), (), s32[]{:S(2)}) async-start(), calls=%async_computation.4 | async-start | bytes 3723264 | tf_op jit(solution)/shard_map/all_gather | solution.py:482
  6.5 1.7 copy-start.2
  8.2 0.7 copy-start.5
  8.9 0.7 copy-start.7
  9.5 61.3 %slice-start = ((s8[4718592]{0:T(1024)(128)(4,1)}), s8[4194304]{0:T(1024)(128)(4,1)S(1)}, s32[]{:S(2)}) async-start(s8[4718592]{0:T(1024)(128)(4,1)} %bitcast.7), calls=%async_computation.6 | async-start | bytes 8388608
  10.5 60.4 %slice-start.1 = ((s8[4718592]{0:T(1024)(128)(4,1)}), s8[524288]{0:T(1024)(128)(4,1)S(1)}, s32[]{:S(2)}) async-start(s8[4718592]{0:T(1024)(128)(4,1)} %bitcast.7), calls=%async_computation.7 | async-start | bytes 1048576
  10.5 60.4 %copy-start.6 = (s32[2,48]{1,0:T(2,128)S(1)}, s32[2,48]{1,0:T(2,128)}, u32[]{:S(2)}) copy-start(s32[2,48]{1,0:T(2,128)} %maps.9) | copy-start | bytes 1156
  70.9 21.4 %copy-start = (f32[64,128,128]{2,1,0:T(8,128)}, f32[64,128,128]{2,1,0:T(8,128)S(1)}, u32[]{:S(2)}) copy-start(f32[64,128,128]{2,1,0:T(8,128)S(1)} %all_to_all.20.moved.moved_far) | copy-start | bytes 12582916
  73.2 19.0 %collective-permute-start = (f32[9,128,128]{2,1,0:T(8,128)S(1)}, f32[9,128,128]{2,1,0:T(8,128)S(1)}, u32[]{:S(2)}, u32[]{:S(2)}) collective-permute-start(f32[9,128,128]{2,1,0:T(8,128)S(1)} %get-tuple-element.13), channel_id=1, source_target_pairs={{0,64},{64,0},{1,65},{65,1},{2,66},{66,2},{3,67},{67,3},{4,68},{68... | collective-permute-start | bytes 1769480 | tf_op jit(solution)/shard_map/ppermute | solution.py:472
  92.2 1.7 copy-start.4
  94.0 30.3 %collective-permute-start.1 = (f32[3,5,128,128]{3,2,1,0:T(8,128)}, f32[3,5,128,128]{3,2,1,0:T(8,128)}, u32[]{:S(2)}, u32[]{:S(2)}) collective-permute-start(f32[3,5,128,128]{3,2,1,0:T(8,128)} %get-tuple-element.14), channel_id=1, source_target_pairs={{0,64},{64,0},{1,65},{65,1},{2,66},{66,2},{3,67},{67,3},{4,68},{68... | collective-permute-start | bytes 2949128 | tf_op jit(solution)/shard_map/ppermute | solution.py:473
  96.7 31.4 %all-to-all-start.1 = ((f32[16,12,8,128]{3,2,1,0:T(8,128)}), f32[16,12,8,128]{3,2,1,0:T(8,128)}, u32[]{:S(2)}, u32[]{:S(2)}) async-start(f32[16,12,8,128]{3,2,1,0:T(8,128)} %pack_rows.1), calls=%async_computation.1 | async-start | bytes 1572864 | tf_op jit(solution)/shard_map/all_to_all | solution.py:497
  105.2 80.3 %all-gather.7.cloned.1.call-start = ((), (), s32[]{:S(2)}) async-start(), calls=%async_computation.5 | async-start | bytes 4177920 | tf_op jit(solution)/shard_map/all_gather | solution.py:515
  122.1 15.9 %copy-start.1 = (f32[6464,128]{1,0:T(8,128)S(1)}, f32[6464,128]{1,0:T(8,128)}, u32[]{:S(2)}) copy-start(f32[6464,128]{1,0:T(8,128)} %all-gather.5.cloned.1.call-done) | copy-start | bytes 9928708
  128.1 1.2 copy-start.3
  131.2 23.0 %all-to-all-start.3 = ((f32[16,15,8,128]{3,2,1,0:T(8,128)}), f32[16,15,8,128]{3,2,1,0:T(8,128)}, u32[]{:S(2)}, u32[]{:S(2)}) async-start(f32[16,15,8,128]{3,2,1,0:T(8,128)} %pack_lead.1.lead), calls=%async_computation.3 | async-start | bytes 1966080 | tf_op jit(solution)/shard_map/all_to_all | solution.py:516
  139.6 0.9 copy-start.8
  140.5 1.0 copy-start.9
Sparse Core Ops, SparseCore 0:
  94.1 27.9 all-gather.4
  131.3 54.1 all-gather.6
